TPU v7x, 32 devices: a whole 2x2x4 slice. The times are simulated.
32 devices in a mesh: dp: 4 (over y, x), fsdp: 8 (over z, core).
Axes of the slice: x: 2, y: 2, z: 4, core: 2. Of those that a mesh axis runs over, the one named last changes fastest.
Arguments:
- tokens: bfloat16 [8192, 2048], P(('dp', 'fsdp')), may hold values from -6 to 6
- lengths: int32 [32, 2], P(('dp', 'fsdp')), may hold values from 1 to 224, as said below
- attn_gain: bfloat16 [2048], P(('dp', 'fsdp')), may hold values from 0.5 to 1.5
- query_down: bfloat16 [2048, 1024], P(('dp', 'fsdp')), may hold values from -0.125 to 0.125
- query_gain: bfloat16 [1024], P(('dp', 'fsdp')), may hold values from 0.5 to 1.5
- query_up: bfloat16 [1024, 4096], P(('dp', 'fsdp')), may hold values from -0.375 to 0.375
- key_weight: bfloat16 [2048, 256], P(('dp', 'fsdp')), may hold values from -0.125 to 0.125
- value_weight: bfloat16 [2048, 256], P(('dp', 'fsdp')), may hold values from -0.125 to 0.125
- out_weight: bfloat16 [4096, 2048], P(('dp', 'fsdp')), may hold values from -0.375 to 0.375
- mlp_gain: bfloat16 [2048], P(('dp', 'fsdp')), may hold values from 0.5 to 1.5
- gate_weight: bfloat16 [2048, 5632], P(('dp', 'fsdp')), may hold values from -0.125 to 0.125
- up_weight: bfloat16 [2048, 5632], P(('dp', 'fsdp')), may hold values from -0.125 to 0.125
- down_weight: bfloat16 [5632, 2048], P(('dp', 'fsdp')), may hold values from -0.109375 to 0.109375
- cotangent: bfloat16 [8192, 2048], P(('dp', 'fsdp')), may hold values from -6 to 6
Outputs:
- layer_out: bfloat16 [8192, 2048], P(('dp', 'fsdp'))
- tokens_grad: float32 [8192, 2048], P(('dp', 'fsdp'))
- attn_gain_grad: float32 [2048], P(('dp', 'fsdp'))
- query_down_grad: float32 [2048, 1024], P(('dp', 'fsdp'))
- query_gain_grad: float32 [1024], P(('dp', 'fsdp'))
- query_up_grad: float32 [1024, 4096], P(('dp', 'fsdp'))
- key_weight_grad: float32 [2048, 256], P(('dp', 'fsdp'))
- value_weight_grad: float32 [2048, 256], P(('dp', 'fsdp'))
- out_weight_grad: float32 [4096, 2048], P(('dp', 'fsdp'))
- mlp_gain_grad: float32 [2048], P(('dp', 'fsdp'))
- gate_weight_grad: float32 [2048, 5632], P(('dp', 'fsdp'))
- up_weight_grad: float32 [2048, 5632], P(('dp', 'fsdp'))
- down_weight_grad: float32 [5632, 2048], P(('dp', 'fsdp'))
Inputs may be any that keep to these rules, and one draw needn't show every extreme that they name: A row holds the lengths of one device's 2 sequences; rounded up to multiples of 32 they sum to at most 256. On one device, drawn from the seed, they sum to exactly 256 and one of its sequences is 224 long.
All inputs are finite; a program needn't handle non-finite values.
Results may differ from a plain program's by a relative error of at most 0.017.
Values may be sent and summed in bfloat16 or wider, within the bound.
No kernel may reach another device: no remote copies, remote signals or barrier semaphores. Data moves between devices by JAX's collectives and lax.ppermute only.
A program may use at most 384 MiB of HBM per device.

v0:
```python
import math

import jax
import jax.numpy as jnp
from jax import lax
from jax.sharding import PartitionSpec as P

H = 16
HD = 256
PAD = 32


eps = 1e-06
rope_base = 10000.0
masked_score = -1e30


def layout(lengths, row_total):
    padded = (lengths + PAD - 1) // PAD * PAD
    slot_end = jnp.cumsum(padded)
    slot_start = slot_end - padded
    row_index = jnp.arange(row_total, dtype=jnp.int32)
    member = (row_index[:, None] >= slot_start[None, :]) & (row_index[:, None] < slot_end[None, :])
    slot_number = jnp.arange(1, lengths.shape[0] + 1, dtype=jnp.int32)
    segment = jnp.sum(jnp.where(member, slot_number[None, :], 0), axis=1)
    offset = row_index - jnp.sum(jnp.where(member, slot_start[None, :], 0), axis=1)
    alive = jnp.any(member & (offset[:, None] < lengths[None, :]), axis=1)
    allowed = (
        (segment[:, None] == segment[None, :])
        & (segment[:, None] > 0)
        & (row_index[None, :] <= row_index[:, None])
        & alive[None, :]
    )
    allowed = allowed | (row_index[:, None] == row_index[None, :])
    return (offset, alive, allowed)


def angles(offset, head_size):
    half_width = head_size // 2
    frequency = jnp.exp(
        jnp.arange(half_width, dtype=jnp.float32) * (-2.0 * math.log(rope_base) / head_size)
    )
    phase = offset.astype(jnp.float32)[:, None] * frequency[None, :]
    return (jnp.cos(phase), jnp.sin(phase))


def rotate(values, cos_part, sin_part):
    half_width = values.shape[-1] // 2
    first_half = values[..., :half_width]
    second_half = values[..., half_width:]
    return jnp.concatenate(
        [
            first_half * cos_part - second_half * sin_part,
            second_half * cos_part + first_half * sin_part,
        ],
        axis=-1,
    )


def normalize(values, scale_gain):
    factor = lax.rsqrt(jnp.mean(values * values, axis=-1, keepdims=True) + eps)
    normed = values * factor
    return (normed * scale_gain.astype(jnp.float32), normed, factor)


def normalize_back(upstream, normed, factor, scale_gain):
    scaled = upstream * scale_gain.astype(jnp.float32)
    gain_grad = jnp.sum(upstream * normed, axis=0)
    inner_mean = jnp.mean(scaled * normed, axis=-1, keepdims=True)
    return (factor * (scaled - normed * inner_mean), gain_grad)


def score_block(query_rot, key_rot, allowed, score_scale):
    scores = (
        jnp.einsum("thd,sd->hts", query_rot, key_rot, preferred_element_type=jnp.float32)
        * score_scale
    )
    return jnp.where(allowed[None, :, :], scores, masked_score)


def shards(
    tokens,
    lengths,
    attn_gain,
    query_down,
    query_gain,
    query_up,
    key_weight,
    value_weight,
    out_weight,
    mlp_gain,
    gate_weight,
    up_weight,
    down_weight,
    cotangent,
):
    row_total = tokens.shape[0]
    offset, alive, allowed = layout(lengths[0], row_total)
    living = alive.astype(jnp.float32)[:, None]
    cos_part, sin_part = angles(offset, HD)
    score_scale = 1.0 / math.sqrt(HD)
    attn_local = (attn_gain, query_down, query_gain, query_up, key_weight, value_weight, out_weight)
    mlp_local = (mlp_gain, gate_weight, up_weight, down_weight)
    attn_full = (
        lax.all_gather(attn_local[0], ("dp", "fsdp"), axis=0, tiled=True),
        lax.all_gather(attn_local[1], ("dp", "fsdp"), axis=0, tiled=True),
        lax.all_gather(attn_local[2], ("dp", "fsdp"), axis=0, tiled=True),
        lax.all_gather(attn_local[3], ("dp", "fsdp"), axis=0, tiled=True),
        lax.all_gather(attn_local[4], ("dp", "fsdp"), axis=0, tiled=True),
        lax.all_gather(attn_local[5], ("dp", "fsdp"), axis=0, tiled=True),
        lax.all_gather(attn_local[6], ("dp", "fsdp"), axis=0, tiled=True),
    )
    attn_scale, latent_down, latent_scale, query_full, key_full, value_full, out_full = attn_full
    token_rows = tokens.astype(jnp.float32)
    attn_out, attn_normed, attn_factor = normalize(token_rows, attn_scale)
    attn_in = attn_out.astype(jnp.bfloat16)
    latent = jnp.dot(attn_in, latent_down, preferred_element_type=jnp.float32)
    latent_out, latent_normed, latent_factor = normalize(latent, latent_scale)
    latent_in = latent_out.astype(jnp.bfloat16)
    queries = jnp.dot(latent_in, query_full, preferred_element_type=jnp.float32).reshape(
        row_total, H, HD
    )
    query_rot = rotate(queries, cos_part[:, None, :], sin_part[:, None, :]).astype(jnp.bfloat16)
    key_plain = jnp.dot(attn_in, key_full, preferred_element_type=jnp.float32)
    key_rot = rotate(key_plain, cos_part, sin_part).astype(jnp.bfloat16)
    value_low = jnp.dot(attn_in, value_full, preferred_element_type=jnp.float32).astype(
        jnp.bfloat16
    )
    scores = score_block(query_rot, key_rot, allowed, score_scale)
    top_score = jnp.max(scores, axis=-1, keepdims=True)
    expo_scores = jnp.exp(scores - top_score)
    total_mass = jnp.sum(expo_scores, axis=-1, keepdims=True)
    log_total = top_score + jnp.log(total_mass)
    probs_low = (expo_scores / total_mass).astype(jnp.bfloat16)
    mixture = jnp.einsum("hts,sd->thd", probs_low, value_low, preferred_element_type=jnp.float32)
    mixture = mixture.reshape(row_total, H * HD).astype(jnp.bfloat16)
    residual = token_rows + living * jnp.dot(mixture, out_full, preferred_element_type=jnp.float32)
    mlp_full = (
        lax.all_gather(mlp_local[0], ("dp", "fsdp"), axis=0, tiled=True),
        lax.all_gather(mlp_local[1], ("dp", "fsdp"), axis=0, tiled=True),
        lax.all_gather(mlp_local[2], ("dp", "fsdp"), axis=0, tiled=True),
        lax.all_gather(mlp_local[3], ("dp", "fsdp"), axis=0, tiled=True),
    )
    mlp_scale, gate_full, up_full, down_full = mlp_full
    ffn_out, ffn_normed, ffn_factor = normalize(residual, mlp_scale)
    ffn_in = ffn_out.astype(jnp.bfloat16)
    gate_act = jnp.dot(ffn_in, gate_full, preferred_element_type=jnp.float32)
    up_act = jnp.dot(ffn_in, up_full, preferred_element_type=jnp.float32)
    sigmoid_gate = jax.nn.sigmoid(gate_act)
    silu_gate = gate_act * sigmoid_gate
    hidden = (silu_gate * up_act).astype(jnp.bfloat16)
    layer_out = (
        residual + living * jnp.dot(hidden, down_full, preferred_element_type=jnp.float32)
    ).astype(jnp.bfloat16)
    mlp_back = (
        lax.all_gather(mlp_local[0], ("dp", "fsdp"), axis=0, tiled=True),
        lax.all_gather(mlp_local[1], ("dp", "fsdp"), axis=0, tiled=True),
        lax.all_gather(mlp_local[2], ("dp", "fsdp"), axis=0, tiled=True),
        lax.all_gather(mlp_local[3], ("dp", "fsdp"), axis=0, tiled=True),
    )
    mlp_scale, gate_full, up_full, down_full = mlp_back
    grad_rows = cotangent.astype(jnp.float32)
    ffn_grad = (living * grad_rows).astype(jnp.bfloat16)
    hidden_grad = jnp.einsum("td,fd->tf", ffn_grad, down_full, preferred_element_type=jnp.float32)
    gate_grad = (
        hidden_grad * up_act * sigmoid_gate * (1.0 + gate_act * (1.0 - sigmoid_gate))
    ).astype(jnp.bfloat16)
    up_grad = (hidden_grad * silu_gate).astype(jnp.bfloat16)
    ffn_in_grad = jnp.einsum(
        "tf,df->td", gate_grad, gate_full, preferred_element_type=jnp.float32
    ) + jnp.einsum("tf,df->td", up_grad, up_full, preferred_element_type=jnp.float32)
    residual_back, mlp_scale_grad = normalize_back(ffn_in_grad, ffn_normed, ffn_factor, mlp_scale)
    residual_grad = grad_rows + residual_back
    down_wgrad = jnp.einsum("tf,td->fd", hidden, ffn_grad, preferred_element_type=jnp.float32)
    gate_wgrad = jnp.einsum("td,tf->df", ffn_in, gate_grad, preferred_element_type=jnp.float32)
    up_wgrad = jnp.einsum("td,tf->df", ffn_in, up_grad, preferred_element_type=jnp.float32)
    gate_share, up_share, down_share = (
        lax.psum_scatter(gate_wgrad, ("dp", "fsdp"), scatter_dimension=0, tiled=True),
        lax.psum_scatter(up_wgrad, ("dp", "fsdp"), scatter_dimension=0, tiled=True),
        lax.psum_scatter(down_wgrad, ("dp", "fsdp"), scatter_dimension=0, tiled=True),
    )
    attn_back = (
        lax.all_gather(attn_local[0], ("dp", "fsdp"), axis=0, tiled=True),
        lax.all_gather(attn_local[1], ("dp", "fsdp"), axis=0, tiled=True),
        lax.all_gather(attn_local[2], ("dp", "fsdp"), axis=0, tiled=True),
        lax.all_gather(attn_local[3], ("dp", "fsdp"), axis=0, tiled=True),
        lax.all_gather(attn_local[4], ("dp", "fsdp"), axis=0, tiled=True),
        lax.all_gather(attn_local[5], ("dp", "fsdp"), axis=0, tiled=True),
        lax.all_gather(attn_local[6], ("dp", "fsdp"), axis=0, tiled=True),
    )
    attn_scale, latent_down, latent_scale, query_full, key_full, value_full, out_full = attn_back
    attn_grad = (living * residual_grad).astype(jnp.bfloat16)
    out_wgrad = jnp.einsum("tc,td->cd", mixture, attn_grad, preferred_element_type=jnp.float32)
    mixture_grad = jnp.einsum("td,cd->tc", attn_grad, out_full, preferred_element_type=jnp.float32)
    mixture_grad = mixture_grad.astype(jnp.bfloat16).reshape(row_total, H, HD)
    scores = score_block(query_rot, key_rot, allowed, score_scale)
    attn_probs = jnp.exp(scores - log_total)
    probs_low = attn_probs.astype(jnp.bfloat16)
    probs_grad = jnp.einsum(
        "thd,sd->hts", mixture_grad, value_low, preferred_element_type=jnp.float32
    )
    row_dot = jnp.sum(attn_probs * probs_grad, axis=-1, keepdims=True)
    score_grad = (attn_probs * (probs_grad - row_dot)).astype(jnp.bfloat16)
    query_rot_grad = (
        jnp.einsum("hts,sd->thd", score_grad, key_rot, preferred_element_type=jnp.float32)
        * score_scale
    )
    key_rot_grad = (
        jnp.einsum("hts,thd->sd", score_grad, query_rot, preferred_element_type=jnp.float32)
        * score_scale
    )
    value_grad = jnp.einsum(
        "hts,thd->sd", probs_low, mixture_grad, preferred_element_type=jnp.float32
    ).astype(jnp.bfloat16)
    query_grad = rotate(query_rot_grad, cos_part[:, None, :], -sin_part[:, None, :])
    query_grad = query_grad.astype(jnp.bfloat16).reshape(row_total, H * HD)
    key_grad = rotate(key_rot_grad, cos_part, -sin_part).astype(jnp.bfloat16)
    query_wgrad = jnp.einsum("tr,tc->rc", latent_in, query_grad, preferred_element_type=jnp.float32)
    key_wgrad = jnp.einsum("td,te->de", attn_in, key_grad, preferred_element_type=jnp.float32)
    value_wgrad = jnp.einsum("td,te->de", attn_in, value_grad, preferred_element_type=jnp.float32)
    latent_in_grad = jnp.einsum(
        "tc,rc->tr", query_grad, query_full, preferred_element_type=jnp.float32
    )
    latent_back, latent_scale_grad = normalize_back(
        latent_in_grad, latent_normed, latent_factor, latent_scale
    )
    latent_grad = latent_back.astype(jnp.bfloat16)
    qdown_wgrad = jnp.einsum("td,tr->dr", attn_in, latent_grad, preferred_element_type=jnp.float32)
    attn_in_grad = (
        jnp.einsum("tr,dr->td", latent_grad, latent_down, preferred_element_type=jnp.float32)
        + jnp.einsum("te,de->td", key_grad, key_full, preferred_element_type=jnp.float32)
        + jnp.einsum("te,de->td", value_grad, value_full, preferred_element_type=jnp.float32)
    )
    token_back, attn_scale_grad = normalize_back(attn_in_grad, attn_normed, attn_factor, attn_scale)
    tokens_grad = residual_grad + token_back
    attn_grads = (
        lax.psum_scatter(attn_scale_grad, ("dp", "fsdp"), scatter_dimension=0, tiled=True),
        lax.psum_scatter(qdown_wgrad, ("dp", "fsdp"), scatter_dimension=0, tiled=True),
        lax.psum_scatter(latent_scale_grad, ("dp", "fsdp"), scatter_dimension=0, tiled=True),
        lax.psum_scatter(query_wgrad, ("dp", "fsdp"), scatter_dimension=0, tiled=True),
        lax.psum_scatter(key_wgrad, ("dp", "fsdp"), scatter_dimension=0, tiled=True),
        lax.psum_scatter(value_wgrad, ("dp", "fsdp"), scatter_dimension=0, tiled=True),
        lax.psum_scatter(out_wgrad, ("dp", "fsdp"), scatter_dimension=0, tiled=True),
        lax.psum_scatter(mlp_scale_grad, ("dp", "fsdp"), scatter_dimension=0, tiled=True),
    )
    return (
        layer_out,
        tokens_grad,
        attn_grads[0],
        attn_grads[1],
        attn_grads[2],
        attn_grads[3],
        attn_grads[4],
        attn_grads[5],
        attn_grads[6],
        attn_grads[7],
        gate_share,
        up_share,
        down_share,
    )


def solution(mesh):
    in_specs = (
        P(("dp", "fsdp"), None),
        P(("dp", "fsdp"), None),
        P(("dp", "fsdp")),
        P(("dp", "fsdp"), None),
        P(("dp", "fsdp")),
        P(("dp", "fsdp"), None),
        P(("dp", "fsdp"), None),
        P(("dp", "fsdp"), None),
        P(("dp", "fsdp"), None),
        P(("dp", "fsdp")),
        P(("dp", "fsdp"), None),
        P(("dp", "fsdp"), None),
        P(("dp", "fsdp"), None),
        P(("dp", "fsdp"), None),
    )
    out_specs = (
        P(("dp", "fsdp"), None),
        P(("dp", "fsdp"), None),
        P(("dp", "fsdp")),
        P(("dp", "fsdp"), None),
        P(("dp", "fsdp")),
        P(("dp", "fsdp"), None),
        P(("dp", "fsdp"), None),
        P(("dp", "fsdp"), None),
        P(("dp", "fsdp"), None),
        P(("dp", "fsdp")),
        P(("dp", "fsdp"), None),
        P(("dp", "fsdp"), None),
        P(("dp", "fsdp"), None),
    )
    return jax.shard_map(shards, mesh=mesh, in_specs=in_specs, out_specs=out_specs, check_vma=False)
```

profile of v0, /device:TPU:0, one launch (start us, length us, event | category | flops | bytes accessed | tf_op | source)
XLA Modules:
  0.0 3337.4 jit_solution(17509845067296465251)
XLA Ops:
  14.4 42.2 %all-reduce.7 = (bf16[2048]{0:T(1024)(128)(2,1)S(1)}, bf16[1024]{0:T(1024)(128)(2,1)S(1)}, bf16[2048]{0:T(1024)(128)(2,1)S(1)}) all-reduce(bf16[2048]{0:T(1024)(128)(2,1)S(1)} %dynamic-update-slice, bf16[1024]{0:T(1024)(128)(2,1)S(1)} %dynamic-update-slice.1, ...), channel_id=1, replica_groups=mesh['dp'=4,'fsdp'=8] {'dp','fsdp'}, use_global_device_ids=true, to_apply=%add | all-reduce | flops 5120 | bytes 20480
  70.3 53.2 %all-gather.9.cloned.1.call-done = bf16[2048,256]{1,0:T(8,128)(2,1)} async-done(((bf16[64,256]{1,0:T(8,128)(2,1)}), bf16[2048,256]{1,0:T(8,128)(2,1)}) %all-gather.9.cloned.1.call-update) | async-done | bytes 1048592 | tf_op jit(solution)/shard_map/all_gather | solution.py:110
  125.2 62.4 %all-gather.13.cloned.1.call-done = bf16[2048,1024]{1,0:T(8,128)(2,1)} async-done(((bf16[64,1024]{1,0:T(8,128)(2,1)}), bf16[2048,1024]{1,0:T(8,128)(2,1)}) %all-gather.13.cloned.1.call-update) | async-done | bytes 4194320 | tf_op jit(solution)/shard_map/all_gather | solution.py:106
  191.2 75.2 %all-gather.15.cloned.1.call-done = bf16[1024,4096]{1,0:T(8,128)(2,1)} async-done(((bf16[32,4096]{1,0:T(8,128)(2,1)}), bf16[1024,4096]{1,0:T(8,128)(2,1)}) %all-gather.15.cloned.1.call-update) | async-done | bytes 8388624 | tf_op jit(solution)/shard_map/all_gather | solution.py:108
  281.4 101.4 %all-gather.17.cloned.1.call-done = bf16[4096,2048]{1,0:T(8,128)(2,1)} async-done(((bf16[128,2048]{1,0:T(8,128)(2,1)}), bf16[4096,2048]{1,0:T(8,128)(2,1)}) %all-gather.17.cloned.1.call-update) | async-done | bytes 16777232 | tf_op jit(solution)/shard_map/all_gather | solution.py:111
  393.4 135.0 %all-gather.21.cloned.1.call-done = bf16[2048,5632]{1,0:T(8,128)(2,1)} async-done(((bf16[64,5632]{1,0:T(8,128)(2,1)}), bf16[2048,5632]{1,0:T(8,128)(2,1)}) %all-gather.21.cloned.1.call-update) | async-done | bytes 23068688 | tf_op jit(solution)/shard_map/all_gather | solution.py:141
  540.9 133.2 %all-gather.19.cloned.1.call-done = bf16[2048,5632]{1,0:T(8,128)(2,1)} async-done(((bf16[64,5632]{1,0:T(8,128)(2,1)}), bf16[2048,5632]{1,0:T(8,128)(2,1)}) %all-gather.19.cloned.1.call-update) | async-done | bytes 23068688 | tf_op jit(solution)/shard_map/all_gather | solution.py:140
  674.1 12.6 fusion.90
  686.7 133.1 %all-gather.23.cloned.1.call-done = bf16[5632,2048]{1,0:T(8,128)(2,1)} async-done(((bf16[176,2048]{1,0:T(8,128)(2,1)}), bf16[5632,2048]{1,0:T(8,128)(2,1)}) %all-gather.23.cloned.1.call-update) | async-done | bytes 23068688 | tf_op jit(solution)/shard_map/all_gather | solution.py:142
  819.8 18.5 multiply_convert_fusion
  838.3 13.0 fusion.92
  851.3 13.9 multiply_reduce_fusion
  927.6 15.1 fusion.75
  942.8 20.0 fusion.44
  962.8 19.7 fusion.95
  982.8 19.6 fusion.94
  1009.7 38.9 %all-reduce.6 = (f32[2048]{0:T(1024)S(1)}, f32[1024]{0:T(1024)S(1)}, f32[2048]{0:T(1024)S(1)}) all-reduce(f32[2048]{0:T(1024)S(1)} %get-tuple-element.15, f32[1024]{0:T(1024)S(1)} %get-tuple-element.17, f32[2048]{0:T(1024)S(1)} %copy-done.30), channel_id=2, replica_groups=mesh['dp'=4,'fsdp'=8] {'dp','fsdp'}, use_global_device_ids=true, to_apply=%region_14.15.clone | all-reduce | flops 5120 | bytes 40960
  1066.1 90.6 %reduce-scatter.13.cloned.1.call-done = f32[64,256]{1,0:T(8,128)} async-done(((f32[2048,256]{1,0:T(8,128)}), f32[64,256]{1,0:T(8,128)}) %reduce-scatter.13.cloned.1.call-update) | async-done | bytes 65552 | tf_op jit(solution)/shard_map/reduce_scatter | solution.py:241
  1156.6 150.8 %reduce-scatter.9.cloned.1.call-done = f32[64,1024]{1,0:T(8,128)} async-done(((f32[2048,1024]{1,0:T(8,128)}), f32[64,1024]{1,0:T(8,128)}) %reduce-scatter.9.cloned.1.call-update) | async-done | bytes 262160 | tf_op jit(solution)/shard_map/reduce_scatter | solution.py:238
  1307.4 187.7 %reduce-scatter.11.cloned.1.call-done = f32[32,4096]{1,0:T(8,128)} async-done(((f32[1024,4096]{1,0:T(8,128)}), f32[32,4096]{1,0:T(8,128)}) %reduce-scatter.11.cloned.1.call-update) | async-done | bytes 524304 | tf_op jit(solution)/shard_map/reduce_scatter | solution.py:240
  1495.1 361.7 %reduce-scatter.17.cloned.1.call-done = f32[128,2048]{1,0:T(8,128)} async-done(((f32[4096,2048]{1,0:T(8,128)}), f32[128,2048]{1,0:T(8,128)}) %reduce-scatter.17.cloned.1.call-update) | async-done | bytes 1048592 | tf_op jit(solution)/shard_map/reduce_scatter | solution.py:243
  1856.8 491.2 %reduce-scatter.23.cloned.1.call-done = f32[176,2048]{1,0:T(8,128)} async-done(((f32[5632,2048]{1,0:T(8,128)}), f32[176,2048]{1,0:T(8,128)}) %reduce-scatter.23.cloned.1.call-update) | async-done | bytes 1441808 | tf_op jit(solution)/shard_map/reduce_scatter | solution.py:180
  2348.0 491.2 %reduce-scatter.21.cloned.1.call-done = f32[64,5632]{1,0:T(8,128)} async-done(((f32[2048,5632]{1,0:T(8,128)}), f32[64,5632]{1,0:T(8,128)}) %reduce-scatter.21.cloned.1.call-update) | async-done | bytes 1441808 | tf_op jit(solution)/shard_map/reduce_scatter | solution.py:179
  2839.2 491.2 %reduce-scatter.19.cloned.1.call-done = f32[64,5632]{1,0:T(8,128)} async-done(((f32[2048,5632]{1,0:T(8,128)}), f32[64,5632]{1,0:T(8,128)}) %reduce-scatter.19.cloned.1.call-update) | async-done | bytes 1441808 | tf_op jit(solution)/shard_map/reduce_scatter | solution.py:178
  (178 shorter events, 151.2 us)
Async XLA Ops:
  7.2 60.3 %all-gather.11.cloned.1.call-start = ((), (), s32[]{:S(2)}) async-start(), calls=%async_computation.9 | async-start | bytes 1081344 | tf_op jit(solution)/shard_map/all_gather | solution.py:109
  8.0 115.5 %all-gather.9.cloned.1.call-start = ((), (), s32[]{:S(2)}) async-start(), calls=%async_computation.8 | async-start | bytes 1081344 | tf_op jit(solution)/shard_map/all_gather | solution.py:110
  8.7 178.9 %all-gather.13.cloned.1.call-start = ((), (), s32[]{:S(2)}) async-start(), calls=%async_computation.10 | async-start | bytes 4325376 | tf_op jit(solution)/shard_map/all_gather | solution.py:106
  9.4 257.0 %all-gather.15.cloned.1.call-start = ((), (), s32[]{:S(2)}) async-start(), calls=%async_computation.11 | async-start | bytes 8650752 | tf_op jit(solution)/shard_map/all_gather | solution.py:108
  10.0 372.8 %all-gather.17.cloned.1.call-start = ((), (), s32[]{:S(2)}) async-start(), calls=%async_computation.12 | async-start | bytes 17301504 | tf_op jit(solution)/shard_map/all_gather | solution.py:111
  10.6 517.7 %all-gather.21.cloned.1.call-start = ((), (), s32[]{:S(2)}) async-start(), calls=%async_computation.14 | async-start | bytes 23789568 | tf_op jit(solution)/shard_map/all_gather | solution.py:141
  11.2 662.9 %all-gather.19.cloned.1.call-start = ((), (), s32[]{:S(2)}) async-start(), calls=%async_computation.13 | async-start | bytes 23789568 | tf_op jit(solution)/shard_map/all_gather | solution.py:140
  11.9 807.9 %all-gather.23.cloned.1.call-start = ((), (), s32[]{:S(2)}) async-start(), calls=%async_computation.15 | async-start | bytes 23789568 | tf_op jit(solution)/shard_map/all_gather | solution.py:142
  12.7 1053.4 %reduce-scatter.15.cloned.1.call-start = ((), (), s32[]{:S(2)}) async-start(), calls=%async_computation.19 | async-start | bytes 2162688 | tf_op jit(solution)/shard_map/reduce_scatter | solution.py:242
  13.1 57.0 %copy-start.28 = (f32[256]{0:T(256)}, f32[256]{0:T(256)S(1)}, u32[]{:S(2)}) copy-start(f32[256]{0:T(256)S(1)} %get-tuple-element.43) | copy-start | bytes 3076
  70.0 205.7 %copy-start.19 = (bf16[256,128]{0,1:T(8,128)(2,1)}, bf16[256,128]{0,1:T(8,128)(2,1)S(1)}, u32[]{:S(2)}) copy-start(bf16[256,128]{0,1:T(8,128)(2,1)S(1)} %get-tuple-element.38) | copy-start | bytes 196612
  70.0 205.7 %copy-start.20 = (bf16[256,128]{0,1:T(8,128)(2,1)}, bf16[256,128]{0,1:T(8,128)(2,1)S(1)}, u32[]{:S(2)}) copy-start(bf16[256,128]{0,1:T(8,128)(2,1)S(1)} %get-tuple-element.39) | copy-start | bytes 196612
  125.2 152.4 %copy-start.21 = (bf16[256,256,1]{1,0,2:T(8,128)(2,1)}, bf16[256,256,1]{1,0,2:T(8,128)(2,1)S(1)}, u32[]{:S(2)}) copy-start(bf16[256,256,1]{1,0,2:T(8,128)(2,1)S(1)} %fusion.43) | copy-start | bytes 393220
  191.2 81.0 %copy-start.6 = (f32[256,1024]{1,0:T(8,128)}, f32[256,1024]{1,0:T(8,128)S(1)}, u32[]{:S(2)}) copy-start(f32[256,1024]{1,0:T(8,128)S(1)} %get-tuple-element.46) | copy-start | bytes 3145732
  191.2 81.0 %copy-start.24 = (f32[256]{0:T(256)}, f32[256]{0:T(256)S(1)}, u32[]{:S(2)}) copy-start(f32[256]{0:T(256)S(1)} %add_rsqrt_fusion.1) | copy-start | bytes 3076
  279.1 103.7 %copy-start.26 = (f32[256]{0:T(256)S(1)}, f32[256]{0:T(256)}, u32[]{:S(2)}) copy-start(f32[256]{0:T(256)} %convert_element_type.98) | copy-start | bytes 3076
  392.0 473.2 %copy-start.3 = (f32[256,2048]{1,0:T(8,128)}, f32[256,2048]{1,0:T(8,128)S(1)}, u32[]{:S(2)}) copy-start(f32[256,2048]{1,0:T(8,128)S(1)} %get-tuple-element.50) | copy-start | bytes 6291460
  885.4 271.2 %reduce-scatter.13.cloned.1.call-start = ((), (), s32[]{:S(2)}) async-start(), calls=%async_computation.18 | async-start | bytes 2162688 | tf_op jit(solution)/shard_map/reduce_scatter | solution.py:241
  894.3 413.1 %reduce-scatter.9.cloned.1.call-start = ((), (), s32[]{:S(2)}) async-start(), calls=%async_computation.16 | async-start | bytes 8650752 | tf_op jit(solution)/shard_map/reduce_scatter | solution.py:238
  915.8 579.3 %reduce-scatter.11.cloned.1.call-start = ((), (), s32[]{:S(2)}) async-start(), calls=%async_computation.17 | async-start | bytes 17301504 | tf_op jit(solution)/shard_map/reduce_scatter | solution.py:240
  926.0 930.8 %reduce-scatter.17.cloned.1.call-start = ((), (), s32[]{:S(2)}) async-start(), calls=%async_computation.20 | async-start | bytes 34603008 | tf_op jit(solution)/shard_map/reduce_scatter | solution.py:243
  942.7 1405.3 %reduce-scatter.23.cloned.1.call-start = ((), (), s32[]{:S(2)}) async-start(), calls=%async_computation.23 | async-start | bytes 47579136 | tf_op jit(solution)/shard_map/reduce_scatter | solution.py:180
  962.8 1876.4 %reduce-scatter.21.cloned.1.call-start = ((), (), s32[]{:S(2)}) async-start(), calls=%async_computation.22 | async-start | bytes 47579136 | tf_op jit(solution)/shard_map/reduce_scatter | solution.py:179
  982.5 2347.9 %reduce-scatter.19.cloned.1.call-start = ((), (), s32[]{:S(2)}) async-start(), calls=%async_computation.21 | async-start | bytes 47579136 | tf_op jit(solution)/shard_map/reduce_scatter | solution.py:178
  (29 other events, 142.5 us)
Sparse Core Ops, SparseCore 0:
  11.1 56.4 all-gather.10
  70.6 52.8 all-gather.8
  126.5 61.0 all-gather.12
  190.4 75.9 all-gather.14
  269.3 113.4 all-gather.16
  385.5 142.7 all-gather.20
  531.2 142.8 all-gather.18
  676.9 142.8 all-gather.22
  885.6 135.1 reduce-scatter.14
  1023.5 133.0 reduce-scatter.12
  1159.5 147.8 reduce-scatter.8
  1310.2 184.8 reduce-scatter.10
  1498.0 358.8 reduce-scatter.16
  1859.6 488.4 reduce-scatter.22
  2350.7 488.4 reduce-scatter.20
  2841.9 488.4 reduce-scatter.18
where the time goes:
time: 3350 us; the launch traced here: 3340 us
  waiting for transfers between devices  2970 us (89%)
  matrix products  234 us (7%)
  blocking collectives  81.1 us (2%)
    reduce_scatter x1, waiting for transfers between devices, shards(): lax.psum_scatter(down_wgrad, ('dp', 'fsdp'), scatter_dimension=0, tiled=T...  491 us
    reduce_scatter x1, waiting for transfers between devices, shards(): lax.psum_scatter(gate_wgrad, ('dp', 'fsdp'), scatter_dimension=0, tiled=T...  491 us
    reduce_scatter x1, waiting for transfers between devices, shards(): lax.psum_scatter(up_wgrad, ('dp', 'fsdp'), scatter_dimension=0, tiled=True)  491 us
    reduce_scatter x1, waiting for transfers between devices, shards(): lax.psum_scatter(out_wgrad, ('dp', 'fsdp'), scatter_dimension=0, tiled=True)  362 us
    reduce_scatter x1, waiting for transfers between devices, shards(): lax.psum_scatter(query_wgrad, ('dp', 'fsdp'), scatter_dimension=0, tiled=...  188 us
    reduce_scatter x1, waiting for transfers between devices, shards(): lax.psum_scatter(qdown_wgrad, ('dp', 'fsdp'), scatter_dimension=0, tiled=...  151 us
    all_gather x1, waiting for transfers between devices, shards(): lax.all_gather(mlp_local[2], ('dp', 'fsdp'), axis=0, tiled=True)  135 us
    all_gather x1, waiting for transfers between devices, shards(): lax.all_gather(mlp_local[1], ('dp', 'fsdp'), axis=0, tiled=True)  133 us
  transfers between devices with their start and end apart: 16, of which 15 were waited for; matrix products, arithmetic and copies ran while one was open for 6% of the time, Pallas kernels for 0%

commit v1 on v0

v1 whole, which is shorter than its diff:
```python
import math

import jax
import jax.numpy as jnp
from jax import lax
from jax.sharding import PartitionSpec as P

H = 16
HD = 256
PAD = 32

eps = 1e-06
rope_base = 10000.0
masked_score = -1e30
ALL = ("dp", "fsdp")
f32 = jnp.float32
bf16 = jnp.bfloat16


def layout(lengths, row_total):
    padded = (lengths + PAD - 1) // PAD * PAD
    count = lengths.shape[0]
    ends = []
    for s in range(count):
        ends.append(padded[s] if s == 0 else ends[-1] + padded[s])
    row = lax.broadcasted_iota(jnp.int32, (row_total, 1), 0)
    segment = jnp.zeros_like(row)
    start = jnp.zeros_like(row)
    alive = jnp.zeros(row.shape, jnp.bool_)
    for s in range(count):
        first = ends[s] - padded[s]
        member = (row >= first) & (row < ends[s])
        segment = jnp.where(member, s + 1, segment)
        start = jnp.where(member, first, start)
        alive = alive | (member & (row - first < lengths[s]))
    return row - start, alive, segment


def mask_of(alive, segment, row_total):
    seg, live = segment[:, 0], alive[:, 0]
    row = jnp.arange(row_total, dtype=jnp.int32)
    allowed = (
        (seg[:, None] == seg[None, :])
        & (seg[:, None] > 0)
        & (row[None, :] <= row[:, None])
        & live[None, :]
    )
    return allowed | (row[:, None] == row[None, :])


def angles(offset, head_size):
    half_width = head_size // 2
    frequency = jnp.exp(
        jnp.arange(half_width, dtype=f32) * (-2.0 * math.log(rope_base) / head_size)
    )
    phase = offset.astype(f32) * frequency[None, :]
    return (jnp.cos(phase), jnp.sin(phase))


def rotate(values, cos_part, sin_part):
    half_width = values.shape[-1] // 2
    first_half = values[..., :half_width]
    second_half = values[..., half_width:]
    return jnp.concatenate(
        [
            first_half * cos_part - second_half * sin_part,
            second_half * cos_part + first_half * sin_part,
        ],
        axis=-1,
    )


def normalize(values, scale_gain):
    factor = lax.rsqrt(jnp.mean(values * values, axis=-1, keepdims=True) + eps)
    normed = values * factor
    return (normed * scale_gain, normed, factor)


def normalize_back(upstream, normed, factor, scale_gain):
    scaled = upstream * scale_gain
    gain_grad = jnp.sum(upstream * normed, axis=0)
    inner_mean = jnp.mean(scaled * normed, axis=-1, keepdims=True)
    return (factor * (scaled - normed * inner_mean), gain_grad)


def dot(a, b):
    return jnp.dot(a, b, preferred_element_type=f32)


def dot_nt(a, b):
    return lax.dot_general(a, b, (((1,), (1,)), ((), ())), preferred_element_type=f32)


def dot_tn(a, b):
    return lax.dot_general(a, b, (((0,), (0,)), ((), ())), preferred_element_type=f32)


def swap(values, mask):
    return lax.ppermute(values, "dp", [(i, i ^ mask) for i in range(4)])


def gather_group(values):
    half = values.shape[0] // 2
    one = swap(values, 1)
    two = swap(values, 2)
    three = jnp.concatenate([swap(two[:half], 1), swap(one[half:], 2)], axis=0)
    return jnp.concatenate([values, one, two, three], axis=0)


def scatter_group(own, others):
    rows = own.shape[0]
    half = rows // 2
    s1, s2, s3 = (others[i * rows : (i + 1) * rows] for i in range(3))
    ra = swap(jnp.concatenate([s1[:half], s3[:half]], axis=0), 1)
    rb = swap(jnp.concatenate([s2[half:], s3[half:]], axis=0), 2)
    pass_a = (s2[:half].astype(f32) + ra[half:].astype(f32)).astype(bf16)
    pass_b = (s1[half:].astype(f32) + rb[half:].astype(f32)).astype(bf16)
    last_a = swap(pass_a, 2)
    last_b = swap(pass_b, 1)
    top = own[:half] + ra[:half].astype(f32) + last_a.astype(f32)
    low = own[half:] + rb[:half].astype(f32) + last_b.astype(f32)
    return jnp.concatenate([top, low], axis=0)


def columns_in(weight, members):
    rows, width = weight.shape
    cut = weight.reshape(rows, members, width // members).transpose(1, 0, 2)
    return lax.all_to_all(cut, "dp", 0, 0, tiled=True).reshape(members * rows, width // members)


def columns_back(grad, members):
    rows, width = grad.shape[0] // members, grad.shape[1]
    cut = lax.all_to_all(grad.reshape(members, rows, width), "dp", 0, 0, tiled=True)
    return cut.transpose(1, 0, 2).reshape(rows, members * width).astype(f32)


def to_shards(values, members, ring):
    rows, width = values.shape
    cut = values.reshape(rows, members, ring, width // (members * ring))
    return cut.transpose(0, 2, 1, 3).reshape(rows, width)


def from_shards(values, members, ring):
    rows, width = values.shape
    cut = values.reshape(rows, ring, members, width // (members * ring))
    return cut.transpose(0, 2, 1, 3).reshape(rows, width)


def shards(
    members,
    ring,
    tokens,
    lengths,
    attn_gain,
    query_down,
    query_gain,
    query_up,
    key_weight,
    value_weight,
    out_weight,
    mlp_gain,
    gate_weight,
    up_weight,
    down_weight,
    cotangent,
):
    rows = tokens.shape[0]
    width = tokens.shape[1]
    latent_width = query_down.shape[1]
    heads = H // members
    devices = members * ring
    score_scale = 1.0 / math.sqrt(HD)
    d_rows = query_down.shape[0]

    def column(v):
        v = v.astype(bf16).reshape(-1, 1)
        return jnp.pad(v, ((0, d_rows - v.shape[0]), (0, 0)))

    extra = jnp.concatenate(
        [column(attn_gain), column(mlp_gain), column(query_gain), column(lengths[0])], axis=1
    )
    extra = jnp.pad(extra, ((0, 0), (0, 128 - extra.shape[1])))
    small = jnp.concatenate([query_down, key_weight, value_weight, extra], axis=1)
    small = lax.all_gather(small, ALL, axis=0, tiled=True)
    qkv_full = small[:, : latent_width + 2 * HD]
    extra = small[:, latent_width + 2 * HD :].astype(f32).T
    attn_scale = extra[0:1]
    mlp_scale = extra[1:2]
    latent_scale = extra[2].reshape(devices, d_rows)[:, : query_gain.shape[0]].reshape(1, -1)
    all_lengths = extra[3].reshape(devices, d_rows)[:, : lengths.shape[1]].astype(jnp.int32)

    query_full = lax.all_gather(columns_in(query_up, members), "fsdp", axis=0, tiled=True)
    out_full = lax.all_gather(out_weight, "fsdp", axis=0, tiled=True)
    gate_up = jnp.concatenate([columns_in(gate_weight, members), columns_in(up_weight, members)], axis=1)
    gate_up = lax.all_gather(gate_up, "fsdp", axis=0, tiled=True)
    cut = gate_up.shape[1] // 2
    gate_full, up_full = gate_up[:, :cut], gate_up[:, cut:]
    down_full = lax.all_gather(down_weight, "fsdp", axis=0, tiled=True)

    me, lane = lax.axis_index("dp"), lax.axis_index("fsdp")
    parts = []
    for slot in range(members):
        mine = lax.dynamic_slice_in_dim(all_lengths, (me ^ slot) * ring + lane, 1, 0)[0]
        parts.append(layout(mine, rows))
    offset = jnp.concatenate([p[0] for p in parts], axis=0)
    alive = parts[0][1]
    living = alive.astype(f32)
    allowed = jnp.stack([mask_of(p[1], p[2], rows) for p in parts])
    cos_part, sin_part = angles(offset, HD)

    grad_rows = cotangent.astype(f32)
    ffn_grad = gather_group((living * grad_rows).astype(bf16))
    token_rows = tokens.astype(f32)
    attn_out, attn_normed, attn_factor = normalize(token_rows, attn_scale)
    attn_in = attn_out.astype(bf16)
    low = dot(attn_in, qkv_full)
    latent = low[:, :latent_width]
    latent_out, latent_normed, latent_factor = normalize(latent, latent_scale)
    latent_in = to_shards(latent_out.astype(bf16), members, ring)
    key_own = rotate(low[:, latent_width : latent_width + HD], cos_part[:rows], sin_part[:rows])
    value_own = low[:, latent_width + HD :]
    packed = jnp.concatenate([latent_in, key_own.astype(bf16), value_own.astype(bf16)], axis=1)
    packed = gather_group(packed)
    latent_in = packed[:, :latent_width]
    key_rot = packed[:, latent_width : latent_width + HD].reshape(members, rows, HD)
    value_low = packed[:, latent_width + HD :].reshape(members, rows, HD)

    queries = dot(latent_in, query_full).reshape(members * rows, heads, HD)
    query_rot = rotate(queries, cos_part[:, None, :], sin_part[:, None, :]).astype(bf16)
    query_rot = query_rot.reshape(members, rows, heads, HD)

    def score_block():
        scores = (
            jnp.einsum("mthd,msd->mhts", query_rot, key_rot, preferred_element_type=f32) * score_scale
        )
        return jnp.where(allowed[:, None], scores, masked_score)

    scores = score_block()
    top_score = jnp.max(scores, axis=-1, keepdims=True)
    expo_scores = jnp.exp(scores - top_score)
    total_mass = jnp.sum(expo_scores, axis=-1, keepdims=True)
    attn_probs = expo_scores / total_mass
    probs_low = attn_probs.astype(bf16)
    mixture = jnp.einsum("mhts,msd->mthd", probs_low, value_low, preferred_element_type=f32)
    mixture = mixture.reshape(members * rows, heads * HD).astype(bf16)
    attn_sum = scatter_group(dot(mixture[:rows], out_full), dot(mixture[rows:], out_full).astype(bf16))
    residual = token_rows + living * attn_sum

    ffn_out, ffn_normed, ffn_factor = normalize(residual, mlp_scale)
    ffn_in = gather_group(to_shards(ffn_out.astype(bf16), members, ring))
    gate_act = dot(ffn_in, gate_full)
    up_act = dot(ffn_in, up_full)
    sigmoid_gate = jax.nn.sigmoid(gate_act)
    silu_gate = gate_act * sigmoid_gate
    hidden = (silu_gate * up_act).astype(bf16)

    hidden_grad = dot_nt(ffn_grad, down_full)
    gate_grad = (
        hidden_grad * up_act * sigmoid_gate * (1.0 + gate_act * (1.0 - sigmoid_gate))
    ).astype(bf16)
    up_grad = (hidden_grad * silu_gate).astype(bf16)
    ffn_in_grad = scatter_group(
        dot_nt(gate_grad[:rows], gate_full) + dot_nt(up_grad[:rows], up_full),
        (dot_nt(gate_grad[rows:], gate_full) + dot_nt(up_grad[rows:], up_full)).astype(bf16),
    )
    ffn_in_grad = from_shards(ffn_in_grad, members, ring)
    down_wgrad = dot_tn(hidden, ffn_grad).astype(bf16)
    gate_wgrad = dot_tn(ffn_in, gate_grad).astype(bf16)
    up_wgrad = dot_tn(ffn_in, up_grad).astype(bf16)
    down_share = lax.psum_scatter(down_wgrad, "fsdp", scatter_dimension=0, tiled=True)
    gate_share = lax.psum_scatter(gate_wgrad, "fsdp", scatter_dimension=0, tiled=True)
    up_share = lax.psum_scatter(up_wgrad, "fsdp", scatter_dimension=0, tiled=True)
    ffn_sum = scatter_group(dot(hidden[:rows], down_full), dot(hidden[rows:], down_full).astype(bf16))
    layer_out = (residual + living * ffn_sum).astype(bf16)

    residual_back, mlp_scale_grad = normalize_back(ffn_in_grad, ffn_normed, ffn_factor, mlp_scale)
    residual_grad = grad_rows + residual_back
    attn_grad = gather_group((living * residual_grad).astype(bf16))
    out_wgrad = dot_tn(mixture, attn_grad).astype(bf16)
    out_share = lax.psum_scatter(out_wgrad, "fsdp", scatter_dimension=0, tiled=True)
    mixture_grad = dot_nt(attn_grad, out_full).astype(bf16).reshape(members, rows, heads, HD)
    probs_grad = jnp.einsum("mthd,msd->mhts", mixture_grad, value_low, preferred_element_type=f32)
    row_dot = jnp.sum(attn_probs * probs_grad, axis=-1, keepdims=True)
    score_grad = (attn_probs * (probs_grad - row_dot)).astype(bf16)
    query_rot_grad = (
        jnp.einsum("mhts,msd->mthd", score_grad, key_rot, preferred_element_type=f32) * score_scale
    )
    key_rot_grad = (
        jnp.einsum("mhts,mthd->msd", score_grad, query_rot, preferred_element_type=f32) * score_scale
    ).reshape(members * rows, HD)
    value_grad = jnp.einsum(
        "mhts,mthd->msd", probs_low, mixture_grad, preferred_element_type=f32
    ).reshape(members * rows, HD)
    query_rot_grad = query_rot_grad.reshape(members * rows, heads, HD)
    query_grad = rotate(query_rot_grad, cos_part[:, None, :], -sin_part[:, None, :])
    query_grad = query_grad.astype(bf16).reshape(members * rows, heads * HD)
    query_wgrad = dot_tn(latent_in, query_grad).astype(bf16)
    query_share = lax.psum_scatter(query_wgrad, "fsdp", scatter_dimension=0, tiled=True)
    packed_grad = jnp.concatenate([dot_nt(query_grad, query_full), key_rot_grad, value_grad], axis=1)
    packed_grad = scatter_group(packed_grad[:rows], packed_grad[rows:].astype(bf16))
    latent_in_grad = from_shards(packed_grad[:, :latent_width], members, ring)
    key_grad = rotate(
        packed_grad[:, latent_width : latent_width + HD], cos_part[:rows], -sin_part[:rows]
    ).astype(bf16)
    value_grad = packed_grad[:, latent_width + HD :].astype(bf16)
    latent_back, latent_scale_grad = normalize_back(
        latent_in_grad, latent_normed, latent_factor, latent_scale
    )
    qkv_grad = jnp.concatenate([latent_back.astype(bf16), key_grad, value_grad], axis=1)
    attn_in_grad = dot_nt(qkv_grad, qkv_full)
    token_back, attn_scale_grad = normalize_back(attn_in_grad, attn_normed, attn_factor, attn_scale)
    tokens_grad = residual_grad + token_back

    small_grad = dot_tn(attn_in, qkv_grad)
    latent_column = jnp.pad(
        latent_scale_grad.reshape(devices, -1), ((0, 0), (0, d_rows - query_gain.shape[0]))
    ).reshape(-1)
    columns = jnp.stack([attn_scale_grad, mlp_scale_grad, latent_column])
    columns = jnp.pad(columns, ((0, 128 - 3), (0, 0))).T
    small_grad = jnp.concatenate([small_grad, columns], axis=1).astype(bf16)
    small_grad = small_grad.reshape(members, ring, d_rows, -1).transpose(1, 0, 2, 3)
    small_grad = small_grad.reshape(devices * d_rows, -1)
    small_share = lax.psum_scatter(small_grad, "fsdp", scatter_dimension=0, tiled=True)
    small_share = lax.psum_scatter(small_share, "dp", scatter_dimension=0, tiled=True).astype(f32)
    return (
        layer_out,
        tokens_grad,
        small_share[:, latent_width + 2 * HD],
        small_share[:, :latent_width],
        small_share[: query_gain.shape[0], latent_width + 2 * HD + 2],
        columns_back(query_share, members),
        small_share[:, latent_width : latent_width + HD],
        small_share[:, latent_width + HD : latent_width + 2 * HD],
        out_share.astype(f32),
        small_share[:, latent_width + 2 * HD + 1],
        columns_back(gate_share, members),
        columns_back(up_share, members),
        down_share.astype(f32),
    )


def solution(mesh):
    members, ring = mesh.shape["dp"], mesh.shape["fsdp"]
    matrix, vector = P(ALL, None), P(ALL)
    in_specs = (
        matrix,
        matrix,
        vector,
        matrix,
        vector,
        matrix,
        matrix,
        matrix,
        matrix,
        vector,
        matrix,
        matrix,
        matrix,
        matrix,
    )
    out_specs = (
        matrix,
        matrix,
        vector,
        matrix,
        vector,
        matrix,
        matrix,
        matrix,
        matrix,
        vector,
        matrix,
        matrix,
        matrix,
    )

    def body(*args):
        return shards(members, ring, *args)

    return jax.shard_map(body, mesh=mesh, in_specs=in_specs, out_specs=out_specs, check_vma=False)
```

time: 3350 us -> 944 us (0.28)
  waiting for transfers between devices: 2970 us -> 494 us
  local copies, waits for them, and re-layouts: 15.7 us -> 112 us
  blocking collectives: 81.1 us -> 10.8 us
  matrix products: 234 us -> 165 us
  other arithmetic: 17.4 us -> 76.6 us
  starting transfers between devices: 1.27 us -> 56.6 us
    reduce_scatter x8 -> x7, waiting for transfers between devices: 2260 us -> 223 us  [the longest x1 60.9 us: shards(): lax.psum_scatter(down_wgrad, 'fsdp', scatter_dimension=0, tiled=True)]
    all_gather x8 -> x5, waiting for transfers between devices: 703 us -> 71 us  [the longest x1 38.4 us: shards(): gate_up = lax.all_gather(gate_up, 'fsdp', axis=0, tiled=True)]
    ppermute x0 -> x32, waiting for transfers between devices: none -> 172 us  [swap(): return lax.ppermute(values, 'dp', [(i, i ^ mask) for i in range(4)])]
    unnamed x2 -> x0, blocking collectives: 81.1 us -> none
    dot_general x30 -> x28, matrix products: 234 us -> 165 us  [the longest x8 57.7 us: dot(): return jnp.dot(a, b, preferred_element_type=f32)]
    ppermute x0 -> x32, starting transfers between devices: none -> 37.1 us  [swap(): return lax.ppermute(values, 'dp', [(i, i ^ mask) for i in range(4)])]
  transfers between devices with their start and end apart: 16 -> 49, of which waited for: 15 -> 34; matrix products, arithmetic and copies ran while one was open for 6% -> 26% of each run, Pallas kernels for 0% -> 0%
where the time goes in v1:
time: 944 us; the launch traced here: 937 us
  waiting for transfers between devices  494 us (52%)
  matrix products  165 us (17%)
  local copies, waits for them, and re-layouts  112 us (12%)
  other arithmetic  76.6 us (8%)
  starting transfers between devices  56.6 us (6%)
  between operations  20.8 us (2%)
  blocking collectives  10.8 us (1%)
    ppermute x32, waiting for transfers between devices, swap(): return lax.ppermute(values, 'dp', [(i, i ^ mask) for i in range(4)])  172 us
    reduce_scatter x1, waiting for transfers between devices, shards(): lax.psum_scatter(down_wgrad, 'fsdp', scatter_dimension=0, tiled=True)  60.9 us
    dot_general x8, matrix products, dot(): return jnp.dot(a, b, preferred_element_type=f32)  57.7 us
    reduce_scatter x1, waiting for transfers between devices, shards(): lax.psum_scatter(up_wgrad, 'fsdp', scatter_dimension=0, tiled=True)  54.8 us
    dot_general x8, matrix products, dot_nt(): lax.dot_general(a, b, (((1,), (1,)), ((), ())), preferred_element_type=f32)  49.5 us
    reduce_scatter x1, waiting for transfers between devices, shards(): lax.psum_scatter(out_wgrad, 'fsdp', scatter_dimension=0, tiled=True)  48.3 us
    dot_general x6, matrix products, dot_tn(): lax.dot_general(a, b, (((0,), (0,)), ((), ())), preferred_element_type=f32)  48.1 us
    all_gather x1, waiting for transfers between devices, shards(): gate_up = lax.all_gather(gate_up, 'fsdp', axis=0, tiled=True)  38.4 us
  transfers between devices with their start and end apart: 49, of which 34 were waited for; matrix products, arithmetic and copies ran while one was open for 26% of the time, Pallas kernels for 0%

profile of v1, /device:TPU:0, one launch (start us, length us, event | category | flops | bytes accessed | tf_op | source)
XLA Modules:
  0.0 936.6 jit_solution(5467654187837435841)
XLA Ops:
  11.7 10.8 %all_to_all.30 = bf16[4,32,1024]{2,1,0:T(8,128)(2,1)} all-to-all(bf16[4,32,1024]{2,1,0:T(8,128)(2,1)S(1)} %copy.127), channel_id=1, replica_groups=mesh['dp'=4,'fsdp'=8] {'dp'}, dimensions={0} | all-to-all | bytes 524288 | tf_op jit(solution)/shard_map/all_to_all | solution.py:128
  41.6 14.4 %all-to-all-done.2 = bf16[4,64,1408]{2,1,0:T(8,128)(2,1)S(1)} async-done(((bf16[4,64,1408]{2,1,0:T(8,128)(2,1)}), bf16[4,64,1408]{2,1,0:T(8,128)(2,1)S(1)}, u32[]{:S(2)}, u32[]{:S(2)}) %all-to-all-start.2) | async-done | bytes 720928 | tf_op jit(solution)/shard_map/all_to_all | solution.py:128
  57.4 32.6 %all-gather.6.cloned.1.call-done = bf16[2048,1664]{1,0:T(8,128)(2,1)} async-done(((bf16[64,1664]{1,0:T(8,128)(2,1)}), bf16[2048,1664]{1,0:T(8,128)(2,1)}) %all-gather.6.cloned.1.call-update) | async-done | bytes 6815760 | tf_op jit(solution)/shard_map/all_gather | solution.py:184
  140.2 27.7 %collective-permute-done.2 = bf16[128,1536]{0,1:T(8,128)(2,1)S(1)} collective-permute-done((bf16[128,1536]{0,1:T(8,128)(2,1)S(1)}, bf16[128,1536]{0,1:T(8,128)(2,1)S(1)}, u32[]{:S(2)}, u32[]{:S(2)}) %collective-permute-start.2) | collective-permute-done | bytes 393248 | tf_op jit(solution)/shard_map/ppermute | solution.py:99
  219.4 14.7 %collective-permute-done.6 = bf16[256,2048]{1,0:T(8,128)(2,1)S(1)} collective-permute-done((bf16[256,2048]{1,0:T(8,128)(2,1)S(1)}, bf16[256,2048]{1,0:T(8,128)(2,1)S(1)}, u32[]{:S(2)}, u32[]{:S(2)}) %collective-permute-start.6) | collective-permute-done | bytes 1048608 | tf_op jit(solution)/shard_map/ppermute | solution.py:99
  261.1 11.8 %fusion.138 = f32[1024,1408]{1,0:T(8,128)} fusion(bf16[1024,2048]{1,0:T(8,128)(2,1)} %constant_dynamic-update-slice_fusion.10, bf16[1408,2048]{1,0:T(8,128)(2,1)} %all-gather.14.cloned.1.call-done), kind=kOutput, calls=%fused_computation.313 | convolution fusion | flops 5905580032 | bytes 15728640 | tf_op jit(solution)/shard_map/dot_general | solution.py:91
  272.9 9.6 %collective-permute-done.9 = bf16[256,2048]{0,1:T(8,128)(2,1)} collective-permute-done((bf16[256,2048]{0,1:T(8,128)(2,1)S(1)}, bf16[256,2048]{0,1:T(8,128)(2,1)}, u32[]{:S(2)}, u32[]{:S(2)}) %collective-permute-start.9) | collective-permute-done | bytes 1048608 | tf_op jit(solution)/shard_map/ppermute | solution.py:99
  298.6 38.4 %all-gather.12.cloned.1.call-done = bf16[2048,2816]{1,0:T(8,128)(2,1)} async-done(((bf16[256,2816]{1,0:T(8,128)(2,1)}), bf16[2048,2816]{1,0:T(8,128)(2,1)}) %all-gather.12.cloned.1.call-update) | async-done | bytes 11534352 | tf_op jit(solution)/shard_map/all_gather | solution.py:195
  337.0 12.4 %fusion.10 = f32[1024,1408]{1,0:T(8,128)} fusion(bf16[1024,2048]{0,1:T(8,128)(2,1)} %constant_dynamic-update-slice_fusion.5, bf16[2048,2816]{1,0:T(8,128)(2,1)} %all-gather.12.cloned.1.call-done), kind=kOutput, calls=%fused_computation.21 | convolution fusion | flops 5905580032 | bytes 15728640 | tf_op jit(solution)/shard_map/dot_general | solution.py:87
  349.4 15.5 %multiply_convert_fusion.1 = (bf16[1024,1408]{1,0:T(8,128)(2,1)}, bf16[1024,1408]{1,0:T(8,128)(2,1)}, bf16[1024,1408]{1,0:T(8,128)(2,1)}) fusion(f32[1024,1408]{1,0:T(8,128)} %fusion.138, f32[1024,1408]{1,0:T(8,128)} %fusion.10, bf16[1024,2048]{0,1:T(8,128)(2,1)} %constant_dynamic-update-slice_fusion.5, bf16[2048,2816]{1,0:T(8,128)(2,1)S(1)} %copy-done.52), kind=kOutput, calls=%fused_computation.9 | convolution fusion | flops 5927206912 | bytes 30146560 | tf_op jit(solution)/shard_map/dot_general | solution.py:87
  387.5 19.3 %collective-permute-done.22 = bf16[256,2048]{1,0:T(8,128)(2,1)S(1)} collective-permute-done((bf16[256,2048]{1,0:T(8,128)(2,1)S(1)}, bf16[256,2048]{1,0:T(8,128)(2,1)S(1)}, u32[]{:S(2)}, u32[]{:S(2)}) %collective-permute-start.22) | collective-permute-done | bytes 1048608 | tf_op jit(solution)/shard_map/ppermute | solution.py:99
  412.5 9.1 collective-permute-done.21
  438.8 20.1 %collective-permute-done.25 = bf16[256,2048]{1,0:T(8,128)(2,1)S(1)} collective-permute-done((bf16[256,2048]{1,0:T(8,128)(2,1)S(1)}, bf16[256,2048]{1,0:T(8,128)(2,1)S(1)}, u32[]{:S(2)}, u32[]{:S(2)}) %collective-permute-start.25) | collective-permute-done | bytes 1048608 | tf_op jit(solution)/shard_map/ppermute | solution.py:99
  462.1 9.2 collective-permute-done.26
  516.9 9.9 %collective-permute-done.30 = bf16[256,1536]{1,0:T(8,128)(2,1)} collective-permute-done((bf16[256,1536]{1,0:T(8,128)(2,1)}, bf16[256,1536]{1,0:T(8,128)(2,1)}, u32[]{:S(2)}, u32[]{:S(2)}) %collective-permute-start.30) | collective-permute-done | bytes 786464 | tf_op jit(solution)/shard_map/ppermute | solution.py:99
  577.1 10.9 %convolution_convert_fusion.3 = bf16[2048,1408]{1,0:T(8,128)(2,1)} fusion(bf16[1024,2048]{0,1:T(8,128)(2,1)} %constant_dynamic-update-slice_fusion.5, bf16[1024,1408]{1,0:T(8,128)(2,1)} %get-tuple-element.41), kind=kOutput, calls=%fused_computation.4 | convolution fusion | flops 5908463616 | bytes 12845056 | tf_op jit(solution)/shard_map/dot_general | solution.py:95
  588.1 10.9 %convolution_convert_fusion.2 = bf16[2048,1408]{1,0:T(8,128)(2,1)} fusion(bf16[1024,2048]{0,1:T(8,128)(2,1)} %constant_dynamic-update-slice_fusion.5, bf16[1024,1408]{1,0:T(8,128)(2,1)} %get-tuple-element.42), kind=kOutput, calls=%fused_computation.3 | convolution fusion | flops 5908463616 | bytes 12845056 | tf_op jit(solution)/shard_map/dot_general | solution.py:95
  599.2 10.5 %convolution_convert_fusion.1 = bf16[1408,2048]{1,0:T(8,128)(2,1)} fusion(bf16[1024,1408]{1,0:T(8,128)(2,1)} %get-tuple-element.43, bf16[1024,2048]{1,0:T(8,128)(2,1)} %constant_dynamic-update-slice_fusion.10), kind=kOutput, calls=%fused_computation.2 | convolution fusion | flops 5908463616 | bytes 12845056 | tf_op jit(solution)/shard_map/dot_general | solution.py:95
  634.2 20.5 %collective-permute-done.14 = bf16[256,2048]{1,0:T(8,128)(2,1)S(1)} collective-permute-done((bf16[256,2048]{1,0:T(8,128)(2,1)S(1)}, bf16[256,2048]{1,0:T(8,128)(2,1)S(1)}, u32[]{:S(2)}, u32[]{:S(2)}) %collective-permute-start.14) | collective-permute-done | bytes 1048608 | tf_op jit(solution)/shard_map/ppermute | solution.py:99
  677.2 37.8 %reduce-scatter.16.cloned.1.call-done = bf16[256,1408]{1,0:T(8,128)(2,1)} async-done(((bf16[2048,1408]{1,0:T(8,128)(2,1)}), bf16[256,1408]{1,0:T(8,128)(2,1)}) %reduce-scatter.16.cloned.1.call-update) | async-done | bytes 720912 | tf_op jit(solution)/shard_map/reduce_scatter | solution.py:271
  725.8 54.8 %reduce-scatter.18.cloned.1.call-done = bf16[256,1408]{1,0:T(8,128)(2,1)} async-done(((bf16[2048,1408]{1,0:T(8,128)(2,1)}), bf16[256,1408]{1,0:T(8,128)(2,1)}) %reduce-scatter.18.cloned.1.call-update) | async-done | bytes 720912 | tf_op jit(solution)/shard_map/reduce_scatter | solution.py:272
  785.1 60.9 %reduce-scatter.20.cloned.1.call-done = bf16[176,2048]{1,0:T(8,128)(2,1)} async-done(((bf16[1408,2048]{1,0:T(8,128)(2,1)}), bf16[176,2048]{1,0:T(8,128)(2,1)}) %reduce-scatter.20.cloned.1.call-update) | async-done | bytes 720912 | tf_op jit(solution)/shard_map/reduce_scatter | solution.py:270
  848.4 48.3 %reduce-scatter.14.cloned.1.call-done = bf16[128,2048]{1,0:T(8,128)(2,1)} async-done(((bf16[1024,2048]{1,0:T(8,128)(2,1)}), bf16[128,2048]{1,0:T(8,128)(2,1)}) %reduce-scatter.14.cloned.1.call-update) | async-done | bytes 524304 | tf_op jit(solution)/shard_map/reduce_scatter | solution.py:280
  902.6 21.6 %reduce-scatter.10.cloned.1.call-done = bf16[64,1664]{1,0:T(8,128)(2,1)} async-done(((bf16[256,1664]{1,0:T(8,128)(2,1)}), bf16[64,1664]{1,0:T(8,128)(2,1)}) %reduce-scatter.10.cloned.1.call-update) | async-done | bytes 213008 | tf_op jit(solution)/shard_map/reduce_scatter | solution.py:324
  (396 shorter events, 384.0 us)
Async XLA Ops:
  7.2 82.8 %all-gather.6.cloned.1.call-start = ((), (), s32[]{:S(2)}) async-start(), calls=%async_computation.13 | async-start | bytes 7028736 | tf_op jit(solution)/shard_map/all_gather | solution.py:184
  10.4 162.6 %all-gather.8.cloned.1.call-start = ((), (), s32[]{:S(2)}) async-start(), calls=%async_computation.14 | async-start | bytes 2359296 | tf_op jit(solution)/shard_map/all_gather | solution.py:192
  22.5 179.0 %all-gather.10.cloned.1.call-start = ((), (), s32[]{:S(2)}) async-start(), calls=%async_computation.15 | async-start | bytes 4718592 | tf_op jit(solution)/shard_map/all_gather | solution.py:193
  23.3 237.8 %all-gather.14.cloned.1.call-start = ((), (), s32[]{:S(2)}) async-start(), calls=%async_computation.17 | async-start | bytes 6488064 | tf_op jit(solution)/shard_map/all_gather | solution.py:198
  41.2 295.8 %all-gather.12.cloned.1.call-start = ((), (), s32[]{:S(2)}) async-start(), calls=%async_computation.16 | async-start | bytes 12976128 | tf_op jit(solution)/shard_map/all_gather | solution.py:195
  57.3 611.2 %reduce-scatter.12.cloned.1.call-start = ((), (), s32[]{:S(2)}) async-start(), calls=%async_computation.20 | async-start | bytes 2359296 | tf_op jit(solution)/shard_map/reduce_scatter | solution.py:298
  123.5 86.5 %collective-permute-start.17 = (bf16[256,2048]{1,0:T(8,128)(2,1)}, bf16[256,2048]{1,0:T(8,128)(2,1)}, u32[]{:S(2)}, u32[]{:S(2)}) collective-permute-start(bf16[256,2048]{1,0:T(8,128)(2,1)} %get-tuple-element.28), channel_id=1, source_target_pairs={{0,16},{8,24},{16,0},{24,8},{1,17},{9,25},{17,1},{25,9},{2,18},{10... | collective-permute-start | bytes 3145736 | tf_op jit(solution)/shard_map/ppermute | solution.py:99
  124.9 86.8 %collective-permute-start.16 = (bf16[256,2048]{1,0:T(8,128)(2,1)}, bf16[256,2048]{1,0:T(8,128)(2,1)}, u32[]{:S(2)}, u32[]{:S(2)}) collective-permute-start(bf16[256,2048]{1,0:T(8,128)(2,1)} %get-tuple-element.28), channel_id=1, source_target_pairs={{0,8},{8,0},{16,24},{24,16},{1,9},{9,1},{17,25},{25,17},{2,10},{10... | collective-permute-start | bytes 3145736 | tf_op jit(solution)/shard_map/ppermute | solution.py:99
  137.8 31.3 %collective-permute-start.3 = (bf16[128,1536]{0,1:T(8,128)(2,1)S(1)}, bf16[128,1536]{0,1:T(8,128)(2,1)S(1)}, u32[]{:S(2)}, u32[]{:S(2)}) collective-permute-start(bf16[128,1536]{0,1:T(8,128)(2,1)S(1)} %slice.547), channel_id=1, source_target_pairs={{0,16},{8,24},{16,0},{24,8},{1,17},{9,25},{17,1},{25,9},{2,18},{10... | collective-permute-start | bytes 1179656 | tf_op jit(solution)/shard_map/ppermute | solution.py:99
  139.4 28.5 %collective-permute-start.2 = (bf16[128,1536]{0,1:T(8,128)(2,1)S(1)}, bf16[128,1536]{0,1:T(8,128)(2,1)S(1)}, u32[]{:S(2)}, u32[]{:S(2)}) collective-permute-start(bf16[128,1536]{0,1:T(8,128)(2,1)S(1)} %slice.546), channel_id=1, source_target_pairs={{0,8},{8,0},{16,24},{24,16},{1,9},{9,1},{17,25},{25,17},{2,10},{10... | collective-permute-start | bytes 1179656 | tf_op jit(solution)/shard_map/ppermute | solution.py:99
  207.9 26.2 %collective-permute-start.6 = (bf16[256,2048]{1,0:T(8,128)(2,1)S(1)}, bf16[256,2048]{1,0:T(8,128)(2,1)S(1)}, u32[]{:S(2)}, u32[]{:S(2)}) collective-permute-start(bf16[256,2048]{1,0:T(8,128)(2,1)S(1)} %pad_maximum_fusion.6), channel_id=1, source_target_pairs={{0,16},{8,24},{16,0},{24,8},{1,17},{9,25},{17,1},{25,9},{2,18},{10... | collective-permute-start | bytes 3145736 | tf_op jit(solution)/shard_map/ppermute | solution.py:99
  208.5 26.2 %collective-permute-start.4 = (bf16[256,2048]{1,0:T(8,128)(2,1)S(1)}, bf16[256,2048]{1,0:T(8,128)(2,1)S(1)}, u32[]{:S(2)}, u32[]{:S(2)}) collective-permute-start(bf16[256,2048]{1,0:T(8,128)(2,1)S(1)} %pad_maximum_fusion.5), channel_id=1, source_target_pairs={{0,8},{8,0},{16,24},{24,16},{1,9},{9,1},{17,25},{25,17},{2,10},{10... | collective-permute-start | bytes 3145736 | tf_op jit(solution)/shard_map/ppermute | solution.py:99
  211.1 34.8 %collective-permute-start.18 = (bf16[128,2048]{1,0:T(8,128)(2,1)S(1)}, bf16[128,2048]{1,0:T(8,128)(2,1)S(1)}, u32[]{:S(2)}, u32[]{:S(2)}) collective-permute-start(bf16[128,2048]{1,0:T(8,128)(2,1)S(1)} %slice.586), channel_id=1, source_target_pairs={{0,8},{8,0},{16,24},{24,16},{1,9},{9,1},{17,25},{25,17},{2,10},{10... | collective-permute-start | bytes 1572872 | tf_op jit(solution)/shard_map/ppermute | solution.py:99
  212.9 33.9 %collective-permute-start.19 = (bf16[128,2048]{1,0:T(8,128)(2,1)S(1)}, bf16[128,2048]{1,0:T(8,128)(2,1)S(1)}, u32[]{:S(2)}, u32[]{:S(2)}) collective-permute-start(bf16[128,2048]{1,0:T(8,128)(2,1)S(1)} %slice.587), channel_id=1, source_target_pairs={{0,16},{8,24},{16,0},{24,8},{1,17},{9,25},{17,1},{25,9},{2,18},{10... | collective-permute-start | bytes 1572872 | tf_op jit(solution)/shard_map/ppermute | solution.py:99
  260.3 25.6 %collective-permute-start.8 = (bf16[256,2048]{0,1:T(8,128)(2,1)S(1)}, bf16[256,2048]{0,1:T(8,128)(2,1)}, u32[]{:S(2)}, u32[]{:S(2)}) collective-permute-start(bf16[256,2048]{0,1:T(8,128)(2,1)S(1)} %bitcast.217), channel_id=1, source_target_pairs={{0,8},{8,0},{16,24},{24,16},{1,9},{9,1},{17,25},{25,17},{2,10},{10... | collective-permute-start | bytes 3145736 | tf_op jit(solution)/shard_map/ppermute | solution.py:99
  381.4 25.4 %collective-permute-start.22 = (bf16[256,2048]{1,0:T(8,128)(2,1)S(1)}, bf16[256,2048]{1,0:T(8,128)(2,1)S(1)}, u32[]{:S(2)}, u32[]{:S(2)}) collective-permute-start(bf16[256,2048]{1,0:T(8,128)(2,1)S(1)} %pad_maximum_fusion.10), channel_id=1, source_target_pairs={{0,16},{8,24},{16,0},{24,8},{1,17},{9,25},{17,1},{25,9},{2,18},{10... | collective-permute-start | bytes 3145736 | tf_op jit(solution)/shard_map/ppermute | solution.py:99
  516.4 155.6 %reduce-scatter.8.cloned.1.call-start = ((), (), s32[]{:S(2)}) async-start(), calls=%async_computation.18 | async-start | bytes 7667712 | tf_op jit(solution)/shard_map/reduce_scatter | solution.py:323
  577.0 138.0 %reduce-scatter.16.cloned.1.call-start = ((), (), s32[]{:S(2)}) async-start(), calls=%async_computation.22 | async-start | bytes 6488064 | tf_op jit(solution)/shard_map/reduce_scatter | solution.py:271
  588.0 192.6 %reduce-scatter.18.cloned.1.call-start = ((), (), s32[]{:S(2)}) async-start(), calls=%async_computation.23 | async-start | bytes 6488064 | tf_op jit(solution)/shard_map/reduce_scatter | solution.py:272
  598.9 247.1 %reduce-scatter.20.cloned.1.call-start = ((), (), s32[]{:S(2)}) async-start(), calls=%async_computation.24 | async-start | bytes 6488064 | tf_op jit(solution)/shard_map/reduce_scatter | solution.py:270
  609.7 287.0 %reduce-scatter.14.cloned.1.call-start = ((), (), s32[]{:S(2)}) async-start(), calls=%async_computation.21 | async-start | bytes 4718592 | tf_op jit(solution)/shard_map/reduce_scatter | solution.py:280
  671.9 252.3 %reduce-scatter.10.cloned.1.call-start = ((), (), s32[]{:S(2)}) async-start(), calls=%async_computation.19 | async-start | bytes 1064960 | tf_op jit(solution)/shard_map/reduce_scatter | solution.py:324
  715.0 65.6 %all-to-all-start.4 = ((bf16[4,64,1408]{2,1,0:T(8,128)(2,1)}), bf16[4,64,1408]{2,1,0:T(8,128)(2,1)}, u32[]{:S(2)}, u32[]{:S(2)}) async-start(bf16[4,64,1408]{2,1,0:T(8,128)(2,1)} %bitcast.238), calls=%async_computation.9 | async-start | bytes 1441792 | tf_op jit(solution)/shard_map/all_to_all | solution.py:133
  780.6 120.6 %all-to-all-start.5 = ((bf16[4,64,1408]{2,1,0:T(8,128)(2,1)}), bf16[4,64,1408]{2,1,0:T(8,128)(2,1)S(1)}, u32[]{:S(2)}, u32[]{:S(2)}) async-start(bf16[4,64,1408]{2,1,0:T(8,128)(2,1)} %bitcast.237), calls=%async_computation.11 | async-start | bytes 1441792 | tf_op jit(solution)/shard_map/all_to_all | solution.py:133
  (82 other events, 791.7 us)
Sparse Core Ops, SparseCore 0:
  11.4 78.4 all-gather.5
  91.6 27.6 all-gather.7
  120.8 46.6 all-gather.9
  169.0 59.1 all-gather.13
  230.2 106.7 all-gather.11
  516.5 32.9 reduce-scatter.11
  577.1 72.2 reduce-scatter.7
  651.8 63.2 reduce-scatter.15
  717.3 63.2 reduce-scatter.17
  782.7 63.2 reduce-scatter.19
  848.3 48.3 reduce-scatter.13
  899.5 24.6 reduce-scatter.9

commit v2 on v1

v2 whole, which is shorter than its diff:
```python
import functools
import math

import jax
import jax.numpy as jnp
from jax import lax
from jax.experimental import pallas as pl
from jax.experimental.pallas import tpu as pltpu
from jax.sharding import PartitionSpec as P

H = 16
HD = 256
PAD = 32

eps = 1e-06
rope_base = 10000.0
masked_score = -1e30
ALL = ("y", "x", "zh", "zl", "r")
DP = ("y", "x")
GROUP = ("x", "y")
RING = ("zh", "zl", "r")
f32 = jnp.float32
bf16 = jnp.bfloat16


def layout(lengths, row_total):
    padded = (lengths + PAD - 1) // PAD * PAD
    count = lengths.shape[0]
    ends = []
    for s in range(count):
        ends.append(padded[s] if s == 0 else ends[-1] + padded[s])
    row = lax.broadcasted_iota(jnp.int32, (row_total, 1), 0)
    segment = jnp.zeros_like(row)
    start = jnp.zeros_like(row)
    alive = jnp.zeros(row.shape, jnp.bool_)
    for s in range(count):
        first = ends[s] - padded[s]
        member = (row >= first) & (row < ends[s])
        segment = jnp.where(member, s + 1, segment)
        start = jnp.where(member, first, start)
        alive = alive | (member & (row - first < lengths[s]))
    return row - start, alive, segment


def angles(offset, head_size):
    half_width = head_size // 2
    frequency = jnp.exp(
        jnp.arange(half_width, dtype=f32) * (-2.0 * math.log(rope_base) / head_size)
    )
    phase = offset.astype(f32) * frequency[None, :]
    return (jnp.cos(phase), jnp.sin(phase))


def rotate(values, cos_part, sin_part):
    half_width = values.shape[-1] // 2
    first_half = values[..., :half_width]
    second_half = values[..., half_width:]
    return jnp.concatenate(
        [
            first_half * cos_part - second_half * sin_part,
            second_half * cos_part + first_half * sin_part,
        ],
        axis=-1,
    )


def normalize(values, scale_gain):
    factor = lax.rsqrt(jnp.mean(values * values, axis=-1, keepdims=True) + eps)
    normed = values * factor
    return (normed * scale_gain, normed, factor)


def normalize_back(upstream, normed, factor, scale_gain):
    scaled = upstream * scale_gain
    gain_grad = jnp.sum(upstream * normed, axis=0)
    inner_mean = jnp.mean(scaled * normed, axis=-1, keepdims=True)
    return (factor * (scaled - normed * inner_mean), gain_grad)


def dot(a, b):
    return jnp.dot(a, b, preferred_element_type=f32)


def dot_nt(a, b):
    return lax.dot_general(a, b, (((1,), (1,)), ((), ())), preferred_element_type=f32)


def dot_tn(a, b):
    return lax.dot_general(a, b, (((0,), (0,)), ((), ())), preferred_element_type=f32)


def after(values, *others):
    return lax.optimization_barrier((values, others))[0]


def trade(values, axis):
    return lax.ppermute(values, axis, [(0, 1), (1, 0)])


def gather_quad(values, first, second):
    half = values.shape[0] // 2
    one = trade(values, first)
    two = trade(values, second)
    three = jnp.concatenate([trade(two[:half], first), trade(one[half:], second)], axis=0)
    return [values, one, two, three]


def scatter_quad(slots, first, second):
    s0, s1, s2, s3 = slots
    half = s0.shape[0] // 2
    ra = trade(jnp.concatenate([s1[:half], s3[:half]], axis=0), first)
    rb = trade(jnp.concatenate([s2[half:], s3[half:]], axis=0), second)
    pass_a = (s2[:half].astype(f32) + ra[half:].astype(f32)).astype(bf16)
    pass_b = (s1[half:].astype(f32) + rb[half:].astype(f32)).astype(bf16)
    last_a = trade(pass_a, second)
    last_b = trade(pass_b, first)
    top = s0[:half].astype(f32) + ra[:half].astype(f32) + last_a.astype(f32)
    low = s0[half:].astype(f32) + rb[:half].astype(f32) + last_b.astype(f32)
    return jnp.concatenate([top, low], axis=0)


def scatter_rows(own, others, first, second):
    rows = own.shape[0]
    slots = [own] + [others[i * rows : (i + 1) * rows] for i in range(3)]
    return scatter_quad(slots, first, second)


def split_cores(values, cores):
    if cores != 2:
        return lax.psum_scatter(values, "r", scatter_dimension=4, tiled=False), None
    core = lax.axis_index("r")
    mine = lax.dynamic_index_in_dim(values, core, 4, keepdims=False)
    theirs = lax.dynamic_index_in_dim(values, 1 - core, 4, keepdims=False)
    return mine, trade(theirs.reshape(-1, values.shape[-1]), "r").reshape(mine.shape)


def join_cores(mine, theirs):
    if theirs is None:
        return mine
    return (mine.astype(f32) + theirs.astype(f32)).astype(bf16)


def scatter_small(values, cores):
    n, c = values.shape[5:]
    total = join_cores(*split_cores(values, cores)).reshape(4, 4, n, c)
    me = lax.axis_index("y") * 2 + lax.axis_index("x")
    slots = [lax.dynamic_index_in_dim(total, me ^ code, 0, keepdims=False) for code in range(4)]
    total = scatter_quad([v.reshape(4 * n, c) for v in slots], "x", "y").astype(bf16).reshape(4, n, c)
    me = lax.axis_index("zh") * 2 + lax.axis_index("zl")
    slots = [lax.dynamic_index_in_dim(total, me ^ code, 0, keepdims=False) for code in range(4)]
    return scatter_quad(slots, "zl", "zh")


def turn(values, cos_part, sin_part):
    half = values.shape[-1] // 2
    one, two = values[:, :half], values[:, half:]
    return jnp.concatenate([one * cos_part - two * sin_part, two * cos_part + one * sin_part], axis=-1)


def probabilities(query_rot, key_rot, seg_ref, code_ref):
    rows = query_rot.shape[0]
    scores = dot_nt(query_rot, key_rot) * (1.0 / math.sqrt(HD))
    i = lax.broadcasted_iota(jnp.int32, (rows, rows), 0)
    j = lax.broadcasted_iota(jnp.int32, (rows, rows), 1)
    allowed = ((seg_ref[...] == code_ref[0]) & (j <= i)) | (i == j)
    scores = jnp.where(allowed, scores, masked_score)
    expo = jnp.exp(scores - jnp.max(scores, axis=-1, keepdims=True))
    return expo / jnp.sum(expo, axis=-1, keepdims=True)


def attend_kernel(
    latent_ref, weight_ref, key_ref, value_ref, cos_ref, sin_ref, seg_ref, code_ref, query_ref, mix_ref
):
    query_rot = turn(dot(latent_ref[...], weight_ref[...]), cos_ref[...], sin_ref[...]).astype(bf16)
    query_ref[...] = query_rot
    probs = probabilities(query_rot, key_ref[...], seg_ref, code_ref)
    mix_ref[...] = dot(probs.astype(bf16), value_ref[...]).astype(bf16)


def attend(packed, query_full, cos_part, sin_part, segment, code, rows, heads):
    total, latent_width = packed.shape[0], query_full.shape[0]
    last = latent_width // HD
    block = pl.BlockSpec((rows, HD), lambda m, h: (m, h))
    trig = pl.BlockSpec((rows, HD // 2), lambda m, h: (m, 0))
    out = jax.ShapeDtypeStruct((total, heads * HD), bf16)
    return pl.pallas_call(
        attend_kernel,
        grid=(total // rows, heads),
        in_specs=[
            pl.BlockSpec((rows, latent_width), lambda m, h: (m, 0)),
            pl.BlockSpec((latent_width, HD), lambda m, h: (0, h)),
            pl.BlockSpec((rows, HD), lambda m, h: (m, last)),
            pl.BlockSpec((rows, HD), lambda m, h: (m, last + 1)),
            trig,
            trig,
            pl.BlockSpec((rows, 1), lambda m, h: (m, 0)),
            pl.BlockSpec((1, 1, rows), lambda m, h: (m, 0, 0)),
        ],
        out_specs=[block, block],
        out_shape=[out, out],
        compiler_params=pltpu.CompilerParams(vmem_limit_bytes=32 * 2**20),
        cost_estimate=pl.CostEstimate(
            flops=2 * total * heads * HD * (latent_width + 2 * rows),
            bytes_accessed=total * heads * HD * 4 + total * latent_width * 3,
            transcendentals=total * heads * rows,
        ),
    )(packed, query_full, packed, packed, cos_part, sin_part, segment, code)


def attend_back_kernel(
    heads,
    grad_ref,
    out_ref,
    weight_ref,
    query_ref,
    key_ref,
    value_ref,
    cos_ref,
    sin_ref,
    seg_ref,
    code_ref,
    query_grad_ref,
    packed_ref,
    total_ref,
):
    head = pl.program_id(1)
    latent_width = weight_ref.shape[0]
    scale = 1.0 / math.sqrt(HD)
    query_rot, key_rot, value_low = query_ref[...], key_ref[...], value_ref[...]
    mixture_grad = dot_nt(grad_ref[...], out_ref[...]).astype(bf16)
    probs = probabilities(query_rot, key_rot, seg_ref, code_ref)
    probs_grad = dot_nt(mixture_grad, value_low)
    row_dot = jnp.sum(probs * probs_grad, axis=-1, keepdims=True)
    score_grad = (probs * (probs_grad - row_dot)).astype(bf16)
    query_rot_grad = dot(score_grad, key_rot) * scale
    query_grad = turn(query_rot_grad, cos_ref[...], -sin_ref[...]).astype(bf16)
    query_grad_ref[...] = query_grad

    @pl.when(head == 0)
    def _():
        total_ref[...] = jnp.zeros_like(total_ref)

    total_ref[:, :latent_width] += dot_nt(query_grad, weight_ref[...])
    total_ref[:, latent_width : latent_width + HD] += dot_tn(score_grad, query_rot) * scale
    total_ref[:, latent_width + HD :] += dot_tn(probs.astype(bf16), mixture_grad)

    @pl.when(head == heads - 1)
    def _():
        packed_ref[...] = total_ref[...].astype(bf16)


def attend_back(attn_grad, out_full, query_full, query_rot, packed, cos_part, sin_part, segment, code, rows, heads):
    total, width = attn_grad.shape
    latent_width = query_full.shape[0]
    last = latent_width // HD
    block = pl.BlockSpec((rows, HD), lambda m, h: (m, h))
    trig = pl.BlockSpec((rows, HD // 2), lambda m, h: (m, 0))
    return pl.pallas_call(
        functools.partial(attend_back_kernel, heads),
        grid=(total // rows, heads),
        in_specs=[
            pl.BlockSpec((rows, width), lambda m, h: (m, 0)),
            pl.BlockSpec((HD, width), lambda m, h: (h, 0)),
            pl.BlockSpec((latent_width, HD), lambda m, h: (0, h)),
            block,
            pl.BlockSpec((rows, HD), lambda m, h: (m, last)),
            pl.BlockSpec((rows, HD), lambda m, h: (m, last + 1)),
            trig,
            trig,
            pl.BlockSpec((rows, 1), lambda m, h: (m, 0)),
            pl.BlockSpec((1, 1, rows), lambda m, h: (m, 0, 0)),
        ],
        out_specs=[block, pl.BlockSpec((rows, packed.shape[1]), lambda m, h: (m, 0))],
        out_shape=[
            jax.ShapeDtypeStruct((total, heads * HD), bf16),
            jax.ShapeDtypeStruct(packed.shape, bf16),
        ],
        scratch_shapes=[pltpu.VMEM((rows, packed.shape[1]), f32)],
        compiler_params=pltpu.CompilerParams(vmem_limit_bytes=32 * 2**20),
        cost_estimate=pl.CostEstimate(
            flops=2 * total * heads * HD * (width + latent_width + 5 * rows),
            bytes_accessed=total * heads * HD * 8 + total * width * 4,
            transcendentals=total * heads * rows,
        ),
    )(attn_grad, out_full, query_full, query_rot, packed, packed, cos_part, sin_part, segment, code)


def by_member(values, members):
    me = lax.axis_index(DP)
    step = values.shape[1] // members
    return jnp.concatenate(
        [lax.dynamic_slice_in_dim(values, (me ^ slot) * step, step, 1) for slot in range(members)], axis=1
    )


def columns_in(weight, members):
    rows, width = weight.shape
    cut = weight.reshape(rows, members, width // members).transpose(1, 0, 2)
    return lax.all_to_all(cut, DP, 0, 0, tiled=True)


def columns_back(grad):
    members, rows, width = grad.shape
    cut = lax.all_to_all(grad, DP, 0, 0, tiled=True)
    return cut.transpose(1, 0, 2).reshape(rows, members * width).astype(f32)


def shards(
    members,
    ring,
    cores,
    tokens,
    lengths,
    attn_gain,
    query_down,
    query_gain,
    query_up,
    key_weight,
    value_weight,
    out_weight,
    mlp_gain,
    gate_weight,
    up_weight,
    down_weight,
    cotangent,
):
    rows = tokens.shape[0]
    width = tokens.shape[1]
    latent_width = query_down.shape[1]
    heads = H // members
    devices = members * ring
    score_scale = 1.0 / math.sqrt(HD)
    d_rows = query_down.shape[0]

    def column(v):
        v = v.astype(bf16).reshape(-1, 1)
        return jnp.pad(v, ((0, d_rows - v.shape[0]), (0, 0)))

    extra = jnp.concatenate(
        [column(attn_gain), column(mlp_gain), column(query_gain), column(lengths[0])], axis=1
    )
    extra = jnp.pad(extra, ((0, 0), (0, 128 - extra.shape[1])))
    small = jnp.concatenate([query_down, key_weight, value_weight, extra], axis=1)
    small = lax.all_gather(small, RING, axis=0, tiled=True)
    gate_up = jnp.stack([gate_weight, up_weight]).reshape(2, d_rows, members, -1)
    gate_up = gate_up.transpose(2, 1, 0, 3).reshape(members, d_rows, -1)
    gate_up = lax.all_to_all(gate_up, DP, 0, 0, tiled=True)
    query_own = columns_in(query_up, members)
    small = after(small, gate_up, query_own)
    small_parts = gather_quad(small, *GROUP)
    query_full = lax.all_gather(query_own, RING, axis=1, tiled=True)
    query_full = query_full.reshape(latent_width, heads * HD)
    out_full = lax.all_gather(after(out_weight, small), RING, axis=0, tiled=True)
    gate_up = after(gate_up, small)
    gate_up = lax.all_gather(gate_up, RING, axis=1, tiled=True).reshape(width, -1)
    cut = gate_up.shape[1] // 2
    down_full = lax.all_gather(after(down_weight, small), RING, axis=0, tiled=True)

    me, lane = lax.axis_index(DP), lax.axis_index(RING)
    qkv_parts = jnp.concatenate([part[:, : latent_width + 2 * HD] for part in small_parts], axis=0)
    extra = jnp.stack([part[:, latent_width + 2 * HD :] for part in small_parts])
    extra = [lax.dynamic_index_in_dim(extra, me ^ slot, 0, keepdims=False) for slot in range(members)]
    extra = jnp.concatenate(extra, axis=0).astype(f32).T
    attn_scale = extra[0:1]
    mlp_scale = extra[1:2]
    latent_scale = extra[2].reshape(devices, d_rows)[:, : query_gain.shape[0]].reshape(1, -1)
    all_lengths = extra[3].reshape(devices, d_rows)[:, : lengths.shape[1]].astype(jnp.int32)

    own_offset, own_alive, own_segment = layout(lengths[0], rows)
    living = own_alive.astype(f32)
    own_cos, own_sin = angles(own_offset, HD)
    parts = [(own_offset, own_alive, own_segment)]
    for slot in range(1, members):
        mine = lax.dynamic_slice_in_dim(all_lengths, (me ^ slot) * ring + lane, 1, 0)[0]
        parts.append(layout(mine, rows))
    offset = jnp.concatenate([p[0] for p in parts], axis=0)
    segment = jnp.concatenate([p[2] for p in parts], axis=0)
    code = jnp.stack([jnp.where(p[1], p[2], -1).reshape(1, rows) for p in parts])
    cos_part, sin_part = angles(offset, HD)

    grad_rows = cotangent.astype(f32)
    ffn_grad = jnp.concatenate(gather_quad((living * grad_rows).astype(bf16), *GROUP), axis=0)
    token_rows = tokens.astype(f32)
    attn_out, attn_normed, attn_factor = normalize(token_rows, attn_scale)
    attn_in = attn_out.astype(bf16)
    low = dot(by_member(attn_in, members), qkv_parts)
    latent = low[:, :latent_width]
    latent_out, latent_normed, latent_factor = normalize(latent, latent_scale)
    latent_in = latent_out.astype(bf16)
    key_own = rotate(low[:, latent_width : latent_width + HD], own_cos, own_sin)
    value_own = low[:, latent_width + HD :]
    packed = jnp.concatenate([latent_in, key_own.astype(bf16), value_own.astype(bf16)], axis=1)
    packed = jnp.concatenate(gather_quad(after(packed, ffn_grad), *GROUP), axis=0)
    query_rot, mixture = attend(packed, query_full, cos_part, sin_part, segment, code, rows, heads)
    attn_sum = scatter_rows(
        dot(mixture[:rows], out_full), dot(mixture[rows:], out_full).astype(bf16), *GROUP
    )
    residual = token_rows + living * attn_sum

    ffn_out, ffn_normed, ffn_factor = normalize(residual, mlp_scale)
    ffn_in = jnp.concatenate(gather_quad(ffn_out.astype(bf16), *GROUP), axis=0)
    gate_up_act = dot(ffn_in, gate_up)
    gate_act, up_act = gate_up_act[:, :cut], gate_up_act[:, cut:]
    sigmoid_gate = jax.nn.sigmoid(gate_act)
    silu_gate = gate_act * sigmoid_gate
    hidden = (silu_gate * up_act).astype(bf16)

    down_wgrad = dot_tn(hidden, ffn_grad).astype(bf16)
    down_share = lax.psum_scatter(down_wgrad, RING, scatter_dimension=0, tiled=True)

    hidden_grad = dot_nt(after(ffn_grad, down_wgrad), down_full)
    gate_grad = (
        hidden_grad * up_act * sigmoid_gate * (1.0 + gate_act * (1.0 - sigmoid_gate))
    ).astype(bf16)
    up_grad = (hidden_grad * silu_gate).astype(bf16)
    gate_up_grad = jnp.concatenate([gate_grad, up_grad], axis=1)
    ffn_in_grad = scatter_rows(
        dot_nt(gate_up_grad[:rows], gate_up), dot_nt(gate_up_grad[rows:], gate_up).astype(bf16), *GROUP
    )
    gate_up_wgrad = dot_tn(ffn_in, gate_up_grad).astype(bf16)
    residual_back, mlp_scale_grad = normalize_back(ffn_in_grad, ffn_normed, ffn_factor, mlp_scale)
    residual_grad = grad_rows + residual_back
    attn_grad = (living * residual_grad).astype(bf16)
    attn_grad = after(attn_grad, down_share, gate_up_wgrad)
    gate_up_share = lax.psum_scatter(
        gate_up_wgrad.reshape(members, width // members, -1), RING, scatter_dimension=1, tiled=True
    )
    attn_grad = jnp.concatenate(gather_quad(attn_grad, *GROUP), axis=0)
    query_grad, packed_grad = attend_back(
        attn_grad, out_full, query_full, query_rot, packed, cos_part, sin_part, segment, code, rows, heads
    )
    hidden = after(hidden, query_grad)
    ffn_sum = scatter_rows(
        dot(hidden[:rows], down_full), dot(hidden[rows:], down_full).astype(bf16), *GROUP
    )
    layer_out = (residual + living * ffn_sum).astype(bf16)
    packed_grad = scatter_rows(packed_grad[:rows], packed_grad[rows:], *GROUP)
    packed_grad = after(packed_grad, gate_up_share)
    out_wgrad = dot_tn(after(mixture, gate_up_share), attn_grad).astype(bf16)
    out_share = lax.psum_scatter(out_wgrad, RING, scatter_dimension=0, tiled=True)
    query_wgrad = dot_tn(packed[:, :latent_width], after(query_grad, gate_up_share)).astype(bf16)
    query_wgrad = query_wgrad.reshape(members, latent_width // members, heads * HD)
    query_share = lax.psum_scatter(query_wgrad, RING, scatter_dimension=1, tiled=True)
    latent_in_grad = packed_grad[:, :latent_width]
    key_grad = rotate(
        packed_grad[:, latent_width : latent_width + HD], own_cos, -own_sin
    ).astype(bf16)
    value_grad = packed_grad[:, latent_width + HD :].astype(bf16)
    latent_back, latent_scale_grad = normalize_back(
        latent_in_grad, latent_normed, latent_factor, latent_scale
    )
    qkv_grad = jnp.concatenate([latent_back.astype(bf16), key_grad, value_grad], axis=1)
    attn_in_grad = by_member(dot_nt(qkv_grad, qkv_parts), members)
    token_back, attn_scale_grad = normalize_back(attn_in_grad, attn_normed, attn_factor, attn_scale)
    tokens_grad = residual_grad + token_back

    small_grad = dot_tn(attn_in, qkv_grad)
    latent_column = jnp.pad(
        latent_scale_grad.reshape(devices, -1), ((0, 0), (0, d_rows - query_gain.shape[0]))
    ).reshape(-1)
    columns = jnp.stack([attn_scale_grad, mlp_scale_grad, latent_column])
    columns = jnp.pad(columns, ((0, 128 - 3), (0, 0))).T
    small_grad = jnp.concatenate([small_grad, columns], axis=1).astype(bf16)
    gate_up_share = after(gate_up_share, small_grad)
    gate_up_share = lax.all_to_all(gate_up_share, DP, 0, 0, tiled=True)
    gate_up_share = gate_up_share.reshape(members, d_rows, 2, -1).transpose(2, 1, 0, 3)
    gate_up_share = gate_up_share.reshape(2, d_rows, -1).astype(f32)
    small_share = scatter_small(small_grad.reshape(2, 2, 2, 2, cores, d_rows, -1), cores)
    return (
        layer_out,
        tokens_grad,
        small_share[:, latent_width + 2 * HD],
        small_share[:, :latent_width],
        small_share[: query_gain.shape[0], latent_width + 2 * HD + 2],
        columns_back(query_share),
        small_share[:, latent_width : latent_width + HD],
        small_share[:, latent_width + HD : latent_width + 2 * HD],
        out_share.astype(f32),
        small_share[:, latent_width + 2 * HD + 1],
        gate_up_share[0],
        gate_up_share[1],
        down_share.astype(f32),
    )


def solution(mesh):
    members, ring = mesh.shape["dp"], mesh.shape["fsdp"]
    cores = mesh.devices.size // 16
    fine = jax.sharding.Mesh(mesh.devices.reshape(2, 2, 2, 2, cores), ALL)
    matrix, vector = P(ALL, None), P(ALL)
    in_specs = (
        matrix,
        matrix,
        vector,
        matrix,
        vector,
        matrix,
        matrix,
        matrix,
        matrix,
        vector,
        matrix,
        matrix,
        matrix,
        matrix,
    )
    out_specs = (
        matrix,
        matrix,
        vector,
        matrix,
        vector,
        matrix,
        matrix,
        matrix,
        matrix,
        vector,
        matrix,
        matrix,
        matrix,
    )

    def body(*args):
        return shards(members, ring, cores, *args)

    return jax.shard_map(body, mesh=fine, in_specs=in_specs, out_specs=out_specs, check_vma=False)
```

time: 944 us -> 691 us (0.73)
  waiting for transfers between devices: 494 us -> 244 us
  Pallas kernels: 0 us -> 44.1 us
  matrix products: 165 us -> 125 us
  local copies, waits for them, and re-layouts: 112 us -> 78.2 us
  blocking collectives: 10.8 us -> 31.4 us
    reduce_scatter x7 -> x4, waiting for transfers between devices: 223 us -> 0.01 us  [the longest x1 0.01 us: shards(): lax.psum_scatter(down_wgrad, RING, scatter_dimension=0, tiled=True)]
    all_gather x5, waiting for transfers between devices: 71 us -> 0.04 us  [the longest x1 0.02 us: shards(): query_full = lax.all_gather(query_own, RING, axis=1, tiled=True)]
    ppermute x32 -> x45, waiting for transfers between devices: 172 us -> 240 us  [trade(): return lax.ppermute(values, axis, [(0, 1), (1, 0)])]
    pallas_call x0 -> x2, Pallas kernels: none -> 44.1 us  [the longest x1 29.2 us: attend_back(): pl.pallas_call(functools.partial(attend_back_kernel, heads), grid=(total...]
    all_to_all x5 -> x2, waiting for transfers between devices: 25.5 us -> 3.79 us  [the longest x1 3.79 us: shards(): gate_up_share = lax.all_to_all(gate_up_share, DP, 0, 0, tiled=True)]
    all_to_all x1 -> x2, blocking collectives: 10.8 us -> 31.4 us  [the longest x1 20.6 us: shards(): gate_up = lax.all_to_all(gate_up, DP, 0, 0, tiled=True)]
    dot_general x8 -> x6, matrix products: 57.7 us -> 39.3 us  [dot(): return jnp.dot(a, b, preferred_element_type=f32)]
    transpose x8 -> x0, local copies, waits for them, and re-layouts: 13.3 us -> none  [the longest x2 5.45 us: from_shards(): return cut.transpose(0, 2, 1, 3).reshape(rows, width)]
  transfers between devices with their start and end apart: 49 -> 56, of which waited for: 34 -> 31; matrix products, arithmetic and copies ran while one was open for 26% -> 38% of each run, Pallas kernels for 0% -> 6%
where the time goes in v2:
time: 691 us; the launch traced here: 684 us
  waiting for transfers between devices  244 us (35%)
  matrix products  125 us (18%)
  other arithmetic  85.4 us (12%)
  local copies, waits for them, and re-layouts  78.2 us (11%)
  starting transfers between devices  53.9 us (8%)
  Pallas kernels  44.1 us (6%)
  blocking collectives  31.4 us (5%)
  between operations  21.2 us (3%)
    ppermute x45, waiting for transfers between devices, trade(): return lax.ppermute(values, axis, [(0, 1), (1, 0)])  240 us
    ppermute x45, starting transfers between devices, trade(): return lax.ppermute(values, axis, [(0, 1), (1, 0)])  45.2 us
    dot_general x5, matrix products, dot_tn(): lax.dot_general(a, b, (((0,), (0,)), ((), ())), preferred_element_type=f32)  43.8 us
    dot_general x4, matrix products, dot_nt(): lax.dot_general(a, b, (((1,), (1,)), ((), ())), preferred_element_type=f32)  41.9 us
    dot_general x6, matrix products, dot(): return jnp.dot(a, b, preferred_element_type=f32)  39.3 us
    unnamed x166, local copies, waits for them, and re-layouts  35.7 us
    pallas_call x1, Pallas kernels, attend_back(): pl.pallas_call(functools.partial(attend_back_kernel, heads), grid=(total...  29.2 us
    all_to_all x1, blocking collectives, shards(): gate_up = lax.all_to_all(gate_up, DP, 0, 0, tiled=True)  20.6 us
  transfers between devices with their start and end apart: 56, of which 31 were waited for; matrix products, arithmetic and copies ran while one was open for 38% of the time, Pallas kernels for 6%

profile of v2, /device:TPU:0, one launch (start us, length us, event | category | flops | bytes accessed | tf_op | source)
XLA Modules:
  0.0 683.6 jit_solution(3441373242221190766)
XLA Ops:
  11.5 10.8 %all_to_all.20 = bf16[4,32,1024]{2,1,0:T(8,128)(2,1)} all-to-all(bf16[4,32,1024]{2,1,0:T(8,128)(2,1)S(1)} %bitcast.197), channel_id=1, replica_groups=mesh['y'=2,'x'=2,'zh'=2,'zl'=2,'r'=2] {'y','x'}, dimensions={0} | all-to-all | bytes 524288 | tf_op jit(solution)/shard_map/all_to_all | solution.py:299
  30.5 20.6 %all_to_all.21 = bf16[4,64,2816]{2,1,0:T(8,128)(2,1)} all-to-all(bf16[4,64,2816]{2,1,0:T(8,128)(2,1)S(1)} %reshape.683), channel_id=1, replica_groups=mesh['y'=2,'x'=2,'zh'=2,'zl'=2,'r'=2] {'y','x'}, dimensions={0} | all-to-all | bytes 2883584 | tf_op jit(solution)/shard_map/all_to_all | solution.py:347
  66.1 18.6 %collective-permute-done.5 = bf16[256,2048]{1,0:T(8,128)(2,1)S(1)} collective-permute-done((bf16[256,2048]{1,0:T(8,128)(2,1)}, bf16[256,2048]{1,0:T(8,128)(2,1)S(1)}, u32[]{:S(2)}, u32[]{:S(2)}) %collective-permute-start.5) | collective-permute-done | bytes 1048608 | tf_op jit(solution)/shard_map/ppermute | solution.py:97
  92.8 36.9 %collective-permute-done.6 = bf16[128,2048]{1,0:T(8,128)(2,1)S(1)} collective-permute-done((bf16[128,2048]{1,0:T(8,128)(2,1)}, bf16[128,2048]{1,0:T(8,128)(2,1)S(1)}, u32[]{:S(2)}, u32[]{:S(2)}) %collective-permute-start.6) | collective-permute-done | bytes 524320 | tf_op jit(solution)/shard_map/ppermute | solution.py:97
  206.0 15.0 %shard_map.237 = (bf16[1024,1024]{1,0:T(8,128)(2,1)S(1)}, bf16[1024,1024]{1,0:T(8,128)(2,1)S(1)}) custom-call(bf16[1024,1536]{1,0:T(8,128)(2,1)S(1)} %constant_dynamic-update-slice_fusion.7.latent_ref.key_ref.value_ref, bf16[1024,1024]{1,0:T(8,128)(2,1)S(1)} %bitcast.177, ...), custom_call_target="tpu_custom_call" | custom-call | flops 3221225472 | bytes 7340032 | tf_op jit(solution)/shard_map/pallas_call | solution.py:186
  223.6 6.1 convolution_convert_fusion.4
  233.1 17.1 %collective-permute-done.14 = bf16[256,2048]{1,0:T(8,128)(2,1)S(1)} collective-permute-done((bf16[256,2048]{1,0:T(8,128)(2,1)S(1)}, bf16[256,2048]{1,0:T(8,128)(2,1)S(1)}, u32[]{:S(2)}, u32[]{:S(2)}) %collective-permute-start.14) | collective-permute-done | bytes 1048608 | tf_op jit(solution)/shard_map/ppermute | solution.py:97
  272.7 18.0 %collective-permute-done.17 = bf16[256,2048]{1,0:T(8,128)(2,1)S(1)} collective-permute-done((bf16[256,2048]{1,0:T(8,128)(2,1)S(1)}, bf16[256,2048]{1,0:T(8,128)(2,1)S(1)}, u32[]{:S(2)}, u32[]{:S(2)}) %collective-permute-start.17) | collective-permute-done | bytes 1048608 | tf_op jit(solution)/shard_map/ppermute | solution.py:97
  303.5 17.4 %fusion.134 = f32[1024,2816]{1,0:T(8,128)S(1)} fusion(bf16[1024,2048]{1,0:T(8,128)(2,1)} %constant_dynamic-update-slice_fusion.12, bf16[2048,2816]{1,0:T(8,128)(2,1)} %bitcast.204), kind=kOutput, calls=%fused_computation.350 | convolution fusion | flops 11811160064 | bytes 27262976 | tf_op jit(solution)/shard_map/dot_general | solution.py:81
  327.9 8.2 %convolution_convert_fusion.2 = bf16[1408,2048]{1,0:T(8,128)(2,1)} fusion(bf16[1024,1408]{1,0:T(8,128)(2,1)S(1)} %multiply_convert_fusion.2, bf16[1024,2048]{1,0:T(8,128)(2,1)S(1)} %copy-done.53), kind=kOutput, calls=%fused_computation.4 | convolution fusion | flops 5908463616 | bytes 12845056 | tf_op jit(solution)/shard_map/dot_general | solution.py:89
  336.2 14.7 %multiply_convert_fusion.1 = (bf16[1024,1408]{1,0:T(8,128)(2,1)S(1)}, bf16[1024,1408]{1,0:T(8,128)(2,1)S(1)}) fusion(f32[1024,2816]{1,0:T(8,128)} %copy-done.25, bf16[1024,2048]{1,0:T(8,128)(2,1)} %constant_dynamic-update-slice_fusion.2, bf16[1408,2048]{1,0:T(8,128)(2,1)} %all-gather.14.cloned.1.call-done), kind=kOutput, calls=%fused_computation.14 | convolution fusion | flops 5924323328 | bytes 27262976 | tf_op jit(solution)/shard_map/dot_general | solution.py:85
  350.9 20.4 %convolution_convert_fusion = bf16[2048,2816]{1,0:T(8,128)(2,1)} fusion(bf16[1024,2048]{1,0:T(8,128)(2,1)} %constant_dynamic-update-slice_fusion.12, bf16[1024,1408]{1,0:T(8,128)(2,1)S(1)} %get-tuple-element.70, bf16[1024,1408]{1,0:T(8,128)(2,1)S(1)} %get-tuple-element.69), kind=kOutput, calls=%fused_computation | convolution fusion | flops 11828461568 | bytes 21495808 | tf_op jit(solution)/shard_map/dot_general | solution.py:89
  371.4 13.6 %fusion.11 = bf16[768,2048]{1,0:T(8,128)(2,1)S(1)} fusion(bf16[2048,2816]{1,0:T(8,128)(2,1)} %bitcast.205, bf16[1024,1408]{1,0:T(8,128)(2,1)} %copy-done.69, bf16[1024,1408]{1,0:T(8,128)(2,1)} %copy-done.67), kind=kOutput, calls=%fused_computation.25 | convolution fusion | flops 8868593664 | bytes 20447232 | tf_op jit(solution)/shard_map/dot_general | solution.py:85
  387.3 18.6 %collective-permute-done.22 = bf16[256,2048]{1,0:T(8,128)(2,1)S(1)} collective-permute-done((bf16[256,2048]{1,0:T(8,128)(2,1)S(1)}, bf16[256,2048]{1,0:T(8,128)(2,1)S(1)}, u32[]{:S(2)}, u32[]{:S(2)}) %collective-permute-start.22) | collective-permute-done | bytes 1048608 | tf_op jit(solution)/shard_map/ppermute | solution.py:97
  409.5 6.3 fusion.35
  427.4 20.5 %collective-permute-done.25 = bf16[256,2048]{1,0:T(8,128)(2,1)S(1)} collective-permute-done((bf16[256,2048]{1,0:T(8,128)(2,1)}, bf16[256,2048]{1,0:T(8,128)(2,1)S(1)}, u32[]{:S(2)}, u32[]{:S(2)}) %collective-permute-start.25) | collective-permute-done | bytes 1048608 | tf_op jit(solution)/shard_map/ppermute | solution.py:97
  450.1 7.1 %collective-permute-done.26 = bf16[128,2048]{1,0:T(8,128)(2,1)S(1)} collective-permute-done((bf16[128,2048]{1,0:T(8,128)(2,1)S(1)}, bf16[128,2048]{1,0:T(8,128)(2,1)S(1)}, u32[]{:S(2)}, u32[]{:S(2)}) %collective-permute-start.26) | collective-permute-done | bytes 524320 | tf_op jit(solution)/shard_map/ppermute | solution.py:97
  459.1 29.2 %shard_map.238 = (bf16[1024,1024]{1,0:T(8,128)(2,1)S(1)}, bf16[1024,1536]{1,0:T(8,128)(2,1)S(1)}) custom-call(bf16[1024,2048]{1,0:T(8,128)(2,1)S(1)} %constant_dynamic-update-slice_fusion.17.grad_ref, bf16[1024,2048]{1,0:T(8,128)(2,1)S(1)} %copy-done.10, bf16[1024,1024]{1,0:T(8,128)(2,1)S(1)} %bitcast.178, bf16[1024,1024]{1,0:T(8,128)(2,1)S(1)} %copy-done.14, ...), custom_call_target="tpu_custom_call" | custom-call | flops 9126805504 | bytes 16777216 | tf_op jit(solution)/shard_map/pallas_call | solution.py:258
  502.7 7.0 %collective-permute-done.32 = bf16[256,1536]{1,0:T(8,128)(2,1)S(1)} collective-permute-done((bf16[256,1536]{1,0:T(8,128)(2,1)S(1)}, bf16[256,1536]{1,0:T(8,128)(2,1)S(1)}, u32[]{:S(2)}, u32[]{:S(2)}) %collective-permute-start.32) | collective-permute-done | bytes 786464 | tf_op jit(solution)/shard_map/ppermute | solution.py:97
  513.8 18.7 %collective-permute-done.33 = bf16[128,1536]{1,0:T(8,128)(2,1)S(1)} collective-permute-done((bf16[128,1536]{1,0:T(8,128)(2,1)}, bf16[128,1536]{1,0:T(8,128)(2,1)S(1)}, u32[]{:S(2)}, u32[]{:S(2)}) %collective-permute-start.33) | collective-permute-done | bytes 393248 | tf_op jit(solution)/shard_map/ppermute | solution.py:97
  555.5 7.4 %fusion.39 = f32[256,2048]{1,0:T(8,128)S(1)} fusion(bf16[512,1536]{1,0:T(8,128)(2,1)} %slice.665, bf16[512,1536]{1,0:T(8,128)(2,1)} %slice.664, bf16[512,1536]{1,0:T(8,128)(2,1)} %slice.663, bf16[512,1536]{1,0:T(8,128)(2,1)} %slice.523, bf16[256,256]{1,0:T(8,128)(2,1)S(1)} %slice.867, bf16[256,128]{1,0:T(8,128)(2,1)S(1)} %get-tuple-element.118, ...), kind=kOutput, calls=%fused_computation.68 | convolution fusion | flops 1638924288 | bytes 9175040 | tf_op jit(solution)/shard_map/dot_general | solution.py:85
  585.5 8.4 %convolution_convert_fusion.3 = bf16[1024,2048]{1,0:T(8,128)(2,1)} fusion(bf16[1024,1024]{1,0:T(8,128)(2,1)S(1)} %copy-done.12, bf16[1024,2048]{1,0:T(8,128)(2,1)} %copy-done.9), kind=kOutput, calls=%fused_computation.22 | convolution fusion | flops 4297064448 | bytes 10485760 | tf_op jit(solution)/shard_map/dot_general | solution.py:89
  622.8 13.2 %collective-permute-done.37 = bf16[256,1664]{1,0:T(8,128)(2,1)} collective-permute-done((bf16[256,1664]{1,0:T(8,128)(2,1)}, bf16[256,1664]{1,0:T(8,128)(2,1)}, u32[]{:S(2)}, u32[]{:S(2)}) %collective-permute-start.37) | collective-permute-done | bytes 852000 | tf_op jit(solution)/shard_map/ppermute | solution.py:97
  640.1 8.6 %collective-permute-done.38 = bf16[128,1664]{1,0:T(8,128)(2,1)S(1)} collective-permute-done((bf16[128,1664]{1,0:T(8,128)(2,1)S(1)}, bf16[128,1664]{1,0:T(8,128)(2,1)S(1)}, u32[]{:S(2)}, u32[]{:S(2)}) %collective-permute-start.38) | collective-permute-done | bytes 426016 | tf_op jit(solution)/shard_map/ppermute | solution.py:97
  (435 shorter events, 300.4 us)
Async XLA Ops:
  7.2 44.0 %all-gather.6.cloned.1.call-start = ((), (), s32[]{:S(2)}) async-start(), calls=%async_computation.8 | async-start | bytes 1916928 | tf_op jit(solution)/shard_map/all_gather | solution.py:344
  10.4 190.8 %all-gather.8.cloned.1.call-start = ((), (), s32[]{:S(2)}) async-start(), calls=%async_computation.9 | async-start | bytes 2359296 | tf_op jit(solution)/shard_map/all_gather | solution.py:351
  22.3 201.4 %all-gather.10.cloned.1.call-start = ((), (), s32[]{:S(2)}) async-start(), calls=%async_computation.10 | async-start | bytes 4718592 | tf_op jit(solution)/shard_map/all_gather | solution.py:353
  51.2 252.3 %all-gather.12.cloned.1.call-start = ((), (), s32[]{:S(2)}) async-start(), calls=%async_computation.11 | async-start | bytes 12976128 | tf_op jit(solution)/shard_map/all_gather | solution.py:355
  51.8 284.4 %all-gather.14.cloned.1.call-start = ((), (), s32[]{:S(2)}) async-start(), calls=%async_computation.12 | async-start | bytes 6488064 | tf_op jit(solution)/shard_map/all_gather | solution.py:357
  58.4 26.3 %collective-permute-start.5 = (bf16[256,2048]{1,0:T(8,128)(2,1)}, bf16[256,2048]{1,0:T(8,128)(2,1)S(1)}, u32[]{:S(2)}, u32[]{:S(2)}) collective-permute-start(bf16[256,2048]{1,0:T(8,128)(2,1)} %get-tuple-element.68), channel_id=1, source_target_pairs={{0,16},{16,0},{1,17},{17,1},{2,18},{18,2},{3,19},{19,3},{4,20},{20... | collective-permute-start | bytes 3145736 | tf_op jit(solution)/shard_map/ppermute | solution.py:97
  59.3 28.2 %collective-permute-start.4 = (bf16[256,2048]{1,0:T(8,128)(2,1)}, bf16[256,2048]{1,0:T(8,128)(2,1)}, u32[]{:S(2)}, u32[]{:S(2)}) collective-permute-start(bf16[256,2048]{1,0:T(8,128)(2,1)} %get-tuple-element.68), channel_id=1, source_target_pairs={{0,8},{8,0},{1,9},{9,1},{2,10},{10,2},{3,11},{11,3},{4,12},{12,4},... | collective-permute-start | bytes 3145736 | tf_op jit(solution)/shard_map/ppermute | solution.py:97
  59.9 70.6 %collective-permute-start.1 = (bf16[512,1664]{1,0:T(8,128)(2,1)}, bf16[512,1664]{1,0:T(8,128)(2,1)S(1)}, u32[]{:S(2)}, u32[]{:S(2)}) collective-permute-start(bf16[512,1664]{1,0:T(8,128)(2,1)} %all-gather.6.cloned.1.call-done), channel_id=1, source_target_pairs={{0,16},{16,0},{1,17},{17,1},{2,18},{18,2},{3,19},{19,3},{4,20},{20... | collective-permute-start | bytes 5111816 | tf_op jit(solution)/shard_map/ppermute | solution.py:97
  63.3 71.4 %collective-permute-start = (bf16[512,1664]{1,0:T(8,128)(2,1)}, bf16[512,1664]{1,0:T(8,128)(2,1)}, u32[]{:S(2)}, u32[]{:S(2)}) collective-permute-start(bf16[512,1664]{1,0:T(8,128)(2,1)} %all-gather.6.cloned.1.call-done), channel_id=1, source_target_pairs={{0,8},{8,0},{1,9},{9,1},{2,10},{10,2},{3,11},{11,3},{4,12},{12,4},... | collective-permute-start | bytes 5111816 | tf_op jit(solution)/shard_map/ppermute | solution.py:97
  86.5 43.1 %collective-permute-start.6 = (bf16[128,2048]{1,0:T(8,128)(2,1)}, bf16[128,2048]{1,0:T(8,128)(2,1)S(1)}, u32[]{:S(2)}, u32[]{:S(2)}) collective-permute-start(bf16[128,2048]{1,0:T(8,128)(2,1)} %slice.672), channel_id=1, source_target_pairs={{0,8},{8,0},{1,9},{9,1},{2,10},{10,2},{3,11},{11,3},{4,12},{12,4},... | collective-permute-start | bytes 1572872 | tf_op jit(solution)/shard_map/ppermute | solution.py:97
  88.7 42.5 %collective-permute-start.7 = (bf16[128,2048]{1,0:T(8,128)(2,1)S(1)}, bf16[128,2048]{1,0:T(8,128)(2,1)S(1)}, u32[]{:S(2)}, u32[]{:S(2)}) collective-permute-start(bf16[128,2048]{1,0:T(8,128)(2,1)S(1)} %slice.673), channel_id=1, source_target_pairs={{0,16},{16,0},{1,17},{17,1},{2,18},{18,2},{3,19},{19,3},{4,20},{20... | collective-permute-start | bytes 1572872 | tf_op jit(solution)/shard_map/ppermute | solution.py:97
  165.0 27.4 %collective-permute-start.8 = (bf16[256,1536]{1,0:T(8,128)(2,1)}, bf16[256,1536]{1,0:T(8,128)(2,1)}, u32[]{:S(2)}, u32[]{:S(2)}) collective-permute-start(bf16[256,1536]{1,0:T(8,128)(2,1)} %pad_maximum_fusion.15), channel_id=1, source_target_pairs={{0,8},{8,0},{1,9},{9,1},{2,10},{10,2},{3,11},{11,3},{4,12},{12,4},... | collective-permute-start | bytes 2359304 | tf_op jit(solution)/shard_map/ppermute | solution.py:97
  166.7 23.6 %collective-permute-start.9 = (bf16[256,1536]{1,0:T(8,128)(2,1)}, bf16[256,1536]{1,0:T(8,128)(2,1)}, u32[]{:S(2)}, u32[]{:S(2)}) collective-permute-start(bf16[256,1536]{1,0:T(8,128)(2,1)} %pad_maximum_fusion.15), channel_id=1, source_target_pairs={{0,16},{16,0},{1,17},{17,1},{2,18},{18,2},{3,19},{19,3},{4,20},{20... | collective-permute-start | bytes 2359304 | tf_op jit(solution)/shard_map/ppermute | solution.py:97
  256.1 171.2 %reduce-scatter.5.cloned.1.call-start = ((), (), s32[]{:S(2)}) async-start(), calls=%async_computation.13 | async-start | bytes 6488064 | tf_op jit(solution)/shard_map/reduce_scatter | solution.py:409
  336.1 208.3 %reduce-scatter.7.cloned.1.call-start = ((), (), s32[]{:S(2)}) async-start(), calls=%async_computation.14 | async-start | bytes 12976128 | tf_op jit(solution)/shard_map/reduce_scatter | solution.py:425
  371.4 248.1 %reduce-scatter.9.cloned.1.call-start = ((), (), s32[]{:S(2)}) async-start(), calls=%async_computation.15 | async-start | bytes 2359296 | tf_op jit(solution)/shard_map/reduce_scatter | solution.py:443
  489.4 24.4 %collective-permute-start.34 = (bf16[256,1536]{1,0:T(8,128)(2,1)}, bf16[256,1536]{1,0:T(8,128)(2,1)}, u32[]{:S(2)}, u32[]{:S(2)}) collective-permute-start(bf16[256,1536]{1,0:T(8,128)(2,1)} %pad_maximum_fusion.17), channel_id=1, source_target_pairs={{0,16},{16,0},{1,17},{17,1},{2,18},{18,2},{3,19},{19,3},{4,20},{20... | collective-permute-start | bytes 2359304 | tf_op jit(solution)/shard_map/ppermute | solution.py:97
  499.8 34.4 %collective-permute-start.30 = (bf16[256,2048]{1,0:T(8,128)(2,1)}, bf16[256,2048]{1,0:T(8,128)(2,1)}, u32[]{:S(2)}, u32[]{:S(2)}) collective-permute-start(bf16[256,2048]{1,0:T(8,128)(2,1)} %pad_maximum_fusion.11), channel_id=1, source_target_pairs={{0,16},{16,0},{1,17},{17,1},{2,18},{18,2},{3,19},{19,3},{4,20},{20... | collective-permute-start | bytes 3145736 | tf_op jit(solution)/shard_map/ppermute | solution.py:97
  501.9 32.2 %collective-permute-start.28 = (bf16[256,2048]{1,0:T(8,128)(2,1)}, bf16[256,2048]{1,0:T(8,128)(2,1)}, u32[]{:S(2)}, u32[]{:S(2)}) collective-permute-start(bf16[256,2048]{1,0:T(8,128)(2,1)} %pad_maximum_fusion.10), channel_id=1, source_target_pairs={{0,8},{8,0},{1,9},{9,1},{2,10},{10,2},{3,11},{11,3},{4,12},{12,4},... | collective-permute-start | bytes 3145736 | tf_op jit(solution)/shard_map/ppermute | solution.py:97
  537.1 40.6 %collective-permute-start.29 = (bf16[128,2048]{1,0:T(8,128)(2,1)}, bf16[128,2048]{1,0:T(8,128)(2,1)}, u32[]{:S(2)}, u32[]{:S(2)}) collective-permute-start(bf16[128,2048]{1,0:T(8,128)(2,1)} %get-tuple-element.87), channel_id=1, source_target_pairs={{0,16},{16,0},{1,17},{17,1},{2,18},{18,2},{3,19},{19,3},{4,20},{20... | collective-permute-start | bytes 1572872 | tf_op jit(solution)/shard_map/ppermute | solution.py:97
  538.4 39.3 %collective-permute-start.31 = (bf16[128,2048]{1,0:T(8,128)(2,1)}, bf16[128,2048]{1,0:T(8,128)(2,1)}, u32[]{:S(2)}, u32[]{:S(2)}) collective-permute-start(bf16[128,2048]{1,0:T(8,128)(2,1)} %get-tuple-element.88), channel_id=1, source_target_pairs={{0,8},{8,0},{1,9},{9,1},{2,10},{10,2},{3,11},{11,3},{4,12},{12,4},... | collective-permute-start | bytes 1572872 | tf_op jit(solution)/shard_map/ppermute | solution.py:97
  574.6 34.8 %collective-permute-start.36 = (bf16[1024,1664]{1,0:T(8,128)(2,1)}, bf16[1024,1664]{1,0:T(8,128)(2,1)}, u32[]{:S(2)}, u32[]{:S(2)}) collective-permute-start(bf16[1024,1664]{1,0:T(8,128)(2,1)} %bitcast.42), channel_id=1, source_target_pairs={{0,1},{1,0},{2,3},{3,2},{4,5},{5,4},{6,7},{7,6},{8,9},{9,8},{10,11... | collective-permute-start | bytes 10223624 | tf_op jit(solution)/shard_map/ppermute | solution.py:97
  585.5 89.1 %reduce-scatter.11.cloned.1.call-start = ((), (), s32[]{:S(2)}) async-start(), calls=%async_computation.16 | async-start | bytes 4718592 | tf_op jit(solution)/shard_map/reduce_scatter | solution.py:440
  619.4 41.6 %all-to-all-start.2 = ((bf16[4,32,1024]{2,1,0:T(8,128)(2,1)}), bf16[4,32,1024]{2,1,0:T(8,128)(2,1)S(1)}, u32[]{:S(2)}, u32[]{:S(2)}) async-start(bf16[4,32,1024]{2,1,0:T(8,128)(2,1)} %reduce-scatter.9.cloned.1.call-done), calls=%async_computation.5 | async-start | bytes 524288 | tf_op jit(solution)/shard_map/all_to_all | solution.py:304
  (106 other events, 1335.8 us)
Sparse Core Ops, SparseCore 0:
  10.6 28.5 all-gather.5
  40.8 28.6 all-gather.7
  71.0 46.6 all-gather.9
  119.2 106.7 all-gather.11
  256.2 60.8 all-gather.13
  336.2 64.7 reduce-scatter.4
  403.4 117.6 reduce-scatter.6
  555.6 35.9 reduce-scatter.8
  594.0 51.4 reduce-scatter.10

commit v3 on v2

v3 whole, which is shorter than its diff:
```python
import functools
import math

import jax
import jax.numpy as jnp
from jax import lax
from jax.experimental import pallas as pl
from jax.experimental.pallas import tpu as pltpu
from jax.sharding import PartitionSpec as P

H = 16
HD = 256
PAD = 32

eps = 1e-06
rope_base = 10000.0
masked_score = -1e30
ALL = ("y", "x", "zh", "zl", "r")
DP = ("y", "x")
GROUP = ("x", "y")
RING = ("zh", "zl", "r")
f32 = jnp.float32
bf16 = jnp.bfloat16


def layout(lengths, row_total):
    padded = (lengths + PAD - 1) // PAD * PAD
    count = lengths.shape[0]
    ends = []
    for s in range(count):
        ends.append(padded[s] if s == 0 else ends[-1] + padded[s])
    row = lax.broadcasted_iota(jnp.int32, (row_total, 1), 0)
    segment = jnp.zeros_like(row)
    start = jnp.zeros_like(row)
    alive = jnp.zeros(row.shape, jnp.bool_)
    for s in range(count):
        first = ends[s] - padded[s]
        member = (row >= first) & (row < ends[s])
        segment = jnp.where(member, s + 1, segment)
        start = jnp.where(member, first, start)
        alive = alive | (member & (row - first < lengths[s]))
    return row - start, alive, segment


def angles(offset, head_size):
    half_width = head_size // 2
    frequency = jnp.exp(
        jnp.arange(half_width, dtype=f32) * (-2.0 * math.log(rope_base) / head_size)
    )
    phase = offset.astype(f32) * frequency[None, :]
    return (jnp.cos(phase), jnp.sin(phase))


def rotate(values, cos_part, sin_part):
    half_width = values.shape[-1] // 2
    first_half = values[..., :half_width]
    second_half = values[..., half_width:]
    return jnp.concatenate(
        [
            first_half * cos_part - second_half * sin_part,
            second_half * cos_part + first_half * sin_part,
        ],
        axis=-1,
    )


def normalize(values, scale_gain):
    factor = lax.rsqrt(jnp.mean(values * values, axis=-1, keepdims=True) + eps)
    normed = values * factor
    return (normed * scale_gain, normed, factor)


def normalize_back(upstream, normed, factor, scale_gain):
    scaled = upstream * scale_gain
    gain_grad = jnp.sum(upstream * normed, axis=0)
    inner_mean = jnp.mean(scaled * normed, axis=-1, keepdims=True)
    return (factor * (scaled - normed * inner_mean), gain_grad)


def dot(a, b):
    return jnp.dot(a, b, preferred_element_type=f32)


def dot_nt(a, b):
    return lax.dot_general(a, b, (((1,), (1,)), ((), ())), preferred_element_type=f32)


def dot_tn(a, b):
    return lax.dot_general(a, b, (((0,), (0,)), ((), ())), preferred_element_type=f32)


def after(values, *others):
    return lax.optimization_barrier((values, others))[0]


def trade(values, axis):
    return lax.ppermute(values, axis, [(0, 1), (1, 0)])


def gather_quad(values, first, second):
    half = values.shape[0] // 2
    one = trade(values, first)
    two = trade(values, second)
    three = jnp.concatenate([trade(two[:half], first), trade(one[half:], second)], axis=0)
    return [values, one, two, three]


def fetch_first(values, first, second):
    return trade(values, first), trade(values, second)


def fetch_last(values, found, first, second):
    one, two = found
    half = values.shape[0] // 2
    return [values, one, two, trade(two[:half], first), trade(one[half:], second)]


def first_loads(slots):
    half = slots[1].shape[0] // 2
    return (
        jnp.concatenate([slots[1][:half], slots[3][:half]], axis=0),
        jnp.concatenate([slots[2][half:], slots[3][half:]], axis=0),
    )


def send_loads(loads, first, second):
    return trade(loads[0], first), trade(loads[1], second)


def last_loads(slots, sent):
    half, (ra, rb) = slots[1].shape[0] // 2, sent
    return (
        (slots[2][:half].astype(f32) + ra[half:].astype(f32)).astype(bf16),
        (slots[1][half:].astype(f32) + rb[half:].astype(f32)).astype(bf16),
    )


def sum_up(own, sent, last):
    half, own = own.shape[0] // 2, own.astype(f32)
    return jnp.concatenate(
        [
            own[:half] + sent[0][:half].astype(f32) + last[0].astype(f32),
            own[half:] + sent[1][:half].astype(f32) + last[1].astype(f32),
        ],
        axis=0,
    )


def send_first(slots, first, second):
    return send_loads(first_loads(slots), first, second)


def send_last(slots, sent, first, second):
    return sum_up(slots[0], sent, send_loads(last_loads(slots, sent), second, first))


def scatter_quad(slots, first, second):
    return send_last(slots, send_first(slots, first, second), first, second)


def scatter_rows(own, others, first, second):
    rows = own.shape[0]
    slots = [own] + [others[i * rows : (i + 1) * rows] for i in range(3)]
    return scatter_quad(slots, first, second)


def split_cores(values, cores):
    if cores != 2:
        return lax.psum_scatter(values, "r", scatter_dimension=4, tiled=False), None
    core = lax.axis_index("r")
    mine = lax.dynamic_index_in_dim(values, core, 4, keepdims=False)
    theirs = lax.dynamic_index_in_dim(values, 1 - core, 4, keepdims=False)
    return mine, trade(theirs.reshape(-1, values.shape[-1]), "r").reshape(mine.shape)


def join_cores(mine, theirs):
    if theirs is None:
        return mine
    return (mine.astype(f32) + theirs.astype(f32)).astype(bf16)


def small_first(values, cores):
    n, c = values.shape[5:]
    total = join_cores(*split_cores(values, cores)).reshape(4, 4 * n, c)
    me = lax.axis_index(DP)
    return [lax.dynamic_index_in_dim(total, me ^ code, 0, keepdims=False) for code in range(4)]


def small_middle(slots):
    total = scatter_quad(slots, *GROUP).astype(bf16)
    total = total.reshape(4, -1, total.shape[1])
    me = lax.axis_index("zh") * 2 + lax.axis_index("zl")
    return [lax.dynamic_index_in_dim(total, me ^ code, 0, keepdims=False) for code in range(4)]


def swap_blocks(block):
    me = lax.axis_index(DP)
    found = [block(me)]
    for code in (1, 2, 3):
        found.append(lax.ppermute(block(me ^ code), DP, [(i, i ^ code) for i in range(4)]))
    return found


def in_order(found):
    me, found = lax.axis_index(DP), jnp.stack(found)
    return [lax.dynamic_index_in_dim(found, me ^ k, 0, keepdims=False) for k in range(4)]


def take_columns(weight, k, members):
    step = weight.shape[1] // members
    return lax.dynamic_slice_in_dim(weight, k * step, step, 1)


def turn(values, cos_part, sin_part):
    half = values.shape[-1] // 2
    one, two = values[:, :half], values[:, half:]
    return jnp.concatenate([one * cos_part - two * sin_part, two * cos_part + one * sin_part], axis=-1)


def spans(lengths_ref, member):
    first, found = 0, []
    for s in range(lengths_ref.shape[1]):
        length = lengths_ref[member, s]
        end = first + (length + PAD - 1) // PAD * PAD
        found.append((first, end, first + length))
        first = end
    return found


def fill_angles(lengths_ref, cos_ref, sin_ref):
    rows, half = cos_ref.shape
    row = lax.broadcasted_iota(jnp.int32, (rows, half), 0)
    position = row
    for first, end, _ in spans(lengths_ref, pl.program_id(0)):
        position = jnp.where((row >= first) & (row < end), row - first, position)
    step = lax.broadcasted_iota(jnp.int32, (rows, half), 1).astype(f32)
    phase = position.astype(f32) * jnp.exp(step * (-math.log(rope_base) / half))
    cos_ref[...] = jnp.cos(phase)
    sin_ref[...] = jnp.sin(phase)


def probabilities(query_rot, key_rot, lengths_ref):
    rows = query_rot.shape[0]
    scores = dot_nt(query_rot, key_rot) * (1.0 / math.sqrt(HD))
    i = lax.broadcasted_iota(jnp.int32, (rows, rows), 0)
    j = lax.broadcasted_iota(jnp.int32, (rows, rows), 1)
    allowed = i == j
    for first, end, live in spans(lengths_ref, pl.program_id(0)):
        allowed = allowed | ((i >= first) & (i < end) & (j >= first) & (j < live) & (j <= i))
    scores = jnp.where(allowed, scores, masked_score)
    expo = jnp.exp(scores - jnp.max(scores, axis=-1, keepdims=True))
    return expo / jnp.sum(expo, axis=-1, keepdims=True)


def attend_kernel(
    lengths_ref, latent_ref, weight_ref, key_ref, value_ref, query_ref, mix_ref, cos_ref, sin_ref
):
    @pl.when(pl.program_id(1) == 0)
    def _():
        fill_angles(lengths_ref, cos_ref, sin_ref)

    query_rot = turn(dot(latent_ref[...], weight_ref[...]), cos_ref[...], sin_ref[...]).astype(bf16)
    query_ref[...] = query_rot
    probs = probabilities(query_rot, key_ref[...], lengths_ref)
    mix_ref[...] = dot(probs.astype(bf16), value_ref[...]).astype(bf16)


def attend(lengths, packed, query_full, rows, heads):
    total, latent_width = packed.shape[0], query_full.shape[0]
    last = latent_width // HD
    block = pl.BlockSpec((rows, HD), lambda m, h, s: (m, h))
    out = jax.ShapeDtypeStruct((total, heads * HD), bf16)
    return pl.pallas_call(
        attend_kernel,
        grid_spec=pltpu.PrefetchScalarGridSpec(
            num_scalar_prefetch=1,
            grid=(total // rows, heads),
            in_specs=[
                pl.BlockSpec((rows, latent_width), lambda m, h, s: (m, 0)),
                pl.BlockSpec((latent_width, HD), lambda m, h, s: (0, h)),
                pl.BlockSpec((rows, HD), lambda m, h, s: (m, last)),
                pl.BlockSpec((rows, HD), lambda m, h, s: (m, last + 1)),
            ],
            out_specs=[block, block],
            scratch_shapes=[pltpu.VMEM((rows, HD // 2), f32), pltpu.VMEM((rows, HD // 2), f32)],
        ),
        out_shape=[out, out],
        compiler_params=pltpu.CompilerParams(vmem_limit_bytes=32 * 2**20),
        cost_estimate=pl.CostEstimate(
            flops=2 * total * heads * HD * (latent_width + 2 * rows),
            bytes_accessed=total * heads * HD * 4 + total * latent_width * 3,
            transcendentals=total * heads * rows,
        ),
    )(lengths, packed, query_full, packed, packed)


def attend_back_kernel(
    members,
    heads,
    lengths_ref,
    grad_ref,
    out_ref,
    weight_ref,
    query_ref,
    latent_ref,
    key_ref,
    value_ref,
    mix_ref,
    packed_ref,
    out_grad_ref,
    weight_grad_ref,
    total_ref,
    out_total_ref,
    weight_total_ref,
    cos_ref,
    sin_ref,
):
    member, head = pl.program_id(0), pl.program_id(1)

    @pl.when(head == 0)
    def _():
        fill_angles(lengths_ref, cos_ref, sin_ref)
        total_ref[...] = jnp.zeros_like(total_ref)

    @pl.when(member == 0)
    def _():
        out_total_ref[head] = jnp.zeros_like(out_total_ref.at[0])
        weight_total_ref[head] = jnp.zeros_like(weight_total_ref.at[0])

    latent_width = weight_ref.shape[0]
    scale = 1.0 / math.sqrt(HD)
    query_rot, key_rot, value_low = query_ref[...], key_ref[...], value_ref[...]
    mixture_grad = dot_nt(grad_ref[...], out_ref[...]).astype(bf16)
    out_total_ref[head] += dot_tn(mix_ref[...], grad_ref[...])
    probs = probabilities(query_rot, key_rot, lengths_ref)
    probs_grad = dot_nt(mixture_grad, value_low)
    row_dot = jnp.sum(probs * probs_grad, axis=-1, keepdims=True)
    score_grad = (probs * (probs_grad - row_dot)).astype(bf16)
    query_rot_grad = dot(score_grad, key_rot) * scale
    query_grad = turn(query_rot_grad, cos_ref[...], -sin_ref[...]).astype(bf16)
    weight_total_ref[head] += dot_tn(latent_ref[...], query_grad)
    total_ref[:, :latent_width] += dot_nt(query_grad, weight_ref[...])
    total_ref[:, latent_width : latent_width + HD] += dot_tn(score_grad, query_rot) * scale
    total_ref[:, latent_width + HD :] += dot_tn(probs.astype(bf16), mixture_grad)

    @pl.when(head == heads - 1)
    def _():
        packed_ref[...] = total_ref[...].astype(bf16)

    @pl.when(member == members - 1)
    def _():
        out_grad_ref[...] = out_total_ref[head].astype(bf16)
        weight_grad_ref[...] = weight_total_ref[head].astype(bf16)


def attend_back(lengths, attn_grad, out_full, query_full, query_rot, mixture, packed, rows, heads):
    total, width = attn_grad.shape
    latent_width = query_full.shape[0]
    last, members = latent_width // HD, total // rows
    block = pl.BlockSpec((rows, HD), lambda m, h, s: (m, h))

    def when_last(m, h):
        return jnp.where(m == members - 1, h, 0)

    return pl.pallas_call(
        functools.partial(attend_back_kernel, members, heads),
        grid_spec=pltpu.PrefetchScalarGridSpec(
            num_scalar_prefetch=1,
            grid=(members, heads),
            in_specs=[
                pl.BlockSpec((rows, width), lambda m, h, s: (m, 0)),
                pl.BlockSpec((HD, width), lambda m, h, s: (h, 0)),
                pl.BlockSpec((latent_width, HD), lambda m, h, s: (0, h)),
                block,
                pl.BlockSpec((rows, latent_width), lambda m, h, s: (m, 0)),
                pl.BlockSpec((rows, HD), lambda m, h, s: (m, last)),
                pl.BlockSpec((rows, HD), lambda m, h, s: (m, last + 1)),
                block,
            ],
            out_specs=[
                pl.BlockSpec((rows, packed.shape[1]), lambda m, h, s: (m, 0)),
                pl.BlockSpec((HD, width), lambda m, h, s: (when_last(m, h), 0)),
                pl.BlockSpec((latent_width, HD), lambda m, h, s: (0, when_last(m, h))),
            ],
            scratch_shapes=[
                pltpu.VMEM((rows, packed.shape[1]), f32),
                pltpu.VMEM((heads, HD, width), f32),
                pltpu.VMEM((heads, latent_width, HD), f32),
                pltpu.VMEM((rows, HD // 2), f32),
                pltpu.VMEM((rows, HD // 2), f32),
            ],
        ),
        out_shape=[
            jax.ShapeDtypeStruct(packed.shape, bf16),
            jax.ShapeDtypeStruct((heads * HD, width), bf16),
            jax.ShapeDtypeStruct((latent_width, heads * HD), bf16),
        ],
        compiler_params=pltpu.CompilerParams(vmem_limit_bytes=48 * 2**20),
        cost_estimate=pl.CostEstimate(
            flops=2 * total * heads * HD * (2 * width + 2 * latent_width + 5 * rows),
            bytes_accessed=total * heads * HD * 8 + total * width * 4,
            transcendentals=total * heads * rows,
        ),
    )(lengths, attn_grad, out_full, query_full, query_rot, packed, packed, packed, mixture)


def by_member(values, members):
    me = lax.axis_index(DP)
    step = values.shape[1] // members
    return jnp.concatenate(
        [lax.dynamic_slice_in_dim(values, (me ^ slot) * step, step, 1) for slot in range(members)], axis=1
    )


def shards(
    members,
    ring,
    cores,
    tokens,
    lengths,
    attn_gain,
    query_down,
    query_gain,
    query_up,
    key_weight,
    value_weight,
    out_weight,
    mlp_gain,
    gate_weight,
    up_weight,
    down_weight,
    cotangent,
):
    rows = tokens.shape[0]
    width = tokens.shape[1]
    latent_width = query_down.shape[1]
    heads = H // members
    devices = members * ring
    score_scale = 1.0 / math.sqrt(HD)
    d_rows = query_down.shape[0]

    def column(v):
        v = v.astype(bf16).reshape(-1, 1)
        return jnp.pad(v, ((0, d_rows - v.shape[0]), (0, 0)))

    own_offset, own_alive, _ = layout(lengths[0], rows)
    living = own_alive.astype(f32)
    own_cos, own_sin = angles(own_offset, HD)
    grad_rows = cotangent.astype(f32)
    ffn_grad_own = (living * grad_rows).astype(bf16)

    extra = jnp.concatenate(
        [column(attn_gain), column(mlp_gain), column(query_gain), column(lengths[0])], axis=1
    )
    extra = jnp.pad(extra, ((0, 0), (0, 128 - extra.shape[1])))
    small = jnp.concatenate([query_down, key_weight, value_weight, extra], axis=1)
    small = lax.all_gather(small, RING, axis=0, tiled=True)
    query_own = jnp.stack(in_order(swap_blocks(lambda k: take_columns(query_up, k, members))))
    gate_up_own = swap_blocks(
        lambda k: jnp.concatenate(
            [take_columns(gate_weight, k, members), take_columns(up_weight, k, members)], axis=1
        )
    )
    gate_up_own = jnp.stack(in_order(gate_up_own))
    query_own = after(query_own, gate_up_own)
    small_parts = gather_quad(after(small, query_own), *GROUP)
    query_full = lax.all_gather(query_own, RING, axis=1, tiled=True)
    query_full = query_full.reshape(latent_width, heads * HD)
    out_full = lax.all_gather(after(out_weight, small), RING, axis=0, tiled=True)
    gate_up = lax.all_gather(after(gate_up_own, small), RING, axis=1, tiled=True).reshape(width, -1)
    cut = gate_up.shape[1] // 2
    down_full = lax.all_gather(after(down_weight, small), RING, axis=0, tiled=True)

    me, lane = lax.axis_index(DP), lax.axis_index(RING)
    qkv_width = latent_width + 2 * HD
    qkv_parts = jnp.concatenate(small_parts, axis=0)
    extra = jnp.stack([part[:, qkv_width:] for part in small_parts])
    group_lengths = lax.dynamic_slice(
        extra, (0, lane * d_rows, 3), (members, lengths.shape[1], 1)
    ).reshape(members, -1).astype(jnp.int32)
    extra = [lax.dynamic_index_in_dim(extra, me ^ slot, 0, keepdims=False) for slot in range(members)]
    extra = jnp.concatenate(extra, axis=0).astype(f32).T
    attn_scale = extra[0:1]
    mlp_scale = extra[1:2]
    latent_scale = extra[2].reshape(devices, d_rows)[:, : query_gain.shape[0]].reshape(1, -1)

    token_rows = tokens.astype(f32)
    attn_out, attn_normed, attn_factor = normalize(token_rows, attn_scale)
    attn_in = attn_out.astype(bf16)
    low = dot(by_member(attn_in, members), qkv_parts)
    latent = low[:, :latent_width]
    latent_out, latent_normed, latent_factor = normalize(latent, latent_scale)
    latent_in = latent_out.astype(bf16)
    key_own = rotate(low[:, latent_width : latent_width + HD], own_cos, own_sin)
    value_own = low[:, latent_width + HD : qkv_width]
    packed = jnp.concatenate([latent_in, key_own.astype(bf16), value_own.astype(bf16)], axis=1)
    packed = jnp.concatenate(gather_quad(packed, *GROUP), axis=0)
    query_rot, mixture = attend(group_lengths, packed, query_full, rows, heads)
    ffn_grad_found = fetch_first(after(ffn_grad_own, packed), *GROUP)
    ffn_grad = fetch_last(ffn_grad_own, after(ffn_grad_found, mixture), *GROUP)
    mixture = after(mixture, ffn_grad_found)
    attn_sum = scatter_rows(
        dot(mixture[:rows], out_full), dot(mixture[rows:], out_full).astype(bf16), *GROUP
    )
    residual = token_rows + living * attn_sum

    ffn_out, ffn_normed, ffn_factor = normalize(residual, mlp_scale)
    ffn_in = jnp.concatenate(gather_quad(ffn_out.astype(bf16), *GROUP), axis=0)
    gate_up_act = dot(ffn_in, gate_up)
    ffn_grad = jnp.concatenate(after(ffn_grad, gate_up_act), axis=0)
    gate_act, up_act = gate_up_act[:, :cut], gate_up_act[:, cut:]
    sigmoid_gate = jax.nn.sigmoid(gate_act)
    silu_gate = gate_act * sigmoid_gate
    hidden = (silu_gate * up_act).astype(bf16)

    down_wgrad = dot_tn(hidden, ffn_grad).astype(bf16)
    down_share = lax.psum_scatter(down_wgrad, RING, scatter_dimension=0, tiled=True)

    hidden_grad = dot_nt(after(ffn_grad, down_wgrad), down_full)
    gate_grad = (
        hidden_grad * up_act * sigmoid_gate * (1.0 + gate_act * (1.0 - sigmoid_gate))
    ).astype(bf16)
    up_grad = (hidden_grad * silu_gate).astype(bf16)
    gate_up_grad = jnp.concatenate([gate_grad, up_grad], axis=1)
    back = dot_nt(gate_up_grad[rows:], gate_up).astype(bf16)
    slots = [None] + [back[i * rows : (i + 1) * rows] for i in range(members - 1)]
    loads = first_loads(slots)
    back_sent = send_loads(loads, *GROUP)
    back_own = dot_nt(after(gate_up_grad[:rows], loads), gate_up)
    loads = last_loads(slots, after(back_sent, back_own))
    ffn_in_grad = sum_up(back_own, back_sent, send_loads(loads, *GROUP[::-1]))
    gate_up_wgrad = dot_tn(ffn_in, after(gate_up_grad, loads)).astype(bf16)
    residual_back, mlp_scale_grad = normalize_back(ffn_in_grad, ffn_normed, ffn_factor, mlp_scale)
    residual_grad = grad_rows + residual_back
    attn_grad = (living * residual_grad).astype(bf16)
    attn_grad = after(attn_grad, down_share, gate_up_wgrad)
    gate_up_share = lax.psum_scatter(
        gate_up_wgrad.reshape(members, width // members, -1), RING, scatter_dimension=1, tiled=True
    )
    attn_found = fetch_first(attn_grad, *GROUP)
    attn_grad = jnp.concatenate(fetch_last(attn_grad, attn_found, *GROUP), axis=0)
    ffn_back = dot(after(hidden, attn_found), down_full).astype(bf16)
    ffn_slots = after(ffn_back, attn_grad)
    ffn_slots = [ffn_slots[i * rows : (i + 1) * rows] for i in range(members)]
    ffn_sent = send_first(ffn_slots, *GROUP)
    packed_grad, out_wgrad, query_wgrad = attend_back(
        group_lengths,
        after(attn_grad, ffn_back),
        out_full,
        query_full,
        query_rot,
        mixture,
        packed,
        rows,
        heads,
    )
    packed_grad = after(packed_grad, ffn_sent)
    slots = [packed_grad[i * rows : (i + 1) * rows] for i in range(members)]
    loads = first_loads(slots)
    packed_sent = send_loads(loads, *GROUP)
    out_share = lax.psum_scatter(out_wgrad, RING, scatter_dimension=0, tiled=True)
    loads = last_loads(slots, packed_sent)
    packed_grad = sum_up(slots[0], packed_sent, send_loads(loads, *GROUP[::-1]))
    packed_grad = after(packed_grad, gate_up_share)
    ffn_sum = send_last(ffn_slots, after(ffn_sent, packed_grad), *GROUP)
    gate_up_found = swap_blocks(
        lambda k: lax.dynamic_index_in_dim(
            after(gate_up_share, packed_grad).reshape(members, d_rows, -1), k, 0, keepdims=False
        )
    )
    query_wgrad = query_wgrad.reshape(members, latent_width // members, heads * HD)
    query_share = lax.psum_scatter(query_wgrad, RING, scatter_dimension=1, tiled=True)
    latent_in_grad = packed_grad[:, :latent_width]
    key_grad = rotate(
        packed_grad[:, latent_width : latent_width + HD], own_cos, -own_sin
    ).astype(bf16)
    value_grad = packed_grad[:, latent_width + HD :].astype(bf16)
    latent_back, latent_scale_grad = normalize_back(
        latent_in_grad, latent_normed, latent_factor, latent_scale
    )
    spare = jnp.zeros((rows, qkv_parts.shape[1] - qkv_width), bf16)
    qkv_grad = jnp.concatenate([latent_back.astype(bf16), key_grad, value_grad, spare], axis=1)
    attn_in_grad = by_member(dot_nt(qkv_grad, qkv_parts), members)
    token_back, attn_scale_grad = normalize_back(attn_in_grad, attn_normed, attn_factor, attn_scale)

    small_grad = dot_tn(attn_in, qkv_grad[:, :qkv_width])
    latent_column = jnp.pad(
        latent_scale_grad.reshape(devices, -1), ((0, 0), (0, d_rows - query_gain.shape[0]))
    ).reshape(-1)
    columns = jnp.stack([attn_scale_grad, mlp_scale_grad, latent_column])
    columns = jnp.pad(columns, ((0, 128 - 3), (0, 0))).T
    small_grad = jnp.concatenate([small_grad, columns], axis=1).astype(bf16)
    small_slots = small_first(small_grad.reshape(2, 2, 2, 2, cores, d_rows, -1), cores)
    small_pairs = small_middle(small_slots)
    small_share = scatter_quad(small_pairs, "zl", "zh")
    out_share, down_share, query_share = after((out_share, down_share, query_share), small_pairs)

    layer_out = (residual + living * after(ffn_sum, small_slots)).astype(bf16)
    tokens_grad = after(residual_grad, small_slots) + token_back
    found = in_order(after(gate_up_found, small_slots))
    gate_share = jnp.concatenate([part[:, :cut] for part in found], axis=1).astype(f32)
    up_share = jnp.concatenate([part[:, cut:] for part in found], axis=1).astype(f32)
    found = in_order(swap_blocks(lambda k: lax.dynamic_index_in_dim(query_share, k, 0, keepdims=False)))
    query_share = jnp.concatenate(found, axis=1).astype(f32)
    return (
        layer_out,
        tokens_grad,
        small_share[:, latent_width + 2 * HD],
        small_share[:, :latent_width],
        small_share[: query_gain.shape[0], latent_width + 2 * HD + 2],
        query_share,
        small_share[:, latent_width : latent_width + HD],
        small_share[:, latent_width + HD : latent_width + 2 * HD],
        out_share.astype(f32),
        small_share[:, latent_width + 2 * HD + 1],
        gate_share,
        up_share,
        down_share.astype(f32),
    )


def solution(mesh):
    members, ring = mesh.shape["dp"], mesh.shape["fsdp"]
    cores = mesh.devices.size // 16
    fine = jax.sharding.Mesh(mesh.devices.reshape(2, 2, 2, 2, cores), ALL)
    matrix, vector = P(ALL, None), P(ALL)
    in_specs = (
        matrix,
        matrix,
        vector,
        matrix,
        vector,
        matrix,
        matrix,
        matrix,
        matrix,
        vector,
        matrix,
        matrix,
        matrix,
        matrix,
    )
    out_specs = (
        matrix,
        matrix,
        vector,
        matrix,
        vector,
        matrix,
        matrix,
        matrix,
        matrix,
        vector,
        matrix,
        matrix,
        matrix,
    )

    def body(*args):
        return shards(members, ring, cores, *args)

    return jax.shard_map(body, mesh=fine, in_specs=in_specs, out_specs=out_specs, check_vma=False)
```

time: 691 us -> 625 us (0.904)
  blocking collectives: 31.4 us -> 0 us
  local copies, waits for them, and re-layouts: 78.2 us -> 54.2 us
  other arithmetic: 85.4 us -> 71 us
  Pallas kernels: 44.1 us -> 57.2 us
  matrix products: 125 us -> 112 us
  starting transfers between devices: 53.9 us -> 66.6 us
    all_to_all x2 -> x0, blocking collectives: 31.4 us -> none  [the longest x1 20.6 us: shards(): gate_up = lax.all_to_all(gate_up, DP, 0, 0, tiled=True)]
    ppermute x45, waiting for transfers between devices: 240 us -> 214 us  [trade(): return lax.ppermute(values, axis, [(0, 1), (1, 0)])]
    ppermute x0 -> x12, waiting for transfers between devices: none -> 22.7 us  [swap_blocks(): lax.ppermute(block(me ^ code), DP, [(i, i ^ code) for i in range(4)])]
    ppermute x0 -> x12, starting transfers between devices: none -> 18.3 us  [swap_blocks(): lax.ppermute(block(me ^ code), DP, [(i, i ^ code) for i in range(4)])]
    dot_general x5 -> x3, matrix products: 43.8 us -> 29.8 us  [dot_tn(): lax.dot_general(a, b, (((0,), (0,)), ((), ())), preferred_element_type=f32)]
    pallas_call x2, Pallas kernels: 44.1 us -> 57.2 us  [the longest x1 38.8 us: attend_back(): pl.pallas_call(functools.partial(attend_back_kernel, members, heads), gri...]
    select_n x6 -> x0, other arithmetic: 10.4 us -> none  [the longest x3 7.79 us: shards(): jnp.where(p[1], p[2], -1).reshape(1, rows)]
    all_to_all x2 -> x0, starting transfers between devices: 7.87 us -> none  [the longest x1 4.46 us: shards(): gate_up_share = lax.all_to_all(gate_up_share, DP, 0, 0, tiled=True)]
  transfers between devices with their start and end apart: 56 -> 66, of which waited for: 31 -> 39; matrix products, arithmetic and copies ran while one was open for 38% -> 35% of each run, Pallas kernels for 6% -> 9%
where the time goes in v3:
time: 625 us; the launch traced here: 617 us
  waiting for transfers between devices  239 us (38%)
  matrix products  112 us (18%)
  other arithmetic  71 us (11%)
  starting transfers between devices  66.6 us (11%)
  Pallas kernels  57.2 us (9%)
  local copies, waits for them, and re-layouts  54.2 us (9%)
  between operations  16.8 us (3%)
    ppermute x45, waiting for transfers between devices, trade(): return lax.ppermute(values, axis, [(0, 1), (1, 0)])  214 us
    ppermute x45, starting transfers between devices, trade(): return lax.ppermute(values, axis, [(0, 1), (1, 0)])  47.7 us
    dot_general x5, matrix products, dot(): return jnp.dot(a, b, preferred_element_type=f32)  41.3 us
    dot_general x4, matrix products, dot_nt(): lax.dot_general(a, b, (((1,), (1,)), ((), ())), preferred_element_type=f32)  41.1 us
    pallas_call x1, Pallas kernels, attend_back(): pl.pallas_call(functools.partial(attend_back_kernel, members, heads), gri...  38.8 us
    unnamed x141, local copies, waits for them, and re-layouts  30.1 us
    dot_general x3, matrix products, dot_tn(): lax.dot_general(a, b, (((0,), (0,)), ((), ())), preferred_element_type=f32)  29.8 us
    ppermute x12, waiting for transfers between devices, swap_blocks(): lax.ppermute(block(me ^ code), DP, [(i, i ^ code) for i in range(4)])  22.7 us
  transfers between devices with their start and end apart: 66, of which 39 were waited for; matrix products, arithmetic and copies ran while one was open for 35% of the time, Pallas kernels for 9%

profile of v3, /device:TPU:0, one launch (start us, length us, event | category | flops | bytes accessed | tf_op | source)
XLA Modules:
  0.0 616.8 jit_solution(4313445618912986034)
XLA Ops:
  28.8 6.8 %collective-permute-done.1 = bf16[32,1024]{1,0:T(8,128)(2,1)S(1)} collective-permute-done((bf16[32,1024]{1,0:T(8,128)(2,1)S(1)}, bf16[32,1024]{1,0:T(8,128)(2,1)S(1)}, u32[]{:S(2)}, u32[]{:S(2)}) %collective-permute-start.1) | collective-permute-done | bytes 65568 | tf_op jit(solution)/shard_map/ppermute | solution.py:200
  48.2 31.1 %collective-permute-done.7 = bf16[512,1664]{1,0:T(8,128)(2,1)S(1)} collective-permute-done((bf16[512,1664]{1,0:T(8,128)(2,1)}, bf16[512,1664]{1,0:T(8,128)(2,1)S(1)}, u32[]{:S(2)}, u32[]{:S(2)}) %collective-permute-start.7) | collective-permute-done | bytes 1703968 | tf_op jit(solution)/shard_map/ppermute | solution.py:97
  86.6 13.2 %collective-permute-done.8 = bf16[256,1664]{1,0:T(8,128)(2,1)S(1)} collective-permute-done((bf16[256,1664]{1,0:T(8,128)(2,1)S(1)}, bf16[256,1664]{1,0:T(8,128)(2,1)S(1)}, u32[]{:S(2)}, u32[]{:S(2)}) %collective-permute-start.8) | collective-permute-done | bytes 852000 | tf_op jit(solution)/shard_map/ppermute | solution.py:97
  120.5 11.9 %collective-permute-done.11 = bf16[256,1536]{1,0:T(8,128)(2,1)S(1)} collective-permute-done((bf16[256,1536]{1,0:T(8,128)(2,1)S(1)}, bf16[256,1536]{1,0:T(8,128)(2,1)S(1)}, u32[]{:S(2)}, u32[]{:S(2)}) %collective-permute-start.11) | collective-permute-done | bytes 786464 | tf_op jit(solution)/shard_map/ppermute | solution.py:97
  135.0 7.0 %collective-permute-done.12 = bf16[128,1536]{1,0:T(8,128)(2,1)S(1)} collective-permute-done((bf16[128,1536]{1,0:T(8,128)(2,1)S(1)}, bf16[128,1536]{1,0:T(8,128)(2,1)S(1)}, u32[]{:S(2)}, u32[]{:S(2)}) %collective-permute-start.12) | collective-permute-done | bytes 393248 | tf_op jit(solution)/shard_map/ppermute | solution.py:97
  147.1 18.4 %shard_map.237 = (bf16[1024,1024]{1,0:T(8,128)(2,1)S(1)}, bf16[1024,1024]{1,0:T(8,128)(2,1)S(1)}) custom-call(s32[4,2]{1,0:T(4,128)S(1)} %copy.113.lengths_ref, bf16[1024,1536]{1,0:T(8,128)(2,1)S(1)} %constant_dynamic-update-slice_fusion.5.latent_ref.key_ref.value_ref, bf16[1024,1024]{1,0:T(8,128)(2,1)S(1)} %bitcast.169, ...), custom_call_target="tpu_custom_call" | custom-call | flops 3221225472 | bytes 7340032 | tf_op jit(solution)/shard_map/pallas_call | solution.py:273
  176.9 18.8 %collective-permute-done.18 = bf16[256,2048]{1,0:T(8,128)(2,1)S(1)} collective-permute-done((bf16[256,2048]{1,0:T(8,128)(2,1)S(1)}, bf16[256,2048]{1,0:T(8,128)(2,1)S(1)}, u32[]{:S(2)}, u32[]{:S(2)}) %collective-permute-start.18) | collective-permute-done | bytes 1048608 | tf_op jit(solution)/shard_map/ppermute | solution.py:97
  213.9 17.5 %collective-permute-done.21 = bf16[256,2048]{1,0:T(8,128)(2,1)S(1)} collective-permute-done((bf16[256,2048]{1,0:T(8,128)(2,1)}, bf16[256,2048]{1,0:T(8,128)(2,1)S(1)}, u32[]{:S(2)}, u32[]{:S(2)}) %collective-permute-start.21) | collective-permute-done | bytes 1048608 | tf_op jit(solution)/shard_map/ppermute | solution.py:97
  247.2 9.0 %collective-permute-done.23 = bf16[128,2048]{1,0:T(8,128)(2,1)S(1)} collective-permute-done((bf16[128,2048]{1,0:T(8,128)(2,1)S(1)}, bf16[128,2048]{1,0:T(8,128)(2,1)S(1)}, u32[]{:S(2)}, u32[]{:S(2)}) %collective-permute-start.23) | collective-permute-done | bytes 524320 | tf_op jit(solution)/shard_map/ppermute | solution.py:97
  257.0 19.0 %fusion.112 = f32[1024,2816]{1,0:T(8,128)} fusion(bf16[1024,2048]{1,0:T(8,128)(2,1)} %constant_dynamic-update-slice_fusion.10, bf16[2048,2816]{1,0:T(8,128)(2,1)} %bitcast.197), kind=kOutput, calls=%fused_computation.341 | convolution fusion | flops 11811160064 | bytes 27262976 | tf_op jit(solution)/shard_map/dot_general | solution.py:81
  282.1 6.7 %multiply_convert_fusion.2 = bf16[1024,1408]{1,0:T(8,128)(2,1)S(1)} fusion(f32[1024,2816]{1,0:T(8,128)} %fusion.112), kind=kLoop, calls=%fused_computation.16 | loop fusion | flops 8650752 | bytes 14417920 | tf_op jit(solution)/shard_map/convert_element_type | solution.py:514
  290.4 8.1 %convolution_convert_fusion.2 = bf16[1408,2048]{1,0:T(8,128)(2,1)} fusion(bf16[1024,1408]{1,0:T(8,128)(2,1)S(1)} %multiply_convert_fusion.2, bf16[1024,2048]{1,0:T(8,128)(2,1)S(1)} %constant_dynamic-update-slice_fusion.15), kind=kOutput, calls=%fused_computation.4 | convolution fusion | flops 5908463616 | bytes 12845056 | tf_op jit(solution)/shard_map/dot_general | solution.py:89
  298.7 14.9 %multiply_convert_fusion = (bf16[1024,1408]{1,0:T(8,128)(2,1)S(1)}, bf16[1024,1408]{1,0:T(8,128)(2,1)S(1)}) fusion(f32[1024,2816]{1,0:T(8,128)} %fusion.112, bf16[1024,2048]{1,0:T(8,128)(2,1)} %copy-done.42, bf16[1408,2048]{1,0:T(8,128)(2,1)} %all-gather.14.cloned.1.call-done), kind=kOutput, calls=%fused_computation.14 | convolution fusion | flops 5924323328 | bytes 27262976 | tf_op jit(solution)/shard_map/dot_general | solution.py:85
  313.5 12.1 %fusion.7 = bf16[768,2048]{1,0:T(8,128)(2,1)S(1)} fusion(bf16[2048,2816]{1,0:T(8,128)(2,1)} %bitcast.198, bf16[1024,1408]{1,0:T(8,128)(2,1)S(1)} %get-tuple-element.127, bf16[1024,1408]{1,0:T(8,128)(2,1)S(1)} %get-tuple-element.126), kind=kOutput, calls=%fused_computation.24 | convolution fusion | flops 8868593664 | bytes 20447232 | tf_op jit(solution)/shard_map/dot_general | solution.py:85
  332.4 9.1 %fusion.113 = f32[256,2048]{1,0:T(8,128)} fusion(bf16[256,2816]{1,0:T(8,128)(2,1)S(1)} %fusion.23, bf16[2048,2816]{1,0:T(8,128)(2,1)} %bitcast.199), kind=kOutput, calls=%fused_computation.342 | convolution fusion | flops 2952790016 | bytes 15073280 | tf_op jit(solution)/shard_map/dot_general | solution.py:85
  347.2 18.4 %convolution_convert_fusion = bf16[2048,2816]{1,0:T(8,128)(2,1)} fusion(bf16[1024,2048]{1,0:T(8,128)(2,1)} %constant_dynamic-update-slice_fusion.10, bf16[1024,2816]{1,0:T(8,128)(2,1)S(1)} %bitcast.175), kind=kOutput, calls=%fused_computation | convolution fusion | flops 11816927232 | bytes 21495808 | tf_op jit(solution)/shard_map/dot_general | solution.py:89
  369.0 6.7 %collective-permute-done.28 = bf16[128,2048]{1,0:T(8,128)(2,1)S(1)} collective-permute-done((bf16[128,2048]{1,0:T(8,128)(2,1)}, bf16[128,2048]{1,0:T(8,128)(2,1)S(1)}, u32[]{:S(2)}, u32[]{:S(2)}) %collective-permute-start.28) | collective-permute-done | bytes 524320 | tf_op jit(solution)/shard_map/ppermute | solution.py:97
  385.4 18.8 %collective-permute-done.31 = bf16[256,2048]{1,0:T(8,128)(2,1)S(1)} collective-permute-done((bf16[256,2048]{1,0:T(8,128)(2,1)S(1)}, bf16[256,2048]{1,0:T(8,128)(2,1)S(1)}, u32[]{:S(2)}, u32[]{:S(2)}) %collective-permute-start.31) | collective-permute-done | bytes 1048608 | tf_op jit(solution)/shard_map/ppermute | solution.py:97
  406.7 8.9 %convolution_convert_fusion.3 = bf16[1024,2048]{1,0:T(8,128)(2,1)S(1)} fusion(bf16[1024,1408]{1,0:T(8,128)(2,1)S(1)} %copy-done.29, bf16[1408,2048]{1,0:T(8,128)(2,1)} %all-gather.14.cloned.1.call-done), kind=kOutput, calls=%fused_computation.21 | convolution fusion | flops 5907677184 | bytes 12845056 | tf_op jit(solution)/shard_map/dot_general | solution.py:81
  425.1 38.8 %shard_map.238 = (bf16[1024,1536]{1,0:T(8,128)(2,1)}, bf16[1024,2048]{1,0:T(8,128)(2,1)}, bf16[1024,1024]{1,0:T(8,128)(2,1)}) custom-call(s32[4,2]{1,0:T(4,128)S(1)} %copy.113.lengths_ref, bf16[1024,2048]{1,0:T(8,128)(2,1)} %copy-done.41, bf16[1024,2048]{1,0:T(8,128)(2,1)} %all-gather.10.cloned.1.call-done.out_ref, bf16[1024,1024]{1,0:T(8,128)(2,1)S(1)} %bitcast.170, ...), custom_call_target="tpu_custom_call" | custom-call | flops 15569256448 | bytes 16777216 | tf_op jit(solution)/shard_map/pallas_call | solution.py:365
  470.5 8.9 %collective-permute-done.38 = bf16[256,1536]{1,0:T(8,128)(2,1)S(1)} collective-permute-done((bf16[256,1536]{1,0:T(8,128)(2,1)}, bf16[256,1536]{1,0:T(8,128)(2,1)S(1)}, u32[]{:S(2)}, u32[]{:S(2)}) %collective-permute-start.38) | collective-permute-done | bytes 786464 | tf_op jit(solution)/shard_map/ppermute | solution.py:97
  528.0 10.5 %collective-permute-done.40 = bf16[128,2048]{1,0:T(8,128)(2,1)S(1)} collective-permute-done((bf16[128,2048]{1,0:T(8,128)(2,1)S(1)}, bf16[128,2048]{1,0:T(8,128)(2,1)S(1)}, u32[]{:S(2)}, u32[]{:S(2)}) %collective-permute-start.40) | collective-permute-done | bytes 524320 | tf_op jit(solution)/shard_map/ppermute | solution.py:97
  546.8 7.9 %collective-permute-done.56 = bf16[64,2816]{1,0:T(8,128)(2,1)S(1)} collective-permute-done((bf16[64,2816]{1,0:T(8,128)(2,1)S(1)}, bf16[64,2816]{1,0:T(8,128)(2,1)S(1)}, u32[]{:S(2)}, u32[]{:S(2)}) %collective-permute-start.56) | collective-permute-done | bytes 360480 | tf_op jit(solution)/shard_map/ppermute | solution.py:200
  563.4 11.9 %collective-permute-done.45 = bf16[256,1664]{1,0:T(8,128)(2,1)S(1)} collective-permute-done((bf16[256,1664]{1,0:T(8,128)(2,1)S(1)}, bf16[256,1664]{1,0:T(8,128)(2,1)S(1)}, u32[]{:S(2)}, u32[]{:S(2)}) %collective-permute-start.45) | collective-permute-done | bytes 852000 | tf_op jit(solution)/shard_map/ppermute | solution.py:97
  (418 shorter events, 265.6 us)
Async XLA Ops:
  7.2 31.9 %all-gather.6.cloned.1.call-start = ((), (), s32[]{:S(2)}) async-start(), calls=%async_computation.4 | async-start | bytes 1916928 | tf_op jit(solution)/shard_map/all_gather | solution.py:457
  10.4 135.1 %all-gather.8.cloned.1.call-start = ((), (), s32[]{:S(2)}) async-start(), calls=%async_computation.5 | async-start | bytes 2359296 | tf_op jit(solution)/shard_map/all_gather | solution.py:467
  12.1 24.3 %collective-permute-start.3 = (bf16[64,2816]{1,0:T(8,128)(2,1)S(1)}, bf16[64,2816]{1,0:T(8,128)(2,1)S(1)}, u32[]{:S(2)}, u32[]{:S(2)}) collective-permute-start(bf16[64,2816]{1,0:T(8,128)(2,1)S(1)} %pad_maximum_fusion.21), channel_id=1, source_target_pairs={{0,8},{8,0},{16,24},{24,16},{1,9},{9,1},{17,25},{25,17},{2,10},{10... | collective-permute-start | bytes 1081352 | tf_op jit(solution)/shard_map/ppermute | solution.py:200
  15.1 21.3 %collective-permute-start.4 = (bf16[64,2816]{1,0:T(8,128)(2,1)S(1)}, bf16[64,2816]{1,0:T(8,128)(2,1)S(1)}, u32[]{:S(2)}, u32[]{:S(2)}) collective-permute-start(bf16[64,2816]{1,0:T(8,128)(2,1)S(1)} %pad_maximum_fusion.22), channel_id=1, source_target_pairs={{0,16},{8,24},{16,0},{24,8},{1,17},{9,25},{17,1},{25,9},{2,18},{10... | collective-permute-start | bytes 1081352 | tf_op jit(solution)/shard_map/ppermute | solution.py:200
  38.0 130.1 %all-gather.10.cloned.1.call-start = ((), (), s32[]{:S(2)}) async-start(), calls=%async_computation.6 | async-start | bytes 4718592 | tf_op jit(solution)/shard_map/all_gather | solution.py:469
  39.1 217.9 %all-gather.12.cloned.1.call-start = ((), (), s32[]{:S(2)}) async-start(), calls=%async_computation.7 | async-start | bytes 12976128 | tf_op jit(solution)/shard_map/all_gather | solution.py:470
  39.7 259.0 %all-gather.14.cloned.1.call-start = ((), (), s32[]{:S(2)}) async-start(), calls=%async_computation.8 | async-start | bytes 6488064 | tf_op jit(solution)/shard_map/all_gather | solution.py:472
  39.7 39.6 %collective-permute-start.7 = (bf16[512,1664]{1,0:T(8,128)(2,1)}, bf16[512,1664]{1,0:T(8,128)(2,1)S(1)}, u32[]{:S(2)}, u32[]{:S(2)}) collective-permute-start(bf16[512,1664]{1,0:T(8,128)(2,1)} %all-gather.6.cloned.1.call-done), channel_id=1, source_target_pairs={{0,16},{16,0},{1,17},{17,1},{2,18},{18,2},{3,19},{19,3},{4,20},{20... | collective-permute-start | bytes 5111816 | tf_op jit(solution)/shard_map/ppermute | solution.py:97
  41.3 39.7 %collective-permute-start.6 = (bf16[512,1664]{1,0:T(8,128)(2,1)}, bf16[512,1664]{1,0:T(8,128)(2,1)}, u32[]{:S(2)}, u32[]{:S(2)}) collective-permute-start(bf16[512,1664]{1,0:T(8,128)(2,1)} %all-gather.6.cloned.1.call-done), channel_id=1, source_target_pairs={{0,8},{8,0},{1,9},{9,1},{2,10},{10,2},{3,11},{11,3},{4,12},{12,4},... | collective-permute-start | bytes 5111816 | tf_op jit(solution)/shard_map/ppermute | solution.py:97
  142.5 25.6 %collective-permute-start.14 = (bf16[256,2048]{1,0:T(8,128)(2,1)}, bf16[256,2048]{1,0:T(8,128)(2,1)}, u32[]{:S(2)}, u32[]{:S(2)}) collective-permute-start(bf16[256,2048]{1,0:T(8,128)(2,1)} %fusion.14), channel_id=1, source_target_pairs={{0,8},{8,0},{1,9},{9,1},{2,10},{10,2},{3,11},{11,3},{4,12},{12,4},... | collective-permute-start | bytes 3145736 | tf_op jit(solution)/shard_map/ppermute | solution.py:97
  143.3 24.9 %collective-permute-start.15 = (bf16[256,2048]{1,0:T(8,128)(2,1)}, bf16[256,2048]{1,0:T(8,128)(2,1)}, u32[]{:S(2)}, u32[]{:S(2)}) collective-permute-start(bf16[256,2048]{1,0:T(8,128)(2,1)} %fusion.14), channel_id=1, source_target_pairs={{0,16},{16,0},{1,17},{17,1},{2,18},{18,2},{3,19},{19,3},{4,20},{20... | collective-permute-start | bytes 3145736 | tf_op jit(solution)/shard_map/ppermute | solution.py:97
  174.5 21.2 %collective-permute-start.18 = (bf16[256,2048]{1,0:T(8,128)(2,1)S(1)}, bf16[256,2048]{1,0:T(8,128)(2,1)S(1)}, u32[]{:S(2)}, u32[]{:S(2)}) collective-permute-start(bf16[256,2048]{1,0:T(8,128)(2,1)S(1)} %pad_maximum_fusion.9), channel_id=1, source_target_pairs={{0,16},{16,0},{1,17},{17,1},{2,18},{18,2},{3,19},{19,3},{4,20},{20... | collective-permute-start | bytes 3145736 | tf_op jit(solution)/shard_map/ppermute | solution.py:97
  175.5 22.7 %collective-permute-start.16 = (bf16[256,2048]{1,0:T(8,128)(2,1)S(1)}, bf16[256,2048]{1,0:T(8,128)(2,1)S(1)}, u32[]{:S(2)}, u32[]{:S(2)}) collective-permute-start(bf16[256,2048]{1,0:T(8,128)(2,1)S(1)} %pad_maximum_fusion.8), channel_id=1, source_target_pairs={{0,8},{8,0},{1,9},{9,1},{2,10},{10,2},{3,11},{11,3},{4,12},{12,4},... | collective-permute-start | bytes 3145736 | tf_op jit(solution)/shard_map/ppermute | solution.py:97
  212.4 25.1 %collective-permute-start.20 = (bf16[256,2048]{1,0:T(8,128)(2,1)}, bf16[256,2048]{1,0:T(8,128)(2,1)}, u32[]{:S(2)}, u32[]{:S(2)}) collective-permute-start(bf16[256,2048]{1,0:T(8,128)(2,1)} %get-tuple-element.123), channel_id=1, source_target_pairs={{0,8},{8,0},{1,9},{9,1},{2,10},{10,2},{3,11},{11,3},{4,12},{12,4},... | collective-permute-start | bytes 3145736 | tf_op jit(solution)/shard_map/ppermute | solution.py:97
  213.8 170.0 %reduce-scatter.5.cloned.1.call-start = ((), (), s32[]{:S(2)}) async-start(), calls=%async_computation.9 | async-start | bytes 6488064 | tf_op jit(solution)/shard_map/reduce_scatter | solution.py:517
  234.9 41.1 %collective-permute-start.24 = (bf16[128,2048]{1,0:T(8,128)(2,1)}, bf16[128,2048]{1,0:T(8,128)(2,1)}, u32[]{:S(2)}, u32[]{:S(2)}) collective-permute-start(bf16[128,2048]{1,0:T(8,128)(2,1)} %slice.488), channel_id=1, source_target_pairs={{0,8},{8,0},{1,9},{9,1},{2,10},{10,2},{3,11},{11,3},{4,12},{12,4},... | collective-permute-start | bytes 1572872 | tf_op jit(solution)/shard_map/ppermute | solution.py:97
  237.3 38.7 %collective-permute-start.25 = (bf16[128,2048]{1,0:T(8,128)(2,1)}, bf16[128,2048]{1,0:T(8,128)(2,1)}, u32[]{:S(2)}, u32[]{:S(2)}) collective-permute-start(bf16[128,2048]{1,0:T(8,128)(2,1)} %slice.489), channel_id=1, source_target_pairs={{0,16},{16,0},{1,17},{17,1},{2,18},{18,2},{3,19},{19,3},{4,20},{20... | collective-permute-start | bytes 1572872 | tf_op jit(solution)/shard_map/ppermute | solution.py:97
  298.6 195.8 %reduce-scatter.7.cloned.1.call-start = ((), (), s32[]{:S(2)}) async-start(), calls=%async_computation.10 | async-start | bytes 12976128 | tf_op jit(solution)/shard_map/reduce_scatter | solution.py:537
  365.6 224.2 %reduce-scatter.11.cloned.1.call-start = ((), (), s32[]{:S(2)}) async-start(), calls=%async_computation.12 | async-start | bytes 2359296 | tf_op jit(solution)/shard_map/reduce_scatter | solution.py:572
  383.9 22.0 %collective-permute-start.30 = (bf16[256,2048]{1,0:T(8,128)(2,1)S(1)}, bf16[256,2048]{1,0:T(8,128)(2,1)S(1)}, u32[]{:S(2)}, u32[]{:S(2)}) collective-permute-start(bf16[256,2048]{1,0:T(8,128)(2,1)S(1)} %get-tuple-element.75), channel_id=1, source_target_pairs={{0,8},{8,0},{1,9},{9,1},{2,10},{10,2},{3,11},{11,3},{4,12},{12,4},... | collective-permute-start | bytes 3145736 | tf_op jit(solution)/shard_map/ppermute | solution.py:97
  423.0 40.9 %collective-permute-start.35 = (bf16[256,2048]{1,0:T(8,128)(2,1)S(1)}, bf16[256,2048]{1,0:T(8,128)(2,1)S(1)}, u32[]{:S(2)}, u32[]{:S(2)}) collective-permute-start(bf16[256,2048]{1,0:T(8,128)(2,1)S(1)} %pad_maximum_fusion.13), channel_id=1, source_target_pairs={{0,16},{16,0},{1,17},{17,1},{2,18},{18,2},{3,19},{19,3},{4,20},{20... | collective-permute-start | bytes 3145736 | tf_op jit(solution)/shard_map/ppermute | solution.py:97
  423.8 40.2 %collective-permute-start.34 = (bf16[256,2048]{1,0:T(8,128)(2,1)S(1)}, bf16[256,2048]{1,0:T(8,128)(2,1)S(1)}, u32[]{:S(2)}, u32[]{:S(2)}) collective-permute-start(bf16[256,2048]{1,0:T(8,128)(2,1)S(1)} %pad_maximum_fusion.12), channel_id=1, source_target_pairs={{0,8},{8,0},{1,9},{9,1},{2,10},{10,2},{3,11},{11,3},{4,12},{12,4},... | collective-permute-start | bytes 3145736 | tf_op jit(solution)/shard_map/ppermute | solution.py:97
  470.2 119.5 %reduce-scatter.9.cloned.1.call-start = ((), (), s32[]{:S(2)}) async-start(), calls=%async_computation.11 | async-start | bytes 4718592 | tf_op jit(solution)/shard_map/reduce_scatter | solution.py:561
  526.0 20.8 %collective-permute-start.54 = (bf16[64,2816]{1,0:T(8,128)(2,1)S(1)}, bf16[64,2816]{1,0:T(8,128)(2,1)S(1)}, u32[]{:S(2)}, u32[]{:S(2)}) collective-permute-start(bf16[64,2816]{1,0:T(8,128)(2,1)S(1)} %get-tuple-element.187), channel_id=1, source_target_pairs={{0,8},{8,0},{16,24},{24,16},{1,9},{9,1},{17,25},{25,17},{2,10},{10... | collective-permute-start | bytes 1081352 | tf_op jit(solution)/shard_map/ppermute | solution.py:200
  (102 other events, 1064.3 us)
Sparse Core Ops, SparseCore 0:
  10.5 28.5 all-gather.5
  41.3 28.6 all-gather.7
  71.5 46.6 all-gather.9
  120.2 106.7 all-gather.11
  228.6 58.6 all-gather.13
  298.7 64.2 reduce-scatter.4
  365.7 119.8 reduce-scatter.6
  487.9 34.1 reduce-scatter.10
  524.4 48.6 reduce-scatter.8

commit v4 on v3

--- a/solution.py
+++ b/solution.py
@@ -186,11 +186,37 @@
     return [lax.dynamic_index_in_dim(total, me ^ code, 0, keepdims=False) for code in range(4)]
 
 
-def small_middle(slots):
-    total = scatter_quad(slots, *GROUP).astype(bf16)
+def pairs_along_z(total):
     total = total.reshape(4, -1, total.shape[1])
     me = lax.axis_index("zh") * 2 + lax.axis_index("zl")
     return [lax.dynamic_index_in_dim(total, me ^ code, 0, keepdims=False) for code in range(4)]
+
+
+def add_up(parts):
+    total = parts[0].astype(f32)
+    for part in parts[1:]:
+        total = total + part.astype(f32)
+    return total
+
+
+def along_z(values, code):
+    return lax.ppermute(values, ("zh", "zl"), [(i, i ^ code) for i in range(4)])
+
+
+def share_small(values, cores):
+    n, c = values.shape
+    if cores != 2:
+        whole = lax.all_gather(values, RING, axis=0, tiled=True)
+        return jnp.concatenate(gather_quad(whole, *GROUP), axis=0), whole
+    core, place = lax.axis_index("r"), lax.axis_index("zh") * 2 + lax.axis_index("zl")
+    line = jnp.stack([values] + [along_z(values, code) for code in (1, 2, 3)])
+    line = [lax.dynamic_index_in_dim(line, place ^ k, 0, keepdims=False) for k in range(4)]
+    line = jnp.concatenate(line, axis=0)
+    total = jnp.zeros((4, 4, 2, n, c), values.dtype)
+    for slot, part in enumerate(gather_quad(line, *GROUP)):
+        for where, piece in ((core, part), (1 - core, trade(part, "r"))):
+            total = lax.dynamic_update_slice(total, piece.reshape(1, 4, 1, n, c), (slot, 0, where, 0, 0))
+    return total.reshape(32 * n, c), line
 
 
 def swap_blocks(block):
@@ -252,46 +278,80 @@
     return expo / jnp.sum(expo, axis=-1, keepdims=True)
 
 
+def query_block(weight_ref, member, heads):
+    ring, rows, width = weight_ref.shape
+    high, low = divmod(member, 2)
+    part = weight_ref[:, low * rows // 2 : (low + 1) * rows // 2, high * width // 2 : (high + 1) * width // 2]
+    return part.reshape(ring * rows // 2, width // 2)
+
+
 def attend_kernel(
-    lengths_ref, latent_ref, weight_ref, key_ref, value_ref, query_ref, mix_ref, cos_ref, sin_ref
+    members,
+    heads,
+    lengths_ref,
+    latent_ref,
+    weight_ref,
+    out_ref,
+    key_ref,
+    value_ref,
+    query_ref,
+    mix_ref,
+    back_ref,
+    cos_ref,
+    sin_ref,
 ):
-    @pl.when(pl.program_id(1) == 0)
-    def _():
-        fill_angles(lengths_ref, cos_ref, sin_ref)
-
-    query_rot = turn(dot(latent_ref[...], weight_ref[...]), cos_ref[...], sin_ref[...]).astype(bf16)
-    query_ref[...] = query_rot
-    probs = probabilities(query_rot, key_ref[...], lengths_ref)
-    mix_ref[...] = dot(probs.astype(bf16), value_ref[...]).astype(bf16)
-
-
-def attend(lengths, packed, query_full, rows, heads):
-    total, latent_width = packed.shape[0], query_full.shape[0]
-    last = latent_width // HD
-    block = pl.BlockSpec((rows, HD), lambda m, h, s: (m, h))
+    fill_angles(lengths_ref, cos_ref, sin_ref)
+    step = latent_ref.shape[1] // members
+    queries = dot(latent_ref[:, :step], query_block(weight_ref, 0, heads))
+    for k in range(1, members):
+        queries += dot(latent_ref[:, k * step : (k + 1) * step], query_block(weight_ref, k, heads))
+    for head in range(heads):
+        columns = slice(head * HD, (head + 1) * HD)
+        query_rot = turn(queries[:, columns], cos_ref[...], sin_ref[...]).astype(bf16)
+        query_ref[:, columns] = query_rot
+        probs = probabilities(query_rot, key_ref[...], lengths_ref)
+        mix_ref[:, columns] = dot(probs.astype(bf16), value_ref[...]).astype(bf16)
+    out_full = out_ref[...].reshape(heads * HD, -1)
+    back_ref[...] = dot(mix_ref[...], out_full).astype(bf16)
+
+
+def packed_specs(gathered):
+    ring, rows, width = gathered.shape
+    third = rows // 3
+    return [
+        pl.BlockSpec((ring, third, width), lambda m, s: (0, 2, 0), pipeline_mode=pl.Buffered(1)),
+        pl.BlockSpec((ring, 2 * third, width), lambda m, s: (0, 0, 0), pipeline_mode=pl.Buffered(1)),
+    ]
+
+
+def attend(lengths, packed, gathered, rows, heads):
+    total, width = packed.shape[0], gathered.shape[2]
+    latent_width = packed.shape[1] - 2 * HD
+    last, members = latent_width // HD, total // rows
+    block = pl.BlockSpec((rows, heads * HD), lambda m, s: (m, 0))
     out = jax.ShapeDtypeStruct((total, heads * HD), bf16)
     return pl.pallas_call(
-        attend_kernel,
+        functools.partial(attend_kernel, members, heads),
         grid_spec=pltpu.PrefetchScalarGridSpec(
             num_scalar_prefetch=1,
-            grid=(total // rows, heads),
+            grid=(members,),
             in_specs=[
-                pl.BlockSpec((rows, latent_width), lambda m, h, s: (m, 0)),
-                pl.BlockSpec((latent_width, HD), lambda m, h, s: (0, h)),
-                pl.BlockSpec((rows, HD), lambda m, h, s: (m, last)),
-                pl.BlockSpec((rows, HD), lambda m, h, s: (m, last + 1)),
+                pl.BlockSpec((rows, latent_width), lambda m, s: (m, 0)),
+                *packed_specs(gathered),
+                pl.BlockSpec((rows, HD), lambda m, s: (m, last)),
+                pl.BlockSpec((rows, HD), lambda m, s: (m, last + 1)),
             ],
-            out_specs=[block, block],
+            out_specs=[block, block, pl.BlockSpec((rows, width), lambda m, s: (m, 0))],
             scratch_shapes=[pltpu.VMEM((rows, HD // 2), f32), pltpu.VMEM((rows, HD // 2), f32)],
         ),
-        out_shape=[out, out],
-        compiler_params=pltpu.CompilerParams(vmem_limit_bytes=32 * 2**20),
+        out_shape=[out, out, jax.ShapeDtypeStruct((total, width), bf16)],
+        compiler_params=pltpu.CompilerParams(vmem_limit_bytes=40 * 2**20),
         cost_estimate=pl.CostEstimate(
-            flops=2 * total * heads * HD * (latent_width + 2 * rows),
-            bytes_accessed=total * heads * HD * 4 + total * latent_width * 3,
+            flops=2 * total * heads * HD * (latent_width + 2 * rows + width),
+            bytes_accessed=total * heads * HD * 4 + total * latent_width * 3 + 8 * 2**20,
             transcendentals=total * heads * rows,
         ),
-    )(lengths, packed, query_full, packed, packed)
+    )(lengths, packed, gathered, gathered, packed, packed)
 
 
 def attend_back_kernel(
@@ -299,116 +359,127 @@
     heads,
     lengths_ref,
     grad_ref,
+    weight_ref,
     out_ref,
-    weight_ref,
     query_ref,
     latent_ref,
     key_ref,
     value_ref,
     mix_ref,
     packed_ref,
-    out_grad_ref,
-    weight_grad_ref,
-    total_ref,
-    out_total_ref,
-    weight_total_ref,
+    gathered_grad_ref,
+    grads_ref,
+    mixes_ref,
+    latents_ref,
+    query_grads_ref,
     cos_ref,
     sin_ref,
 ):
-    member, head = pl.program_id(0), pl.program_id(1)
-
-    @pl.when(head == 0)
-    def _():
-        fill_angles(lengths_ref, cos_ref, sin_ref)
-        total_ref[...] = jnp.zeros_like(total_ref)
-
-    @pl.when(member == 0)
-    def _():
-        out_total_ref[head] = jnp.zeros_like(out_total_ref.at[0])
-        weight_total_ref[head] = jnp.zeros_like(weight_total_ref.at[0])
-
-    latent_width = weight_ref.shape[0]
+    member = pl.program_id(0)
+    fill_angles(lengths_ref, cos_ref, sin_ref)
+    latent_width = latent_ref.shape[1]
+    step = latent_width // members
+    out_full = out_ref[...].reshape(heads * HD, -1)
     scale = 1.0 / math.sqrt(HD)
-    query_rot, key_rot, value_low = query_ref[...], key_ref[...], value_ref[...]
-    mixture_grad = dot_nt(grad_ref[...], out_ref[...]).astype(bf16)
-    out_total_ref[head] += dot_tn(mix_ref[...], grad_ref[...])
-    probs = probabilities(query_rot, key_rot, lengths_ref)
-    probs_grad = dot_nt(mixture_grad, value_low)
-    row_dot = jnp.sum(probs * probs_grad, axis=-1, keepdims=True)
-    score_grad = (probs * (probs_grad - row_dot)).astype(bf16)
-    query_rot_grad = dot(score_grad, key_rot) * scale
-    query_grad = turn(query_rot_grad, cos_ref[...], -sin_ref[...]).astype(bf16)
-    weight_total_ref[head] += dot_tn(latent_ref[...], query_grad)
-    total_ref[:, :latent_width] += dot_nt(query_grad, weight_ref[...])
-    total_ref[:, latent_width : latent_width + HD] += dot_tn(score_grad, query_rot) * scale
-    total_ref[:, latent_width + HD :] += dot_tn(probs.astype(bf16), mixture_grad)
-
-    @pl.when(head == heads - 1)
-    def _():
-        packed_ref[...] = total_ref[...].astype(bf16)
+    grads_ref[member] = grad_ref[...]
+    mixes_ref[member] = mix_ref[...]
+    latents_ref[member] = latent_ref[...]
+    key_rot, value_low = key_ref[...], value_ref[...]
+    mixture_grads = dot_nt(grad_ref[...], out_full).astype(bf16)
+    key_grad = jnp.zeros(key_rot.shape, f32)
+    value_grad = jnp.zeros(key_rot.shape, f32)
+    for head in range(heads):
+        columns = slice(head * HD, (head + 1) * HD)
+        query_rot, mixture_grad = query_ref[:, columns], mixture_grads[:, columns]
+        probs = probabilities(query_rot, key_rot, lengths_ref)
+        probs_grad = dot_nt(mixture_grad, value_low)
+        row_dot = jnp.sum(probs * probs_grad, axis=-1, keepdims=True)
+        score_grad = (probs * (probs_grad - row_dot)).astype(bf16)
+        query_rot_grad = dot(score_grad, key_rot) * scale
+        query_grads_ref[member, :, columns] = turn(query_rot_grad, cos_ref[...], -sin_ref[...]).astype(bf16)
+        key_grad += dot_tn(score_grad, query_rot)
+        value_grad += dot_tn(probs.astype(bf16), mixture_grad)
+    for k in range(members):
+        latent_part = dot_nt(query_grads_ref[member], query_block(weight_ref, k, heads))
+        packed_ref[:, k * step : (k + 1) * step] = latent_part.astype(bf16)
+    packed_ref[:, latent_width : latent_width + HD] = (key_grad * scale).astype(bf16)
+    packed_ref[:, latent_width + HD :] = value_grad.astype(bf16)
 
     @pl.when(member == members - 1)
     def _():
-        out_grad_ref[...] = out_total_ref[head].astype(bf16)
-        weight_grad_ref[...] = weight_total_ref[head].astype(bf16)
-
-
-def attend_back(lengths, attn_grad, out_full, query_full, query_rot, mixture, packed, rows, heads):
+        rows = members * grad_ref.shape[0]
+        grads = grads_ref[...].reshape(rows, -1)
+        mixes = mixes_ref[...].reshape(rows, -1)
+        latents = latents_ref[...].reshape(rows, -1)
+        query_grads = query_grads_ref[...].reshape(rows, -1)
+        ring, held, width = gathered_grad_ref.shape
+        held = held // 3
+        count = HD // (2 * held)
+        for head in range(heads):
+            columns = slice(head * HD, (head + 1) * HD)
+            part = dot_tn(mixes[:, columns], grads).astype(bf16)
+            gathered_grad_ref[head * count : (head + 1) * count, : 2 * held] = part.reshape(count, 2 * held, width)
+        for k in range(members):
+            part = dot_tn(latents[:, k * step : (k + 1) * step], query_grads).astype(bf16)
+            high, low = divmod(k, 2)
+            place = slice(2 * held + low * held // 2, 2 * held + (low + 1) * held // 2)
+            columns = slice(high * width // 2, (high + 1) * width // 2)
+            gathered_grad_ref[:, place, columns] = part.reshape(ring, held // 2, width // 2)
+
+
+def attend_back(lengths, attn_grad, gathered, query_rot, mixture, packed, rows, heads):
     total, width = attn_grad.shape
-    latent_width = query_full.shape[0]
+    latent_width = packed.shape[1] - 2 * HD
     last, members = latent_width // HD, total // rows
-    block = pl.BlockSpec((rows, HD), lambda m, h, s: (m, h))
-
-    def when_last(m, h):
-        return jnp.where(m == members - 1, h, 0)
+    block = pl.BlockSpec((rows, heads * HD), lambda m, s: (m, 0))
+
+    def kept(columns):
+        return pltpu.VMEM((members, rows, columns), bf16)
 
     return pl.pallas_call(
         functools.partial(attend_back_kernel, members, heads),
         grid_spec=pltpu.PrefetchScalarGridSpec(
             num_scalar_prefetch=1,
-            grid=(members, heads),
+            grid=(members,),
             in_specs=[
-                pl.BlockSpec((rows, width), lambda m, h, s: (m, 0)),
-                pl.BlockSpec((HD, width), lambda m, h, s: (h, 0)),
-                pl.BlockSpec((latent_width, HD), lambda m, h, s: (0, h)),
+                pl.BlockSpec((rows, width), lambda m, s: (m, 0)),
+                *packed_specs(gathered),
                 block,
-                pl.BlockSpec((rows, latent_width), lambda m, h, s: (m, 0)),
-                pl.BlockSpec((rows, HD), lambda m, h, s: (m, last)),
-                pl.BlockSpec((rows, HD), lambda m, h, s: (m, last + 1)),
+                pl.BlockSpec((rows, latent_width), lambda m, s: (m, 0)),
+                pl.BlockSpec((rows, HD), lambda m, s: (m, last)),
+                pl.BlockSpec((rows, HD), lambda m, s: (m, last + 1)),
                 block,
             ],
             out_specs=[
-                pl.BlockSpec((rows, packed.shape[1]), lambda m, h, s: (m, 0)),
-                pl.BlockSpec((HD, width), lambda m, h, s: (when_last(m, h), 0)),
-                pl.BlockSpec((latent_width, HD), lambda m, h, s: (0, when_last(m, h))),
+                pl.BlockSpec((rows, packed.shape[1]), lambda m, s: (m, 0)),
+                pl.BlockSpec(gathered.shape, lambda m, s: (0, 0, 0)),
             ],
             scratch_shapes=[
-                pltpu.VMEM((rows, packed.shape[1]), f32),
-                pltpu.VMEM((heads, HD, width), f32),
-                pltpu.VMEM((heads, latent_width, HD), f32),
+                kept(width),
+                kept(heads * HD),
+                kept(latent_width),
+                kept(heads * HD),
                 pltpu.VMEM((rows, HD // 2), f32),
                 pltpu.VMEM((rows, HD // 2), f32),
             ],
         ),
         out_shape=[
             jax.ShapeDtypeStruct(packed.shape, bf16),
-            jax.ShapeDtypeStruct((heads * HD, width), bf16),
-            jax.ShapeDtypeStruct((latent_width, heads * HD), bf16),
+            jax.ShapeDtypeStruct(gathered.shape, bf16),
         ],
-        compiler_params=pltpu.CompilerParams(vmem_limit_bytes=48 * 2**20),
+        compiler_params=pltpu.CompilerParams(vmem_limit_bytes=56 * 2**20),
         cost_estimate=pl.CostEstimate(
             flops=2 * total * heads * HD * (2 * width + 2 * latent_width + 5 * rows),
             bytes_accessed=total * heads * HD * 8 + total * width * 4,
             transcendentals=total * heads * rows,
         ),
-    )(lengths, attn_grad, out_full, query_full, query_rot, packed, packed, packed, mixture)
-
-
-def by_member(values, members):
-    me = lax.axis_index(DP)
-    step = values.shape[1] // members
+    )(lengths, attn_grad, gathered, gathered, query_rot, packed, packed, packed, mixture)
+
+
+def by_block(values, code, count):
+    step = values.shape[1] // count
     return jnp.concatenate(
-        [lax.dynamic_slice_in_dim(values, (me ^ slot) * step, step, 1) for slot in range(members)], axis=1
+        [lax.dynamic_slice_in_dim(values, (code ^ k) * step, step, 1) for k in range(count)], axis=1
     )
 
 
@@ -454,31 +525,28 @@
     )
     extra = jnp.pad(extra, ((0, 0), (0, 128 - extra.shape[1])))
     small = jnp.concatenate([query_down, key_weight, value_weight, extra], axis=1)
-    small = lax.all_gather(small, RING, axis=0, tiled=True)
-    query_own = jnp.stack(in_order(swap_blocks(lambda k: take_columns(query_up, k, members))))
+    query_own = in_order(swap_blocks(lambda k: take_columns(query_up, k, members)))
+    query_own = jnp.concatenate(
+        [jnp.concatenate(query_own[:2], axis=0), jnp.concatenate(query_own[2:], axis=0)], axis=1
+    )
+    gathered = jnp.concatenate([out_weight, query_own], axis=0)
+    gathered = lax.all_gather(gathered, RING, axis=0, tiled=False)
+    qkv_parts, line = share_small(small, cores)
     gate_up_own = swap_blocks(
         lambda k: jnp.concatenate(
             [take_columns(gate_weight, k, members), take_columns(up_weight, k, members)], axis=1
         )
     )
-    gate_up_own = jnp.stack(in_order(gate_up_own))
-    query_own = after(query_own, gate_up_own)
-    small_parts = gather_quad(after(small, query_own), *GROUP)
-    query_full = lax.all_gather(query_own, RING, axis=1, tiled=True)
-    query_full = query_full.reshape(latent_width, heads * HD)
-    out_full = lax.all_gather(after(out_weight, small), RING, axis=0, tiled=True)
-    gate_up = lax.all_gather(after(gate_up_own, small), RING, axis=1, tiled=True).reshape(width, -1)
-    cut = gate_up.shape[1] // 2
-    down_full = lax.all_gather(after(down_weight, small), RING, axis=0, tiled=True)
+    gate_up_own, down_own = after((jnp.stack(in_order(gate_up_own)), down_weight), qkv_parts)
+    down_full = lax.all_gather(down_own, RING, axis=0, tiled=True)
 
     me, lane = lax.axis_index(DP), lax.axis_index(RING)
     qkv_width = latent_width + 2 * HD
-    qkv_parts = jnp.concatenate(small_parts, axis=0)
-    extra = jnp.stack([part[:, qkv_width:] for part in small_parts])
+    extra = qkv_parts[:, qkv_width:].reshape(members, ring * d_rows, -1)
     group_lengths = lax.dynamic_slice(
         extra, (0, lane * d_rows, 3), (members, lengths.shape[1], 1)
     ).reshape(members, -1).astype(jnp.int32)
-    extra = [lax.dynamic_index_in_dim(extra, me ^ slot, 0, keepdims=False) for slot in range(members)]
+    extra = [lax.dynamic_index_in_dim(extra, me ^ k, 0, keepdims=False) for k in range(members)]
     extra = jnp.concatenate(extra, axis=0).astype(f32).T
     attn_scale = extra[0:1]
     mlp_scale = extra[1:2]
@@ -487,27 +555,35 @@
     token_rows = tokens.astype(f32)
     attn_out, attn_normed, attn_factor = normalize(token_rows, attn_scale)
     attn_in = attn_out.astype(bf16)
-    low = dot(by_member(attn_in, members), qkv_parts)
+    low = dot(by_block(attn_in, me, members), qkv_parts)
     latent = low[:, :latent_width]
     latent_out, latent_normed, latent_factor = normalize(latent, latent_scale)
     latent_in = latent_out.astype(bf16)
     key_own = rotate(low[:, latent_width : latent_width + HD], own_cos, own_sin)
     value_own = low[:, latent_width + HD : qkv_width]
     packed = jnp.concatenate([latent_in, key_own.astype(bf16), value_own.astype(bf16)], axis=1)
-    packed = jnp.concatenate(gather_quad(packed, *GROUP), axis=0)
-    query_rot, mixture = attend(group_lengths, packed, query_full, rows, heads)
+    packed_found = fetch_first(packed, *GROUP)
+    gate_up = lax.all_gather(gate_up_own, RING, axis=1, tiled=True).reshape(width, -1)
+    cut = gate_up.shape[1] // 2
+    packed = jnp.concatenate(fetch_last(packed, packed_found, *GROUP), axis=0)
+    query_rot, mixture, attn_back = attend(group_lengths, packed, gathered, rows, heads)
     ffn_grad_found = fetch_first(after(ffn_grad_own, packed), *GROUP)
-    ffn_grad = fetch_last(ffn_grad_own, after(ffn_grad_found, mixture), *GROUP)
-    mixture = after(mixture, ffn_grad_found)
-    attn_sum = scatter_rows(
-        dot(mixture[:rows], out_full), dot(mixture[rows:], out_full).astype(bf16), *GROUP
-    )
+    attn_back = after(attn_back, ffn_grad_found)
+    attn_slots = [attn_back[i * rows : (i + 1) * rows] for i in range(members)]
+    attn_sent = send_first(attn_slots, *GROUP)
+    one, two = ffn_grad_found
+    ffn_grad = jnp.concatenate([ffn_grad_own, one, two, two], axis=0)
+    ffn_grad_rest = (two[: rows // 2], one[rows // 2 :])
+    attn_sum = send_last(attn_slots, after(attn_sent, ffn_grad, ffn_grad_rest), *GROUP)
     residual = token_rows + living * attn_sum
 
     ffn_out, ffn_normed, ffn_factor = normalize(residual, mlp_scale)
     ffn_in = jnp.concatenate(gather_quad(ffn_out.astype(bf16), *GROUP), axis=0)
     gate_up_act = dot(ffn_in, gate_up)
-    ffn_grad = jnp.concatenate(after(ffn_grad, gate_up_act), axis=0)
+    ffn_grad_rest = after(ffn_grad_rest, ffn_in)
+    ffn_grad_rest = after((trade(ffn_grad_rest[0], "x"), trade(ffn_grad_rest[1], "y")), gate_up_act)
+    ffn_grad = lax.dynamic_update_slice(ffn_grad, ffn_grad_rest[0], (3 * rows, 0))
+    ffn_grad = lax.dynamic_update_slice(ffn_grad, ffn_grad_rest[1], (3 * rows + rows // 2, 0))
     gate_act, up_act = gate_up_act[:, :cut], gate_up_act[:, cut:]
     sigmoid_gate = jax.nn.sigmoid(gate_act)
     silu_gate = gate_act * sigmoid_gate
@@ -522,14 +598,15 @@
     ).astype(bf16)
     up_grad = (hidden_grad * silu_gate).astype(bf16)
     gate_up_grad = jnp.concatenate([gate_grad, up_grad], axis=1)
-    back = dot_nt(gate_up_grad[rows:], gate_up).astype(bf16)
-    slots = [None] + [back[i * rows : (i + 1) * rows] for i in range(members - 1)]
+    back = dot_nt(gate_up_grad, gate_up).astype(bf16)
+    slots = [back[i * rows : (i + 1) * rows] for i in range(members)]
     loads = first_loads(slots)
     back_sent = send_loads(loads, *GROUP)
-    back_own = dot_nt(after(gate_up_grad[:rows], loads), gate_up)
-    loads = last_loads(slots, after(back_sent, back_own))
-    ffn_in_grad = sum_up(back_own, back_sent, send_loads(loads, *GROUP[::-1]))
-    gate_up_wgrad = dot_tn(ffn_in, after(gate_up_grad, loads)).astype(bf16)
+    ffn_back = dot(after(hidden, loads), down_full).astype(bf16)
+    back_sent = after(back_sent, ffn_back)
+    ffn_slots = [ffn_back[i * rows : (i + 1) * rows] for i in range(members)]
+    gate_up_wgrad = dot_tn(ffn_in, after(gate_up_grad, back_sent)).astype(bf16)
+    ffn_in_grad = send_last(slots, after(back_sent, gate_up_wgrad), *GROUP)
     residual_back, mlp_scale_grad = normalize_back(ffn_in_grad, ffn_normed, ffn_factor, mlp_scale)
     residual_grad = grad_rows + residual_back
     attn_grad = (living * residual_grad).astype(bf16)
@@ -539,15 +616,11 @@
     )
     attn_found = fetch_first(attn_grad, *GROUP)
     attn_grad = jnp.concatenate(fetch_last(attn_grad, attn_found, *GROUP), axis=0)
-    ffn_back = dot(after(hidden, attn_found), down_full).astype(bf16)
-    ffn_slots = after(ffn_back, attn_grad)
-    ffn_slots = [ffn_slots[i * rows : (i + 1) * rows] for i in range(members)]
-    ffn_sent = send_first(ffn_slots, *GROUP)
-    packed_grad, out_wgrad, query_wgrad = attend_back(
+    ffn_sent = send_loads(after(first_loads(ffn_slots), attn_grad), *GROUP)
+    packed_grad, gathered_grad = attend_back(
         group_lengths,
-        after(attn_grad, ffn_back),
-        out_full,
-        query_full,
+        attn_grad,
+        gathered,
         query_rot,
         mixture,
         packed,
@@ -558,18 +631,9 @@
     slots = [packed_grad[i * rows : (i + 1) * rows] for i in range(members)]
     loads = first_loads(slots)
     packed_sent = send_loads(loads, *GROUP)
-    out_share = lax.psum_scatter(out_wgrad, RING, scatter_dimension=0, tiled=True)
+    gathered_share = lax.psum_scatter(gathered_grad, RING, scatter_dimension=0, tiled=False)
     loads = last_loads(slots, packed_sent)
     packed_grad = sum_up(slots[0], packed_sent, send_loads(loads, *GROUP[::-1]))
-    packed_grad = after(packed_grad, gate_up_share)
-    ffn_sum = send_last(ffn_slots, after(ffn_sent, packed_grad), *GROUP)
-    gate_up_found = swap_blocks(
-        lambda k: lax.dynamic_index_in_dim(
-            after(gate_up_share, packed_grad).reshape(members, d_rows, -1), k, 0, keepdims=False
-        )
-    )
-    query_wgrad = query_wgrad.reshape(members, latent_width // members, heads * HD)
-    query_share = lax.psum_scatter(query_wgrad, RING, scatter_dimension=1, tiled=True)
     latent_in_grad = packed_grad[:, :latent_width]
     key_grad = rotate(
         packed_grad[:, latent_width : latent_width + HD], own_cos, -own_sin
@@ -580,7 +644,7 @@
     )
     spare = jnp.zeros((rows, qkv_parts.shape[1] - qkv_width), bf16)
     qkv_grad = jnp.concatenate([latent_back.astype(bf16), key_grad, value_grad, spare], axis=1)
-    attn_in_grad = by_member(dot_nt(qkv_grad, qkv_parts), members)
+    attn_in_grad = by_block(dot_nt(qkv_grad, qkv_parts), me, members)
     token_back, attn_scale_grad = normalize_back(attn_in_grad, attn_normed, attn_factor, attn_scale)
 
     small_grad = dot_tn(attn_in, qkv_grad[:, :qkv_width])
@@ -591,16 +655,31 @@
     columns = jnp.pad(columns, ((0, 128 - 3), (0, 0))).T
     small_grad = jnp.concatenate([small_grad, columns], axis=1).astype(bf16)
     small_slots = small_first(small_grad.reshape(2, 2, 2, 2, cores, d_rows, -1), cores)
-    small_pairs = small_middle(small_slots)
-    small_share = scatter_quad(small_pairs, "zl", "zh")
-    out_share, down_share, query_share = after((out_share, down_share, query_share), small_pairs)
-
-    layer_out = (residual + living * after(ffn_sum, small_slots)).astype(bf16)
+    ffn_last = send_loads(last_loads(ffn_slots, ffn_sent), *GROUP[::-1])
+    small_slots = after(small_slots, gate_up_share, ffn_last)
+    small_sent = send_first(small_slots, *GROUP)
+    loads = last_loads(small_slots, small_sent)
+    small_last = send_loads(loads, *GROUP[::-1])
+    small_pairs = pairs_along_z(sum_up(small_slots[0], small_sent, small_last).astype(bf16))
+    small_share = add_up([small_pairs[0]] + [along_z(small_pairs[code], code) for code in (1, 2, 3)])
+    gate_up_share = after(gate_up_share, small_last).reshape(members, d_rows, -1)
+    gate_up_found = swap_blocks(lambda k: lax.dynamic_index_in_dim(gate_up_share, k, 0, keepdims=False))
+    gathered_share, down_share = after((gathered_share, down_share), small_last)
+    held = out_weight.shape[0]
+    out_share = gathered_share[:held]
+
+    def query_part(k):
+        low = lax.dynamic_slice_in_dim(gathered_share, held + (k % 2) * (held // 4), held // 4, 0)
+        return lax.dynamic_slice_in_dim(low, (k // 2) * (width // 2), width // 2, 1)
+
+    query_found = swap_blocks(query_part)
+    ffn_sum = sum_up(ffn_slots[0], ffn_sent, after(ffn_last, small_slots))
+    layer_out = (residual + living * ffn_sum).astype(bf16)
     tokens_grad = after(residual_grad, small_slots) + token_back
-    found = in_order(after(gate_up_found, small_slots))
+    found = in_order(gate_up_found)
     gate_share = jnp.concatenate([part[:, :cut] for part in found], axis=1).astype(f32)
     up_share = jnp.concatenate([part[:, cut:] for part in found], axis=1).astype(f32)
-    found = in_order(swap_blocks(lambda k: lax.dynamic_index_in_dim(query_share, k, 0, keepdims=False)))
+    found = in_order(query_found)
     query_share = jnp.concatenate(found, axis=1).astype(f32)
     return (
         layer_out,

time: 625 us -> 602 us (0.963)
  matrix products: 112 us -> 101 us
  Pallas kernels: 57.2 us -> 49.6 us
    ppermute x0 -> x6, waiting for transfers between devices: none -> 27.7 us  [along_z(): return lax.ppermute(values, ('zh', 'zl'), [(i, i ^ code) for i in range(4)])]
    ppermute x45, waiting for transfers between devices: 214 us -> 198 us  [trade(): return lax.ppermute(values, axis, [(0, 1), (1, 0)])]
    ppermute x12, waiting for transfers between devices: 22.7 us -> 8.34 us  [swap_blocks(): lax.ppermute(block(me ^ code), DP, [(i, i ^ code) for i in range(4)])]
    unnamed x141 -> x157, local copies, waits for them, and re-layouts: 30.1 us -> 15.9 us
    ppermute x0 -> x6, starting transfers between devices: none -> 9.04 us  [along_z(): return lax.ppermute(values, ('zh', 'zl'), [(i, i ^ code) for i in range(4)])]
    slice x0 -> x7, local copies, waits for them, and re-layouts: none -> 8.33 us  [the longest x2 3.77 us: shards(): ffn_grad_rest = (two[:rows // 2], one[rows // 2:])]
    dynamic_update_slice x0 -> x10, local copies, waits for them, and re-layouts: none -> 8.05 us  [the longest x8 7.98 us: share_small(): lax.dynamic_update_slice(total, piece.reshape(1, 4, 1, n, c), (slot, 0, w...]
    dot_general x5 -> x3, matrix products: 41.3 us -> 33.6 us  [dot(): return jnp.dot(a, b, preferred_element_type=f32)]
  transfers between devices with their start and end apart: 66 -> 69, of which waited for: 39 -> 42; matrix products, arithmetic and copies ran while one was open for 35% -> 34% of each run, Pallas kernels for 9% -> 8%
where the time goes in v4:
time: 602 us; the launch traced here: 597 us
  waiting for transfers between devices  237 us (39%)
  matrix products  101 us (17%)
  other arithmetic  70.2 us (12%)
  starting transfers between devices  66.7 us (11%)
  local copies, waits for them, and re-layouts  55.5 us (9%)
  Pallas kernels  49.6 us (8%)
  between operations  17.8 us (3%)
    ppermute x45, waiting for transfers between devices, trade(): return lax.ppermute(values, axis, [(0, 1), (1, 0)])  198 us
    ppermute x45, starting transfers between devices, trade(): return lax.ppermute(values, axis, [(0, 1), (1, 0)])  42 us
    dot_general x3, matrix products, dot_nt(): lax.dot_general(a, b, (((1,), (1,)), ((), ())), preferred_element_type=f32)  38 us
    dot_general x3, matrix products, dot(): return jnp.dot(a, b, preferred_element_type=f32)  33.6 us
    pallas_call x1, Pallas kernels, attend_back(): pl.pallas_call(functools.partial(attend_back_kernel, members, heads), gri...  33.1 us
    dot_general x3, matrix products, dot_tn(): lax.dot_general(a, b, (((0,), (0,)), ((), ())), preferred_element_type=f32)  29.4 us
    ppermute x6, waiting for transfers between devices, along_z(): return lax.ppermute(values, ('zh', 'zl'), [(i, i ^ code) for i in range(4)])  27.7 us
    pallas_call x1, Pallas kernels, attend(): pl.pallas_call(functools.partial(attend_kernel, members, heads), grid_spe...  16.5 us
  transfers between devices with their start and end apart: 69, of which 42 were waited for; matrix products, arithmetic and copies ran while one was open for 34% of the time, Pallas kernels for 8%

profile of v4, /device:TPU:0, one launch (start us, length us, event | category | flops | bytes accessed | tf_op | source)
XLA Modules:
  0.0 597.3 jit_solution(2541059102865936795)
XLA Ops:
  28.1 11.4 %collective-permute-done.1 = bf16[64,1664]{1,0:T(8,128)(2,1)S(1)} collective-permute-done((bf16[64,1664]{1,0:T(8,128)(2,1)S(1)}, bf16[64,1664]{1,0:T(8,128)(2,1)S(1)}, u32[]{:S(2)}, u32[]{:S(2)}) %collective-permute-start.1) | collective-permute-done | bytes 213024 | tf_op jit(solution)/shard_map/ppermute | solution.py:203
  53.5 7.5 %collective-permute-done.6 = bf16[256,1664]{1,0:T(8,128)(2,1)S(1)} collective-permute-done((bf16[256,1664]{1,0:T(8,128)(2,1)S(1)}, bf16[256,1664]{1,0:T(8,128)(2,1)S(1)}, u32[]{:S(2)}, u32[]{:S(2)}) %collective-permute-start.6) | collective-permute-done | bytes 852000 | tf_op jit(solution)/shard_map/ppermute | solution.py:97
  61.0 8.0 %collective-permute-done.4 = bf16[256,1664]{1,0:T(8,128)(2,1)S(1)} collective-permute-done((bf16[256,1664]{1,0:T(8,128)(2,1)S(1)}, bf16[256,1664]{1,0:T(8,128)(2,1)S(1)}, u32[]{:S(2)}, u32[]{:S(2)}) %collective-permute-start.4) | collective-permute-done | bytes 852000 | tf_op jit(solution)/shard_map/ppermute | solution.py:97
  102.2 14.5 %collective-permute-done.11 = bf16[256,1536]{1,0:T(8,128)(2,1)S(1)} collective-permute-done((bf16[256,1536]{1,0:T(8,128)(2,1)S(1)}, bf16[256,1536]{1,0:T(8,128)(2,1)S(1)}, u32[]{:S(2)}, u32[]{:S(2)}) %collective-permute-start.11) | collective-permute-done | bytes 786464 | tf_op jit(solution)/shard_map/ppermute | solution.py:97
  118.7 9.1 %collective-permute-done.13 = bf16[128,1536]{1,0:T(8,128)(2,1)S(1)} collective-permute-done((bf16[128,1536]{1,0:T(8,128)(2,1)S(1)}, bf16[128,1536]{1,0:T(8,128)(2,1)S(1)}, u32[]{:S(2)}, u32[]{:S(2)}) %collective-permute-start.13) | collective-permute-done | bytes 393248 | tf_op jit(solution)/shard_map/ppermute | solution.py:97
  131.3 16.5 %shard_map.237 = (bf16[1024,1024]{1,0:T(8,128)(2,1)S(1)}, bf16[1024,1024]{1,0:T(8,128)(2,1)S(1)}, bf16[1024,2048]{1,0:T(8,128)(2,1)S(1)}) custom-call(s32[4,2]{1,0:T(4,128)S(1)} %copy.42.lengths_ref, bf16[1024,1536]{1,0:T(8,128)(2,1)S(1)} %constant_dynamic-update-slice_fusion.2.latent_ref.key_ref.value_ref, bf16[8,192,2048]{2,1,0:T(8,128)(2,1)} %bitcast.186, ...), custom_call_target="tpu_custom_call" | custom-call | flops 7516192768 | bytes 15728640 | tf_op jit(solution)/shard_map/pallas_call | solution.py:333
  164.6 11.7 %collective-permute-done.20 = bf16[256,2048]{1,0:T(8,128)(2,1)S(1)} collective-permute-done((bf16[256,2048]{1,0:T(8,128)(2,1)S(1)}, bf16[256,2048]{1,0:T(8,128)(2,1)S(1)}, u32[]{:S(2)}, u32[]{:S(2)}) %collective-permute-start.20) | collective-permute-done | bytes 1048608 | tf_op jit(solution)/shard_map/ppermute | solution.py:97
  181.0 8.6 %collective-permute-done.22 = bf16[128,2048]{1,0:T(8,128)(2,1)S(1)} collective-permute-done((bf16[128,2048]{1,0:T(8,128)(2,1)S(1)}, bf16[128,2048]{1,0:T(8,128)(2,1)S(1)}, u32[]{:S(2)}, u32[]{:S(2)}) %collective-permute-start.22) | collective-permute-done | bytes 524320 | tf_op jit(solution)/shard_map/ppermute | solution.py:97
  193.1 20.1 %collective-permute-done.25 = bf16[256,2048]{1,0:T(8,128)(2,1)S(1)} collective-permute-done((bf16[256,2048]{1,0:T(8,128)(2,1)S(1)}, bf16[256,2048]{1,0:T(8,128)(2,1)S(1)}, u32[]{:S(2)}, u32[]{:S(2)}) %collective-permute-start.25) | collective-permute-done | bytes 1048608 | tf_op jit(solution)/shard_map/ppermute | solution.py:97
  230.1 17.5 %fusion.101 = f32[1024,2816]{1,0:T(8,128)S(1)} fusion(bf16[1024,2048]{1,0:T(8,128)(2,1)} %copy-done.50, bf16[2048,2816]{1,0:T(8,128)(2,1)} %bitcast.184), kind=kOutput, calls=%fused_computation.313 | convolution fusion | flops 11811160064 | bytes 27262976 | tf_op jit(solution)/shard_map/dot_general | solution.py:81
  254.7 8.1 %convolution_convert_fusion.2 = bf16[1408,2048]{1,0:T(8,128)(2,1)} fusion(bf16[1024,1408]{1,0:T(8,128)(2,1)S(1)} %multiply_convert_fusion.2, bf16[1024,2048]{1,0:T(8,128)(2,1)S(1)} %constant_dynamic-update-slice_fusion.22), kind=kOutput, calls=%fused_computation.4 | convolution fusion | flops 5908463616 | bytes 12845056 | tf_op jit(solution)/shard_map/dot_general | solution.py:89
  266.2 15.3 %multiply_convert_fusion.1 = (bf16[1024,1408]{1,0:T(8,128)(2,1)S(1)}, bf16[1024,1408]{1,0:T(8,128)(2,1)}) fusion(f32[1024,2816]{1,0:T(8,128)} %copy-done.14, bf16[1024,2048]{1,0:T(8,128)(2,1)} %copy-done.27, bf16[1408,2048]{1,0:T(8,128)(2,1)} %all-gather.7.cloned.1.call-done), kind=kOutput, calls=%fused_computation.11 | convolution fusion | flops 5924323328 | bytes 27262976 | tf_op jit(solution)/shard_map/dot_general | solution.py:85
  281.5 17.4 %convolution_convert_fusion.3 = bf16[1024,2048]{1,0:T(8,128)(2,1)S(1)} fusion(bf16[2048,2816]{1,0:T(8,128)(2,1)} %bitcast.185, bf16[1024,1408]{1,0:T(8,128)(2,1)} %get-tuple-element.113, bf16[1024,1408]{1,0:T(8,128)(2,1)S(1)} %get-tuple-element.112), kind=kOutput, calls=%fused_computation.16 | convolution fusion | flops 11824791552 | bytes 21495808 | tf_op jit(solution)/shard_map/dot_general | solution.py:85
  305.4 11.0 %convolution_convert_fusion.4 = bf16[1024,2048]{1,0:T(8,128)(2,1)} fusion(bf16[1024,1408]{1,0:T(8,128)(2,1)S(1)} %copy-done.35, bf16[1408,2048]{1,0:T(8,128)(2,1)} %all-gather.7.cloned.1.call-done), kind=kOutput, calls=%fused_computation.17 | convolution fusion | flops 5907677184 | bytes 12845056 | tf_op jit(solution)/shard_map/dot_general | solution.py:81
  318.7 8.3 %collective-permute-done.33 = bf16[256,2048]{1,0:T(8,128)(2,1)S(1)} collective-permute-done((bf16[256,2048]{1,0:T(8,128)(2,1)}, bf16[256,2048]{1,0:T(8,128)(2,1)S(1)}, u32[]{:S(2)}, u32[]{:S(2)}) %collective-permute-start.33) | collective-permute-done | bytes 1048608 | tf_op jit(solution)/shard_map/ppermute | solution.py:97
  329.3 18.0 %convolution_convert_fusion = bf16[2048,2816]{1,0:T(8,128)(2,1)} fusion(bf16[1024,2048]{1,0:T(8,128)(2,1)} %copy-done.50, bf16[1024,2816]{1,0:T(8,128)(2,1)S(1)} %pad_maximum_fusion), kind=kOutput, calls=%fused_computation | convolution fusion | flops 11816927232 | bytes 21495808 | tf_op jit(solution)/shard_map/dot_general | solution.py:89
  352.7 9.4 %collective-permute-done.35 = bf16[128,2048]{1,0:T(8,128)(2,1)S(1)} collective-permute-done((bf16[128,2048]{1,0:T(8,128)(2,1)S(1)}, bf16[128,2048]{1,0:T(8,128)(2,1)S(1)}, u32[]{:S(2)}, u32[]{:S(2)}) %collective-permute-start.35) | collective-permute-done | bytes 524320 | tf_op jit(solution)/shard_map/ppermute | solution.py:97
  371.2 20.0 %collective-permute-done.38 = bf16[256,2048]{1,0:T(8,128)(2,1)S(1)} collective-permute-done((bf16[256,2048]{1,0:T(8,128)(2,1)S(1)}, bf16[256,2048]{1,0:T(8,128)(2,1)S(1)}, u32[]{:S(2)}, u32[]{:S(2)}) %collective-permute-start.38) | collective-permute-done | bytes 1048608 | tf_op jit(solution)/shard_map/ppermute | solution.py:97
  394.5 8.6 %collective-permute-done.39 = bf16[128,2048]{1,0:T(8,128)(2,1)S(1)} collective-permute-done((bf16[128,2048]{1,0:T(8,128)(2,1)S(1)}, bf16[128,2048]{1,0:T(8,128)(2,1)S(1)}, u32[]{:S(2)}, u32[]{:S(2)}) %collective-permute-start.39) | collective-permute-done | bytes 524320 | tf_op jit(solution)/shard_map/ppermute | solution.py:97
  405.2 33.1 %shard_map.238 = (bf16[1024,1536]{1,0:T(8,128)(2,1)}, bf16[8,192,2048]{2,1,0:T(8,128)(2,1)}) custom-call(s32[4,2]{1,0:T(4,128)} %copy-done.3, bf16[1024,2048]{1,0:T(8,128)(2,1)} %copy-done.51, bf16[8,192,2048]{2,1,0:T(8,128)(2,1)} %bitcast.188, bf16[8,192,2048]{2,1,0:T(8,128)(2,1)} %bitcast.189, bf16[1024,1024]{1,0:T(8,128)(2,1)} %copy-done.4, ...), custom_call_target="tpu_custom_call" | custom-call | flops 15569256448 | bytes 16777216 | tf_op jit(solution)/shard_map/pallas_call | solution.py:439
  444.5 13.6 %collective-permute-done.47 = bf16[256,1536]{1,0:T(8,128)(2,1)S(1)} collective-permute-done((bf16[256,1536]{1,0:T(8,128)(2,1)}, bf16[256,1536]{1,0:T(8,128)(2,1)S(1)}, u32[]{:S(2)}, u32[]{:S(2)}) %collective-permute-start.47) | collective-permute-done | bytes 786464 | tf_op jit(solution)/shard_map/ppermute | solution.py:97
  507.6 7.2 %collective-permute-done.44 = bf16[128,2048]{1,0:T(8,128)(2,1)} collective-permute-done((bf16[128,2048]{1,0:T(8,128)(2,1)S(1)}, bf16[128,2048]{1,0:T(8,128)(2,1)}, u32[]{:S(2)}, u32[]{:S(2)}) %collective-permute-start.44) | collective-permute-done | bytes 524320 | tf_op jit(solution)/shard_map/ppermute | solution.py:97
  527.7 12.0 %collective-permute-done.52 = bf16[256,1664]{1,0:T(8,128)(2,1)S(1)} collective-permute-done((bf16[256,1664]{1,0:T(8,128)(2,1)S(1)}, bf16[256,1664]{1,0:T(8,128)(2,1)S(1)}, u32[]{:S(2)}, u32[]{:S(2)}) %collective-permute-start.52) | collective-permute-done | bytes 852000 | tf_op jit(solution)/shard_map/ppermute | solution.py:97
  564.8 6.9 %collective-permute-done.55 = bf16[64,1664]{1,0:T(8,128)(2,1)S(1)} collective-permute-done((bf16[64,1664]{1,0:T(8,128)(2,1)S(1)}, bf16[64,1664]{1,0:T(8,128)(2,1)S(1)}, u32[]{:S(2)}, u32[]{:S(2)}) %collective-permute-start.55) | collective-permute-done | bytes 213024 | tf_op jit(solution)/shard_map/ppermute | solution.py:203
  (444 shorter events, 265.7 us)
Async XLA Ops:
  7.3 124.1 %all-gather.9.cloned.1.call-start = ((), (), s32[]{:S(2)}) async-start(), calls=%async_computation.8 | async-start | bytes 7077888 | tf_op jit(solution)/shard_map/all_gather | solution.py:533
  19.5 210.5 %all-gather.5.cloned.1.call-start = ((), (), s32[]{:S(2)}) async-start(), calls=%async_computation.3 | async-start | bytes 12976128 | tf_op jit(solution)/shard_map/all_gather | solution.py:566
  24.4 25.9 %collective-permute-start.29 = (bf16[64,2816]{1,0:T(8,128)(2,1)S(1)}, bf16[64,2816]{1,0:T(8,128)(2,1)}, u32[]{:S(2)}, u32[]{:S(2)}) collective-permute-start(bf16[64,2816]{1,0:T(8,128)(2,1)S(1)} %pad_maximum_fusion.22), channel_id=1, source_target_pairs={{0,16},{8,24},{16,0},{24,8},{1,17},{9,25},{17,1},{25,9},{2,18},{10... | collective-permute-start | bytes 1081352 | tf_op jit(solution)/shard_map/ppermute | solution.py:226
  26.0 24.3 %collective-permute-start.30 = (bf16[64,2816]{1,0:T(8,128)(2,1)}, bf16[64,2816]{1,0:T(8,128)(2,1)}, u32[]{:S(2)}, u32[]{:S(2)}) collective-permute-start(bf16[64,2816]{1,0:T(8,128)(2,1)} %pad_maximum_fusion.23), channel_id=1, source_target_pairs={{0,24},{8,16},{16,8},{24,0},{1,25},{9,17},{17,9},{25,1},{2,26},{10... | collective-permute-start | bytes 1081352 | tf_op jit(solution)/shard_map/ppermute | solution.py:226
  44.9 24.2 %collective-permute-start.4 = (bf16[256,1664]{1,0:T(8,128)(2,1)S(1)}, bf16[256,1664]{1,0:T(8,128)(2,1)S(1)}, u32[]{:S(2)}, u32[]{:S(2)}) collective-permute-start(bf16[256,1664]{1,0:T(8,128)(2,1)S(1)} %pad_maximum_fusion.14), channel_id=1, source_target_pairs={{0,8},{8,0},{1,9},{9,1},{2,10},{10,2},{3,11},{11,3},{4,12},{12,4},... | collective-permute-start | bytes 2555912 | tf_op jit(solution)/shard_map/ppermute | solution.py:97
  82.4 183.7 %all-gather.7.cloned.1.call-start = ((), (), s32[]{:S(2)}) async-start(), calls=%async_computation.4 | async-start | bytes 6488064 | tf_op jit(solution)/shard_map/all_gather | solution.py:541
  127.8 24.3 %collective-permute-start.19 = (bf16[256,2048]{1,0:T(8,128)(2,1)}, bf16[256,2048]{1,0:T(8,128)(2,1)}, u32[]{:S(2)}, u32[]{:S(2)}) collective-permute-start(bf16[256,2048]{1,0:T(8,128)(2,1)} %fusion.8), channel_id=1, source_target_pairs={{0,16},{16,0},{1,17},{17,1},{2,18},{18,2},{3,19},{19,3},{4,20},{20... | collective-permute-start | bytes 3145736 | tf_op jit(solution)/shard_map/ppermute | solution.py:97
  129.6 23.8 %collective-permute-start.18 = (bf16[256,2048]{1,0:T(8,128)(2,1)}, bf16[256,2048]{1,0:T(8,128)(2,1)}, u32[]{:S(2)}, u32[]{:S(2)}) collective-permute-start(bf16[256,2048]{1,0:T(8,128)(2,1)} %fusion.8), channel_id=1, source_target_pairs={{0,8},{8,0},{1,9},{9,1},{2,10},{10,2},{3,11},{11,3},{4,12},{12,4},... | collective-permute-start | bytes 3145736 | tf_op jit(solution)/shard_map/ppermute | solution.py:97
  153.7 22.6 %collective-permute-start.20 = (bf16[256,2048]{1,0:T(8,128)(2,1)S(1)}, bf16[256,2048]{1,0:T(8,128)(2,1)S(1)}, u32[]{:S(2)}, u32[]{:S(2)}) collective-permute-start(bf16[256,2048]{1,0:T(8,128)(2,1)S(1)} %pad_maximum_fusion.7), channel_id=1, source_target_pairs={{0,8},{8,0},{1,9},{9,1},{2,10},{10,2},{3,11},{11,3},{4,12},{12,4},... | collective-permute-start | bytes 3145736 | tf_op jit(solution)/shard_map/ppermute | solution.py:97
  155.6 23.0 %collective-permute-start.21 = (bf16[256,2048]{1,0:T(8,128)(2,1)}, bf16[256,2048]{1,0:T(8,128)(2,1)S(1)}, u32[]{:S(2)}, u32[]{:S(2)}) collective-permute-start(bf16[256,2048]{1,0:T(8,128)(2,1)} %pad_maximum_fusion.8), channel_id=1, source_target_pairs={{0,16},{16,0},{1,17},{17,1},{2,18},{18,2},{3,19},{19,3},{4,20},{20... | collective-permute-start | bytes 3145736 | tf_op jit(solution)/shard_map/ppermute | solution.py:97
  156.5 211.7 %reduce-scatter.4.cloned.1.call-start = ((), (), s32[]{:S(2)}) async-start(), calls=%async_computation.5 | async-start | bytes 6488064 | tf_op jit(solution)/shard_map/reduce_scatter | solution.py:593
  190.9 22.3 %collective-permute-start.25 = (bf16[256,2048]{1,0:T(8,128)(2,1)S(1)}, bf16[256,2048]{1,0:T(8,128)(2,1)S(1)}, u32[]{:S(2)}, u32[]{:S(2)}) collective-permute-start(bf16[256,2048]{1,0:T(8,128)(2,1)S(1)} %get-tuple-element.109), channel_id=1, source_target_pairs={{0,16},{16,0},{1,17},{17,1},{2,18},{18,2},{3,19},{19,3},{4,20},{20... | collective-permute-start | bytes 3145736 | tf_op jit(solution)/shard_map/ppermute | solution.py:97
  192.0 22.9 %collective-permute-start.24 = (bf16[256,2048]{1,0:T(8,128)(2,1)S(1)}, bf16[256,2048]{1,0:T(8,128)(2,1)S(1)}, u32[]{:S(2)}, u32[]{:S(2)}) collective-permute-start(bf16[256,2048]{1,0:T(8,128)(2,1)S(1)} %get-tuple-element.109), channel_id=1, source_target_pairs={{0,8},{8,0},{1,9},{9,1},{2,10},{10,2},{3,11},{11,3},{4,12},{12,4},... | collective-permute-start | bytes 3145736 | tf_op jit(solution)/shard_map/ppermute | solution.py:97
  262.8 253.0 %reduce-scatter.6.cloned.1.call-start = ((), (), s32[]{:S(2)}) async-start(), calls=%async_computation.6 | async-start | bytes 12976128 | tf_op jit(solution)/shard_map/reduce_scatter | solution.py:614
  301.4 25.5 %collective-permute-start.33 = (bf16[256,2048]{1,0:T(8,128)(2,1)}, bf16[256,2048]{1,0:T(8,128)(2,1)S(1)}, u32[]{:S(2)}, u32[]{:S(2)}) collective-permute-start(bf16[256,2048]{1,0:T(8,128)(2,1)} %pad_maximum_fusion.9), channel_id=1, source_target_pairs={{0,8},{8,0},{1,9},{9,1},{2,10},{10,2},{3,11},{11,3},{4,12},{12,4},... | collective-permute-start | bytes 3145736 | tf_op jit(solution)/shard_map/ppermute | solution.py:97
  303.9 25.3 %collective-permute-start.34 = (bf16[256,2048]{1,0:T(8,128)(2,1)}, bf16[256,2048]{1,0:T(8,128)(2,1)}, u32[]{:S(2)}, u32[]{:S(2)}) collective-permute-start(bf16[256,2048]{1,0:T(8,128)(2,1)} %pad_maximum_fusion.10), channel_id=1, source_target_pairs={{0,16},{16,0},{1,17},{17,1},{2,18},{18,2},{3,19},{19,3},{4,20},{20... | collective-permute-start | bytes 3145736 | tf_op jit(solution)/shard_map/ppermute | solution.py:97
  347.3 226.6 %reduce-scatter.8.cloned.1.call-start = ((), (), s32[]{:S(2)}) async-start(), calls=%async_computation.7 | async-start | bytes 7077888 | tf_op jit(solution)/shard_map/reduce_scatter | solution.py:634
  368.2 23.0 %collective-permute-start.38 = (bf16[256,2048]{1,0:T(8,128)(2,1)S(1)}, bf16[256,2048]{1,0:T(8,128)(2,1)S(1)}, u32[]{:S(2)}, u32[]{:S(2)}) collective-permute-start(bf16[256,2048]{1,0:T(8,128)(2,1)S(1)} %get-tuple-element.67), channel_id=1, source_target_pairs={{0,16},{16,0},{1,17},{17,1},{2,18},{18,2},{3,19},{19,3},{4,20},{20... | collective-permute-start | bytes 3145736 | tf_op jit(solution)/shard_map/ppermute | solution.py:97
  368.7 23.2 %collective-permute-start.37 = (bf16[256,2048]{1,0:T(8,128)(2,1)S(1)}, bf16[256,2048]{1,0:T(8,128)(2,1)S(1)}, u32[]{:S(2)}, u32[]{:S(2)}) collective-permute-start(bf16[256,2048]{1,0:T(8,128)(2,1)S(1)} %get-tuple-element.67), channel_id=1, source_target_pairs={{0,8},{8,0},{1,9},{9,1},{2,10},{10,2},{3,11},{11,3},{4,12},{12,4},... | collective-permute-start | bytes 3145736 | tf_op jit(solution)/shard_map/ppermute | solution.py:97
  403.2 35.1 %collective-permute-start.41 = (bf16[256,2048]{1,0:T(8,128)(2,1)S(1)}, bf16[256,2048]{1,0:T(8,128)(2,1)S(1)}, u32[]{:S(2)}, u32[]{:S(2)}) collective-permute-start(bf16[256,2048]{1,0:T(8,128)(2,1)S(1)} %pad_maximum_fusion.11), channel_id=1, source_target_pairs={{0,8},{8,0},{1,9},{9,1},{2,10},{10,2},{3,11},{11,3},{4,12},{12,4},... | collective-permute-start | bytes 3145736 | tf_op jit(solution)/shard_map/ppermute | solution.py:97
  404.3 34.0 %collective-permute-start.43 = (bf16[256,2048]{1,0:T(8,128)(2,1)S(1)}, bf16[256,2048]{1,0:T(8,128)(2,1)S(1)}, u32[]{:S(2)}, u32[]{:S(2)}) collective-permute-start(bf16[256,2048]{1,0:T(8,128)(2,1)S(1)} %pad_maximum_fusion.12), channel_id=1, source_target_pairs={{0,16},{16,0},{1,17},{17,1},{2,18},{18,2},{3,19},{19,3},{4,20},{20... | collective-permute-start | bytes 3145736 | tf_op jit(solution)/shard_map/ppermute | solution.py:97
  555.9 29.4 %collective-permute-start.62 = (bf16[64,2816]{1,0:T(8,128)(2,1)S(1)}, bf16[64,2816]{1,0:T(8,128)(2,1)S(1)}, u32[]{:S(2)}, u32[]{:S(2)}) collective-permute-start(bf16[64,2816]{1,0:T(8,128)(2,1)S(1)} %get-tuple-element.165), channel_id=1, source_target_pairs={{0,24},{8,16},{16,8},{24,0},{1,25},{9,17},{17,9},{25,1},{2,26},{10... | collective-permute-start | bytes 1081352 | tf_op jit(solution)/shard_map/ppermute | solution.py:226
  557.4 27.9 %collective-permute-start.61 = (bf16[64,2816]{1,0:T(8,128)(2,1)S(1)}, bf16[64,2816]{1,0:T(8,128)(2,1)S(1)}, u32[]{:S(2)}, u32[]{:S(2)}) collective-permute-start(bf16[64,2816]{1,0:T(8,128)(2,1)S(1)} %get-tuple-element.166), channel_id=1, source_target_pairs={{0,16},{8,24},{16,0},{24,8},{1,17},{9,25},{17,1},{25,9},{2,18},{10... | collective-permute-start | bytes 1081352 | tf_op jit(solution)/shard_map/ppermute | solution.py:226
  560.1 25.2 %collective-permute-start.60 = (bf16[64,2816]{1,0:T(8,128)(2,1)S(1)}, bf16[64,2816]{1,0:T(8,128)(2,1)}, u32[]{:S(2)}, u32[]{:S(2)}) collective-permute-start(bf16[64,2816]{1,0:T(8,128)(2,1)S(1)} %get-tuple-element.167), channel_id=1, source_target_pairs={{0,8},{8,0},{16,24},{24,16},{1,9},{9,1},{17,25},{25,17},{2,10},{10... | collective-permute-start | bytes 1081352 | tf_op jit(solution)/shard_map/ppermute | solution.py:226
  (117 other events, 1067.0 us)
Sparse Core Ops, SparseCore 0:
  19.7 73.7 all-gather.8
  95.6 110.1 all-gather.4
  207.5 58.6 all-gather.6
  268.3 74.8 reduce-scatter.3
  347.4 123.4 reduce-scatter.5
  473.1 68.1 reduce-scatter.7

commit v5 on v4

--- a/solution.py
+++ b/solution.py
@@ -164,24 +164,19 @@
     return scatter_quad(slots, first, second)
 
 
-def split_cores(values, cores):
-    if cores != 2:
-        return lax.psum_scatter(values, "r", scatter_dimension=4, tiled=False), None
-    core = lax.axis_index("r")
-    mine = lax.dynamic_index_in_dim(values, core, 4, keepdims=False)
-    theirs = lax.dynamic_index_in_dim(values, 1 - core, 4, keepdims=False)
-    return mine, trade(theirs.reshape(-1, values.shape[-1]), "r").reshape(mine.shape)
-
-
 def join_cores(mine, theirs):
     if theirs is None:
         return mine
     return (mine.astype(f32) + theirs.astype(f32)).astype(bf16)
 
 
-def small_first(values, cores):
-    n, c = values.shape[5:]
-    total = join_cores(*split_cores(values, cores)).reshape(4, 4 * n, c)
+def small_first(values, cores, n):
+    if cores == 2:
+        total = join_cores(values[0], trade(values[1], "r"))
+    else:
+        total = values[0].reshape(16, cores, n, -1)
+        total = lax.psum_scatter(total, "r", scatter_dimension=1, tiled=False)
+    total = total.reshape(4, 4 * n, -1)
     me = lax.axis_index(DP)
     return [lax.dynamic_index_in_dim(total, me ^ code, 0, keepdims=False) for code in range(4)]
 
@@ -362,28 +357,18 @@
     weight_ref,
     out_ref,
     query_ref,
-    latent_ref,
     key_ref,
     value_ref,
-    mix_ref,
     packed_ref,
-    gathered_grad_ref,
-    grads_ref,
-    mixes_ref,
-    latents_ref,
     query_grads_ref,
     cos_ref,
     sin_ref,
 ):
-    member = pl.program_id(0)
     fill_angles(lengths_ref, cos_ref, sin_ref)
-    latent_width = latent_ref.shape[1]
+    latent_width = packed_ref.shape[1] - 2 * HD
     step = latent_width // members
     out_full = out_ref[...].reshape(heads * HD, -1)
     scale = 1.0 / math.sqrt(HD)
-    grads_ref[member] = grad_ref[...]
-    mixes_ref[member] = mix_ref[...]
-    latents_ref[member] = latent_ref[...]
     key_rot, value_low = key_ref[...], value_ref[...]
     mixture_grads = dot_nt(grad_ref[...], out_full).astype(bf16)
     key_grad = jnp.zeros(key_rot.shape, f32)
@@ -396,45 +381,59 @@
         row_dot = jnp.sum(probs * probs_grad, axis=-1, keepdims=True)
         score_grad = (probs * (probs_grad - row_dot)).astype(bf16)
         query_rot_grad = dot(score_grad, key_rot) * scale
-        query_grads_ref[member, :, columns] = turn(query_rot_grad, cos_ref[...], -sin_ref[...]).astype(bf16)
+        query_grads_ref[:, columns] = turn(query_rot_grad, cos_ref[...], -sin_ref[...]).astype(bf16)
         key_grad += dot_tn(score_grad, query_rot)
         value_grad += dot_tn(probs.astype(bf16), mixture_grad)
     for k in range(members):
-        latent_part = dot_nt(query_grads_ref[member], query_block(weight_ref, k, heads))
+        latent_part = dot_nt(query_grads_ref[...], query_block(weight_ref, k, heads))
         packed_ref[:, k * step : (k + 1) * step] = latent_part.astype(bf16)
     packed_ref[:, latent_width : latent_width + HD] = (key_grad * scale).astype(bf16)
     packed_ref[:, latent_width + HD :] = value_grad.astype(bf16)
 
-    @pl.when(member == members - 1)
-    def _():
-        rows = members * grad_ref.shape[0]
-        grads = grads_ref[...].reshape(rows, -1)
-        mixes = mixes_ref[...].reshape(rows, -1)
-        latents = latents_ref[...].reshape(rows, -1)
-        query_grads = query_grads_ref[...].reshape(rows, -1)
-        ring, held, width = gathered_grad_ref.shape
-        held = held // 3
-        count = HD // (2 * held)
-        for head in range(heads):
-            columns = slice(head * HD, (head + 1) * HD)
-            part = dot_tn(mixes[:, columns], grads).astype(bf16)
-            gathered_grad_ref[head * count : (head + 1) * count, : 2 * held] = part.reshape(count, 2 * held, width)
-        for k in range(members):
-            part = dot_tn(latents[:, k * step : (k + 1) * step], query_grads).astype(bf16)
-            high, low = divmod(k, 2)
-            place = slice(2 * held + low * held // 2, 2 * held + (low + 1) * held // 2)
-            columns = slice(high * width // 2, (high + 1) * width // 2)
-            gathered_grad_ref[:, place, columns] = part.reshape(ring, held // 2, width // 2)
-
-
-def attend_back(lengths, attn_grad, gathered, query_rot, mixture, packed, rows, heads):
+
+def gathered_grad_kernel(members, heads, grads_ref, mixes_ref, latents_ref, query_grads_ref, gathered_grad_ref):
+    ring, held, width = gathered_grad_ref.shape
+    held = held // 3
+    count, step = HD // (2 * held), latents_ref.shape[1] // members
+    for head in range(heads):
+        columns = slice(head * HD, (head + 1) * HD)
+        part = dot_tn(mixes_ref[:, columns], grads_ref[...]).astype(bf16)
+        gathered_grad_ref[head * count : (head + 1) * count, : 2 * held] = part.reshape(count, 2 * held, width)
+    for k in range(members):
+        part = dot_tn(latents_ref[:, k * step : (k + 1) * step], query_grads_ref[...]).astype(bf16)
+        high, low = divmod(k, 2)
+        place = slice(2 * held + low * held // 2, 2 * held + (low + 1) * held // 2)
+        columns = slice(high * width // 2, (high + 1) * width // 2)
+        gathered_grad_ref[:, place, columns] = part.reshape(ring, held // 2, width // 2)
+
+
+def gathered_grads(attn_grad, mixture, packed, query_grads, shape, heads):
+    total, width = attn_grad.shape
+    members, latent_width = 4, packed.shape[1] - 2 * HD
+
+    def whole(columns):
+        return pl.BlockSpec((total, columns), lambda i: (0, 0))
+
+    return pl.pallas_call(
+        functools.partial(gathered_grad_kernel, members, heads),
+        grid=(1,),
+        in_specs=[whole(width), whole(heads * HD), whole(latent_width), whole(heads * HD)],
+        out_specs=pl.BlockSpec(shape, lambda i: (0, 0, 0)),
+        out_shape=jax.ShapeDtypeStruct(shape, bf16),
+        compiler_params=pltpu.CompilerParams(vmem_limit_bytes=52 * 2**20),
+        cost_estimate=pl.CostEstimate(
+            flops=2 * total * heads * HD * (width + latent_width),
+            bytes_accessed=16 * 2**20,
+            transcendentals=0,
+        ),
+    )(attn_grad, mixture, packed, query_grads)
+
+
+def attend_back(lengths, attn_grad, gathered, query_rot, packed, rows, heads):
     total, width = attn_grad.shape
     latent_width = packed.shape[1] - 2 * HD
     last, members = latent_width // HD, total // rows
     block = pl.BlockSpec((rows, heads * HD), lambda m, s: (m, 0))
-
-    def kept(columns):
-        return pltpu.VMEM((members, rows, columns), bf16)
 
     return pl.pallas_call(
         functools.partial(attend_back_kernel, members, heads),
@@ -445,35 +444,129 @@
                 pl.BlockSpec((rows, width), lambda m, s: (m, 0)),
                 *packed_specs(gathered),
                 block,
-                pl.BlockSpec((rows, latent_width), lambda m, s: (m, 0)),
                 pl.BlockSpec((rows, HD), lambda m, s: (m, last)),
                 pl.BlockSpec((rows, HD), lambda m, s: (m, last + 1)),
-                block,
             ],
             out_specs=[
                 pl.BlockSpec((rows, packed.shape[1]), lambda m, s: (m, 0)),
-                pl.BlockSpec(gathered.shape, lambda m, s: (0, 0, 0)),
+                block,
             ],
             scratch_shapes=[
-                kept(width),
-                kept(heads * HD),
-                kept(latent_width),
-                kept(heads * HD),
                 pltpu.VMEM((rows, HD // 2), f32),
                 pltpu.VMEM((rows, HD // 2), f32),
             ],
         ),
         out_shape=[
             jax.ShapeDtypeStruct(packed.shape, bf16),
-            jax.ShapeDtypeStruct(gathered.shape, bf16),
+            jax.ShapeDtypeStruct((total, heads * HD), bf16),
         ],
         compiler_params=pltpu.CompilerParams(vmem_limit_bytes=56 * 2**20),
         cost_estimate=pl.CostEstimate(
-            flops=2 * total * heads * HD * (2 * width + 2 * latent_width + 5 * rows),
+            flops=2 * total * heads * HD * (width + latent_width + 5 * rows),
             bytes_accessed=total * heads * HD * 8 + total * width * 4,
             transcendentals=total * heads * rows,
         ),
-    )(lengths, attn_grad, gathered, gathered, query_rot, packed, packed, packed, mixture)
+    )(lengths, attn_grad, gathered, gathered, query_rot, packed, packed)
+
+
+def finish_kernel(
+    devices,
+    held,
+    cores,
+    me_ref,
+    own_ref,
+    first_ref,
+    second_ref,
+    last_a_ref,
+    last_b_ref,
+    latent_ref,
+    latent_scale_ref,
+    cos_ref,
+    sin_ref,
+    attn_in_ref,
+    tokens_ref,
+    attn_scale_ref,
+    parts_ref,
+    residual_grad_ref,
+    mlp_gain_ref,
+    *results,
+):
+    small_refs, (tokens_grad_ref, qkv_ref, back_ref) = results[:-3], results[-3:]
+    rows, latent_width = latent_ref.shape
+    width = tokens_ref.shape[1]
+    qkv_width = qkv_ref.shape[1]
+    half, members = rows // 2, 4
+    step = width // members
+    top = own_ref[:half].astype(f32) + first_ref[:half].astype(f32) + last_a_ref[...].astype(f32)
+    low = own_ref[half:].astype(f32) + second_ref[:half].astype(f32) + last_b_ref[...].astype(f32)
+    grads = jnp.concatenate([top, low], axis=0)
+    _, normed, factor = normalize(latent_ref[...], 1.0)
+    upstream = grads[:, :latent_width]
+    latent_gain = jnp.sum(upstream * normed, axis=0, keepdims=True)
+    scaled = upstream * latent_scale_ref[...]
+    inner = jnp.mean(scaled * normed, axis=-1, keepdims=True)
+    qkv_ref[:, :latent_width] = (factor * (scaled - normed * inner)).astype(bf16)
+    key_grad = turn(grads[:, latent_width : latent_width + HD], cos_ref[...], -sin_ref[...])
+    qkv_ref[:, latent_width : latent_width + HD] = key_grad.astype(bf16)
+    qkv_ref[:, latent_width + HD :] = grads[:, latent_width + HD :].astype(bf16)
+    qkv_grad = qkv_ref[...]
+    for slot in range(members):
+        part = dot_nt(qkv_grad, parts_ref[slot * step : (slot + 1) * step, :qkv_width])
+        place = pl.multiple_of((me_ref[0] ^ slot) * step, step)
+        back_ref[:, pl.ds(place, step)] = part
+    _, normed, factor = normalize(tokens_ref[...].astype(f32), 1.0)
+    upstream = back_ref[...]
+    attn_gain = jnp.sum(upstream * normed, axis=0, keepdims=True)
+    scaled = upstream * attn_scale_ref[...]
+    inner = jnp.mean(scaled * normed, axis=-1, keepdims=True)
+    tokens_grad_ref[...] = residual_grad_ref[...] + factor * (scaled - normed * inner)
+    def store(start, columns, part):
+        if cores != 2:
+            small_refs[0][start : start + part.shape[0], columns] = part
+            return
+        part = part.reshape(-1, 2, width // devices, part.shape[1])
+        one, two = (part[:, r].reshape(-1, part.shape[3]) for r in range(2))
+        place = slice(start // 2, start // 2 + one.shape[0])
+        for core, (mine, other) in enumerate(((one, two), (two, one))):
+
+            @pl.when(me_ref[1] == core)
+            def _():
+                small_refs[0][place, columns] = mine
+                small_refs[1][place, columns] = other
+
+    for start in range(0, width, step):
+        part = dot_tn(attn_in_ref[:, start : start + step], qkv_grad)
+        store(start, slice(0, qkv_width), part.astype(bf16))
+    line = lax.broadcasted_iota(jnp.int32, (128, width), 0)
+    gains = jnp.where(line == 0, attn_gain, jnp.where(line == 1, mlp_gain_ref[...], 0.0))
+    line = lax.broadcasted_iota(jnp.int32, (128, latent_width), 0)
+    latents = jnp.where(line == 2, latent_gain, 0.0).T.reshape(devices, held, 128)
+    gap = jnp.zeros((devices, width // devices - held, 128), f32)
+    latents = jnp.concatenate([latents, gap], axis=1).reshape(width, 128)
+    store(0, slice(qkv_width, qkv_width + 128), (gains.T + latents).astype(bf16))
+
+
+def finish(me, cores, devices, held, own, sent, last, latent, latent_scale, cos_part, sin_part, attn_in, tokens,
+           attn_scale, parts, residual_grad, mlp_gain_grad):
+    args = (own, *sent, *last, latent, latent_scale, cos_part, sin_part, attn_in, tokens, attn_scale, parts,
+            residual_grad, mlp_gain_grad)
+    width, qkv_width = tokens.shape[1], own.shape[1]
+    whole = pl.BlockSpec(memory_space=pltpu.VMEM)
+    halves = 2 if cores == 2 else 1
+    small = [jax.ShapeDtypeStruct((parts.shape[0] // halves, parts.shape[1]), bf16)] * halves
+    return pl.pallas_call(
+        functools.partial(finish_kernel, devices, held, cores),
+        in_specs=[pl.BlockSpec(memory_space=pltpu.SMEM)] + [whole] * len(args),
+        out_specs=[whole] * (len(small) + 1),
+        out_shape=[*small, jax.ShapeDtypeStruct(residual_grad.shape, f32)],
+        scratch_shapes=[pltpu.VMEM(own.shape, bf16), pltpu.VMEM(tokens.shape, f32)],
+        compiler_params=pltpu.CompilerParams(vmem_limit_bytes=52 * 2**20),
+        cost_estimate=pl.CostEstimate(
+            flops=4 * tokens.shape[0] * width * qkv_width,
+            bytes_accessed=parts.size * 4 + tokens.size * 14,
+            transcendentals=0,
+        ),
+    )(jnp.stack([me, lax.axis_index("r")]), *args)
 
 
 def by_block(values, code, count):
@@ -530,8 +623,8 @@
         [jnp.concatenate(query_own[:2], axis=0), jnp.concatenate(query_own[2:], axis=0)], axis=1
     )
     gathered = jnp.concatenate([out_weight, query_own], axis=0)
-    gathered = lax.all_gather(gathered, RING, axis=0, tiled=False)
     qkv_parts, line = share_small(small, cores)
+    gathered = lax.all_gather(after(gathered, line), RING, axis=0, tiled=False)
     gate_up_own = swap_blocks(
         lambda k: jnp.concatenate(
             [take_columns(gate_weight, k, members), take_columns(up_weight, k, members)], axis=1
@@ -553,11 +646,11 @@
     latent_scale = extra[2].reshape(devices, d_rows)[:, : query_gain.shape[0]].reshape(1, -1)
 
     token_rows = tokens.astype(f32)
-    attn_out, attn_normed, attn_factor = normalize(token_rows, attn_scale)
+    attn_out, _, _ = normalize(token_rows, attn_scale)
     attn_in = attn_out.astype(bf16)
     low = dot(by_block(attn_in, me, members), qkv_parts)
     latent = low[:, :latent_width]
-    latent_out, latent_normed, latent_factor = normalize(latent, latent_scale)
+    latent_out, _, _ = normalize(latent, latent_scale)
     latent_in = latent_out.astype(bf16)
     key_own = rotate(low[:, latent_width : latent_width + HD], own_cos, own_sin)
     value_own = low[:, latent_width + HD : qkv_width]
@@ -602,11 +695,10 @@
     slots = [back[i * rows : (i + 1) * rows] for i in range(members)]
     loads = first_loads(slots)
     back_sent = send_loads(loads, *GROUP)
-    ffn_back = dot(after(hidden, loads), down_full).astype(bf16)
-    back_sent = after(back_sent, ffn_back)
-    ffn_slots = [ffn_back[i * rows : (i + 1) * rows] for i in range(members)]
-    gate_up_wgrad = dot_tn(ffn_in, after(gate_up_grad, back_sent)).astype(bf16)
-    ffn_in_grad = send_last(slots, after(back_sent, gate_up_wgrad), *GROUP)
+    gate_up_wgrad = dot_tn(ffn_in, after(gate_up_grad, loads)).astype(bf16)
+    loads = last_loads(slots, after(back_sent, gate_up_wgrad))
+    gate_up_wgrad = after(gate_up_wgrad, loads)
+    ffn_in_grad = sum_up(slots[0], back_sent, send_loads(loads, *GROUP[::-1]))
     residual_back, mlp_scale_grad = normalize_back(ffn_in_grad, ffn_normed, ffn_factor, mlp_scale)
     residual_grad = grad_rows + residual_back
     attn_grad = (living * residual_grad).astype(bf16)
@@ -615,14 +707,16 @@
         gate_up_wgrad.reshape(members, width // members, -1), RING, scatter_dimension=1, tiled=True
     )
     attn_found = fetch_first(attn_grad, *GROUP)
+    ffn_back = dot(after(hidden, attn_grad), down_full).astype(bf16)
+    ffn_slots = [ffn_back[i * rows : (i + 1) * rows] for i in range(members)]
+    attn_found = after(attn_found, ffn_back)
     attn_grad = jnp.concatenate(fetch_last(attn_grad, attn_found, *GROUP), axis=0)
     ffn_sent = send_loads(after(first_loads(ffn_slots), attn_grad), *GROUP)
-    packed_grad, gathered_grad = attend_back(
+    packed_grad, query_grads = attend_back(
         group_lengths,
         attn_grad,
         gathered,
         query_rot,
-        mixture,
         packed,
         rows,
         heads,
@@ -631,40 +725,45 @@
     slots = [packed_grad[i * rows : (i + 1) * rows] for i in range(members)]
     loads = first_loads(slots)
     packed_sent = send_loads(loads, *GROUP)
+    gathered_grad = gathered_grads(
+        attn_grad, mixture, packed, after(query_grads, loads), gathered.shape, heads
+    )
+    loads = last_loads(slots, after(packed_sent, gathered_grad))
+    gathered_grad = after(gathered_grad, loads)
     gathered_share = lax.psum_scatter(gathered_grad, RING, scatter_dimension=0, tiled=False)
-    loads = last_loads(slots, packed_sent)
-    packed_grad = sum_up(slots[0], packed_sent, send_loads(loads, *GROUP[::-1]))
-    latent_in_grad = packed_grad[:, :latent_width]
-    key_grad = rotate(
-        packed_grad[:, latent_width : latent_width + HD], own_cos, -own_sin
-    ).astype(bf16)
-    value_grad = packed_grad[:, latent_width + HD :].astype(bf16)
-    latent_back, latent_scale_grad = normalize_back(
-        latent_in_grad, latent_normed, latent_factor, latent_scale
-    )
-    spare = jnp.zeros((rows, qkv_parts.shape[1] - qkv_width), bf16)
-    qkv_grad = jnp.concatenate([latent_back.astype(bf16), key_grad, value_grad, spare], axis=1)
-    attn_in_grad = by_block(dot_nt(qkv_grad, qkv_parts), me, members)
-    token_back, attn_scale_grad = normalize_back(attn_in_grad, attn_normed, attn_factor, attn_scale)
-
-    small_grad = dot_tn(attn_in, qkv_grad[:, :qkv_width])
-    latent_column = jnp.pad(
-        latent_scale_grad.reshape(devices, -1), ((0, 0), (0, d_rows - query_gain.shape[0]))
-    ).reshape(-1)
-    columns = jnp.stack([attn_scale_grad, mlp_scale_grad, latent_column])
-    columns = jnp.pad(columns, ((0, 128 - 3), (0, 0))).T
-    small_grad = jnp.concatenate([small_grad, columns], axis=1).astype(bf16)
-    small_slots = small_first(small_grad.reshape(2, 2, 2, 2, cores, d_rows, -1), cores)
+    packed_last = send_loads(loads, *GROUP[::-1])
+    *small_grad, tokens_grad = finish(
+        me,
+        cores,
+        devices,
+        query_gain.shape[0],
+        slots[0],
+        packed_sent,
+        packed_last,
+        latent,
+        latent_scale,
+        own_cos,
+        own_sin,
+        attn_in,
+        tokens,
+        attn_scale,
+        qkv_parts,
+        residual_grad,
+        mlp_scale_grad.reshape(1, -1),
+    )
     ffn_last = send_loads(last_loads(ffn_slots, ffn_sent), *GROUP[::-1])
-    small_slots = after(small_slots, gate_up_share, ffn_last)
+    small_grad = after(small_grad, ffn_last)
+    small_slots = small_first(small_grad, cores, d_rows)
+    small_slots = after(small_slots, gate_up_share)
     small_sent = send_first(small_slots, *GROUP)
     loads = last_loads(small_slots, small_sent)
     small_last = send_loads(loads, *GROUP[::-1])
+    gate_up_share = after(gate_up_share, loads).reshape(members, d_rows, -1)
+    gate_up_found = swap_blocks(lambda k: lax.dynamic_index_in_dim(gate_up_share, k, 0, keepdims=False))
+    small_last = after(small_last, gate_up_found)
     small_pairs = pairs_along_z(sum_up(small_slots[0], small_sent, small_last).astype(bf16))
-    small_share = add_up([small_pairs[0]] + [along_z(small_pairs[code], code) for code in (1, 2, 3)])
-    gate_up_share = after(gate_up_share, small_last).reshape(members, d_rows, -1)
-    gate_up_found = swap_blocks(lambda k: lax.dynamic_index_in_dim(gate_up_share, k, 0, keepdims=False))
-    gathered_share, down_share = after((gathered_share, down_share), small_last)
+    along = [along_z(small_pairs[code], code) for code in (1, 2, 3)]
+    gathered_share, down_share = after((gathered_share, down_share), small_pairs)
     held = out_weight.shape[0]
     out_share = gathered_share[:held]
 
@@ -673,9 +772,9 @@
         return lax.dynamic_slice_in_dim(low, (k // 2) * (width // 2), width // 2, 1)
 
     query_found = swap_blocks(query_part)
+    small_share = add_up([small_pairs[0], *after(along, query_found)])
     ffn_sum = sum_up(ffn_slots[0], ffn_sent, after(ffn_last, small_slots))
     layer_out = (residual + living * ffn_sum).astype(bf16)
-    tokens_grad = after(residual_grad, small_slots) + token_back
     found = in_order(gate_up_found)
     gate_share = jnp.concatenate([part[:, :cut] for part in found], axis=1).astype(f32)
     up_share = jnp.concatenate([part[:, cut:] for part in found], axis=1).astype(f32)

time: 602 us -> 566 us (0.940)
  waiting for transfers between devices: 237 us -> 203 us
  Pallas kernels: 49.6 us -> 68.8 us
  matrix products: 101 us -> 90.5 us
  other arithmetic: 70.2 us -> 59.7 us
  local copies, waits for them, and re-layouts: 55.5 us -> 48.3 us
  starting transfers between devices: 66.7 us -> 73.7 us
    ppermute x45, waiting for transfers between devices: 198 us -> 163 us  [trade(): return lax.ppermute(values, axis, [(0, 1), (1, 0)])]
    pallas_call x0 -> x2, Pallas kernels: none -> 28.9 us  [the longest x1 15.4 us: finish(): pl.pallas_call(functools.partial(finish_kernel, devices, held, cores), in...]
    ppermute x12, waiting for transfers between devices: 8.34 us -> 24.1 us  [swap_blocks(): lax.ppermute(block(me ^ code), DP, [(i, i ^ code) for i in range(4)])]
    ppermute x6, waiting for transfers between devices: 27.7 us -> 13.8 us  [along_z(): return lax.ppermute(values, ('zh', 'zl'), [(i, i ^ code) for i in range(4)])]
    pallas_call x1, Pallas kernels: 33.1 us -> 23.4 us  [attend_back(): pl.pallas_call(functools.partial(attend_back_kernel, members, heads), gri...]
    ppermute x45, starting transfers between devices: 42 us -> 48.6 us  [trade(): return lax.ppermute(values, axis, [(0, 1), (1, 0)])]
    dot_general x3 -> x2, matrix products: 38 us -> 32.4 us  [dot_nt(): lax.dot_general(a, b, (((1,), (1,)), ((), ())), preferred_element_type=f32)]
    unnamed x157 -> x97, local copies, waits for them, and re-layouts: 15.9 us -> 12 us
  transfers between devices with their start and end apart: 69 -> 69, of which waited for: 42 -> 41; matrix products, arithmetic and copies ran while one was open for 34% -> 32% of each run, Pallas kernels for 8% -> 12%
where the time goes in v5:
time: 566 us; the launch traced here: 561 us
  waiting for transfers between devices  203 us (36%)
  matrix products  90.5 us (16%)
  starting transfers between devices  73.7 us (13%)
  Pallas kernels  68.8 us (12%)
  other arithmetic  59.7 us (11%)
  local copies, waits for them, and re-layouts  48.3 us (9%)
  between operations  17.1 us (3%)
    ppermute x45, waiting for transfers between devices, trade(): return lax.ppermute(values, axis, [(0, 1), (1, 0)])  163 us
    ppermute x45, starting transfers between devices, trade(): return lax.ppermute(values, axis, [(0, 1), (1, 0)])  48.6 us
    dot_general x2, matrix products, dot_nt(): lax.dot_general(a, b, (((1,), (1,)), ((), ())), preferred_element_type=f32)  32.4 us
    dot_general x3, matrix products, dot(): return jnp.dot(a, b, preferred_element_type=f32)  32 us
    dot_general x2, matrix products, dot_tn(): lax.dot_general(a, b, (((0,), (0,)), ((), ())), preferred_element_type=f32)  26.1 us
    ppermute x12, waiting for transfers between devices, swap_blocks(): lax.ppermute(block(me ^ code), DP, [(i, i ^ code) for i in range(4)])  24.1 us
    pallas_call x1, Pallas kernels, attend_back(): pl.pallas_call(functools.partial(attend_back_kernel, members, heads), gri...  23.4 us
    pallas_call x1, Pallas kernels, attend(): pl.pallas_call(functools.partial(attend_kernel, members, heads), grid_spe...  16.5 us
  transfers between devices with their start and end apart: 69, of which 41 were waited for; matrix products, arithmetic and copies ran while one was open for 32% of the time, Pallas kernels for 12%

profile of v5, /device:TPU:0, one launch (start us, length us, event | category | flops | bytes accessed | tf_op | source)
XLA Modules:
  0.0 561.0 jit_solution(4086344027388350135)
XLA Ops:
  44.0 6.5 %collective-permute-done.29 = bf16[64,2816]{1,0:T(8,128)(2,1)} collective-permute-done((bf16[64,2816]{1,0:T(8,128)(2,1)}, bf16[64,2816]{1,0:T(8,128)(2,1)}, u32[]{:S(2)}, u32[]{:S(2)}) %collective-permute-start.29) | collective-permute-done | bytes 360480 | tf_op jit(solution)/shard_map/ppermute | solution.py:221
  55.2 11.3 %collective-permute-done.6 = bf16[256,1664]{1,0:T(8,128)(2,1)S(1)} collective-permute-done((bf16[256,1664]{1,0:T(8,128)(2,1)S(1)}, bf16[256,1664]{1,0:T(8,128)(2,1)S(1)}, u32[]{:S(2)}, u32[]{:S(2)}) %collective-permute-start.6) | collective-permute-done | bytes 852000 | tf_op jit(solution)/shard_map/ppermute | solution.py:97
  104.0 14.0 %collective-permute-done.11 = bf16[256,1536]{1,0:T(8,128)(2,1)S(1)} collective-permute-done((bf16[256,1536]{1,0:T(8,128)(2,1)S(1)}, bf16[256,1536]{1,0:T(8,128)(2,1)S(1)}, u32[]{:S(2)}, u32[]{:S(2)}) %collective-permute-start.11) | collective-permute-done | bytes 786464 | tf_op jit(solution)/shard_map/ppermute | solution.py:97
  120.5 10.0 %collective-permute-done.13 = bf16[128,1536]{1,0:T(8,128)(2,1)S(1)} collective-permute-done((bf16[128,1536]{1,0:T(8,128)(2,1)S(1)}, bf16[128,1536]{1,0:T(8,128)(2,1)S(1)}, u32[]{:S(2)}, u32[]{:S(2)}) %collective-permute-start.13) | collective-permute-done | bytes 393248 | tf_op jit(solution)/shard_map/ppermute | solution.py:97
  133.3 16.5 %shard_map.237 = (bf16[1024,1024]{1,0:T(8,128)(2,1)S(1)}, bf16[1024,1024]{1,0:T(8,128)(2,1)S(1)}, bf16[1024,2048]{1,0:T(8,128)(2,1)S(1)}) custom-call(s32[4,2]{1,0:T(4,128)S(1)} %copy.41.lengths_ref, bf16[1024,1536]{1,0:T(8,128)(2,1)S(1)} %constant_dynamic-update-slice_fusion.2.latent_ref.key_ref.value_ref.latents_ref, bf16[8,192,2048]{2,1,0:T(8,128)(2,1)} %bitcast.181, ...), custom_call_target="tpu_custom_call" | custom-call | flops 7516192768 | bytes 15728640 | tf_op jit(solution)/shard_map/pallas_call | solution.py:328
  166.5 11.7 %collective-permute-done.20 = bf16[256,2048]{1,0:T(8,128)(2,1)S(1)} collective-permute-done((bf16[256,2048]{1,0:T(8,128)(2,1)S(1)}, bf16[256,2048]{1,0:T(8,128)(2,1)S(1)}, u32[]{:S(2)}, u32[]{:S(2)}) %collective-permute-start.20) | collective-permute-done | bytes 1048608 | tf_op jit(solution)/shard_map/ppermute | solution.py:97
  183.8 7.9 %collective-permute-done.22 = bf16[128,2048]{1,0:T(8,128)(2,1)S(1)} collective-permute-done((bf16[128,2048]{1,0:T(8,128)(2,1)S(1)}, bf16[128,2048]{1,0:T(8,128)(2,1)S(1)}, u32[]{:S(2)}, u32[]{:S(2)}) %collective-permute-start.22) | collective-permute-done | bytes 524320 | tf_op jit(solution)/shard_map/ppermute | solution.py:97
  195.5 20.0 %collective-permute-done.25 = bf16[256,2048]{1,0:T(8,128)(2,1)S(1)} collective-permute-done((bf16[256,2048]{1,0:T(8,128)(2,1)S(1)}, bf16[256,2048]{1,0:T(8,128)(2,1)S(1)}, u32[]{:S(2)}, u32[]{:S(2)}) %collective-permute-start.25) | collective-permute-done | bytes 1048608 | tf_op jit(solution)/shard_map/ppermute | solution.py:97
  219.0 6.4 %collective-permute-done.26 = bf16[128,2048]{1,0:T(8,128)(2,1)S(1)} collective-permute-done((bf16[128,2048]{1,0:T(8,128)(2,1)S(1)}, bf16[128,2048]{1,0:T(8,128)(2,1)S(1)}, u32[]{:S(2)}, u32[]{:S(2)}) %collective-permute-start.26) | collective-permute-done | bytes 524320 | tf_op jit(solution)/shard_map/ppermute | solution.py:97
  231.9 17.4 %fusion.49 = f32[1024,2816]{1,0:T(8,128)S(1)} fusion(bf16[1024,2048]{1,0:T(8,128)(2,1)} %copy-done.37, bf16[2048,2816]{1,0:T(8,128)(2,1)} %bitcast.179), kind=kOutput, calls=%fused_computation.235 | convolution fusion | flops 11811160064 | bytes 27262976 | tf_op jit(solution)/shard_map/dot_general | solution.py:81
  257.2 8.1 %convolution_convert_fusion.1 = bf16[1408,2048]{1,0:T(8,128)(2,1)} fusion(bf16[1024,1408]{1,0:T(8,128)(2,1)S(1)} %multiply_convert_fusion.2, bf16[1024,2048]{1,0:T(8,128)(2,1)S(1)} %constant_dynamic-update-slice_fusion.17), kind=kOutput, calls=%fused_computation.1 | convolution fusion | flops 5908463616 | bytes 12845056 | tf_op jit(solution)/shard_map/dot_general | solution.py:89
  267.6 15.6 %multiply_convert_fusion.1 = (bf16[1024,1408]{1,0:T(8,128)(2,1)}, bf16[1024,1408]{1,0:T(8,128)(2,1)}) fusion(f32[1024,2816]{1,0:T(8,128)} %copy-done.10, bf16[1024,2048]{1,0:T(8,128)(2,1)} %copy-done.14, bf16[1408,2048]{1,0:T(8,128)(2,1)} %all-gather.7.cloned.1.call-done), kind=kOutput, calls=%fused_computation.5 | convolution fusion | flops 5924323328 | bytes 27262976 | tf_op jit(solution)/shard_map/dot_general | solution.py:85
  283.2 16.8 %convolution_convert_fusion.2 = bf16[1024,2048]{1,0:T(8,128)(2,1)S(1)} fusion(bf16[2048,2816]{1,0:T(8,128)(2,1)} %bitcast.180, bf16[1024,1408]{1,0:T(8,128)(2,1)} %get-tuple-element.126, bf16[1024,1408]{1,0:T(8,128)(2,1)} %get-tuple-element.125), kind=kOutput, calls=%fused_computation.10 | convolution fusion | flops 11824791552 | bytes 21495808 | tf_op jit(solution)/shard_map/dot_general | solution.py:85
  308.7 17.9 %convolution_convert_fusion = bf16[2048,2816]{1,0:T(8,128)(2,1)} fusion(bf16[1024,2048]{1,0:T(8,128)(2,1)} %copy-done.37, bf16[1024,2816]{1,0:T(8,128)(2,1)S(1)} %pad_maximum_fusion), kind=kOutput, calls=%fused_computation | convolution fusion | flops 11816927232 | bytes 21495808 | tf_op jit(solution)/shard_map/dot_general | solution.py:89
  334.6 9.8 %collective-permute-done.35 = bf16[128,2048]{1,0:T(8,128)(2,1)S(1)} collective-permute-done((bf16[128,2048]{1,0:T(8,128)(2,1)}, bf16[128,2048]{1,0:T(8,128)(2,1)S(1)}, u32[]{:S(2)}, u32[]{:S(2)}) %collective-permute-start.35) | collective-permute-done | bytes 524320 | tf_op jit(solution)/shard_map/ppermute | solution.py:97
  350.8 9.5 %convolution_convert_fusion.3 = bf16[1024,2048]{1,0:T(8,128)(2,1)S(1)} fusion(bf16[1024,1408]{1,0:T(8,128)(2,1)} %copy-done.21, bf16[1408,2048]{1,0:T(8,128)(2,1)} %all-gather.7.cloned.1.call-done), kind=kOutput, calls=%fused_computation.11 | convolution fusion | flops 5907677184 | bytes 12845056 | tf_op jit(solution)/shard_map/dot_general | solution.py:81
  360.7 12.2 %collective-permute-done.38 = bf16[256,2048]{1,0:T(8,128)(2,1)S(1)} collective-permute-done((bf16[256,2048]{1,0:T(8,128)(2,1)}, bf16[256,2048]{1,0:T(8,128)(2,1)S(1)}, u32[]{:S(2)}, u32[]{:S(2)}) %collective-permute-start.38) | collective-permute-done | bytes 1048608 | tf_op jit(solution)/shard_map/ppermute | solution.py:97
  376.1 9.4 %collective-permute-done.39 = bf16[128,2048]{1,0:T(8,128)(2,1)S(1)} collective-permute-done((bf16[128,2048]{1,0:T(8,128)(2,1)S(1)}, bf16[128,2048]{1,0:T(8,128)(2,1)S(1)}, u32[]{:S(2)}, u32[]{:S(2)}) %collective-permute-start.39) | collective-permute-done | bytes 524320 | tf_op jit(solution)/shard_map/ppermute | solution.py:97
  388.4 23.4 %shard_map.238 = (bf16[1024,1536]{1,0:T(8,128)(2,1)}, bf16[1024,1024]{1,0:T(8,128)(2,1)}) custom-call(s32[4,2]{1,0:T(4,128)} %copy-done.5, bf16[1024,2048]{1,0:T(8,128)(2,1)} %copy-done.38, bf16[8,192,2048]{2,1,0:T(8,128)(2,1)} %bitcast.183, bf16[8,192,2048]{2,1,0:T(8,128)(2,1)} %bitcast.184, bf16[1024,1024]{1,0:T(8,128)(2,1)} %copy-done.7, ...), custom_call_target="tpu_custom_call" | custom-call | flops 9126805504 | bytes 16777216 | tf_op jit(solution)/shard_map/pallas_call | solution.py:438
  417.9 13.5 %shard_map.239 = bf16[8,192,2048]{2,1,0:T(8,128)(2,1)} custom-call(bf16[1024,2048]{1,0:T(8,128)(2,1)} %copy-done.38, bf16[1024,1024]{1,0:T(8,128)(2,1)} %copy-done.6, bf16[1024,1536]{1,0:T(8,128)(2,1)} %copy-done.2, bf16[1024,1024]{1,0:T(8,128)(2,1)} %get-tuple-element.92.query_grads_ref), custom_call_target="tpu_custom_call" | custom-call | flops 6442450944 | bytes 16777216 | tf_op jit(solution)/shard_map/pallas_call | solution.py:417
  445.8 15.4 %shard_map.240 = (bf16[1024,1664]{1,0:T(8,128)(2,1)}, bf16[1024,1664]{1,0:T(8,128)(2,1)}, f32[256,2048]{1,0:T(8,128)}) custom-call(s32[2]{0:T(128)S(1)} %pad_add_fusion.me_ref, bf16[256,1536]{1,0:T(8,128)(2,1)S(1)} %slice.406.own_ref, bf16[256,1536]{1,0:T(8,128)(2,1)} %copy-done.23, bf16[256,1536]{1,0:T(8,128)(2,1)} %collective-permute-done.46.second_ref, ...), custom_call_target="tpu_custom_call" | custom-call | flops 3221225472 | bytes 20971520 | tf_op jit(solution)/shard_map/pallas_call | solution.py:557
  461.5 6.2 %collective-permute-done.49 = bf16[1024,1664]{1,0:T(8,128)(2,1)} collective-permute-done((bf16[1024,1664]{1,0:T(8,128)(2,1)}, bf16[1024,1664]{1,0:T(8,128)(2,1)}, u32[]{:S(2)}, u32[]{:S(2)}) %collective-permute-start.49) | collective-permute-done | bytes 3407904 | tf_op jit(solution)/shard_map/ppermute | solution.py:97
  481.9 14.9 %collective-permute-done.50 = bf16[256,1664]{1,0:T(8,128)(2,1)S(1)} collective-permute-done((bf16[256,1664]{1,0:T(8,128)(2,1)S(1)}, bf16[256,1664]{1,0:T(8,128)(2,1)S(1)}, u32[]{:S(2)}, u32[]{:S(2)}) %collective-permute-start.50) | collective-permute-done | bytes 852000 | tf_op jit(solution)/shard_map/ppermute | solution.py:97
  541.8 8.2 %collective-permute-done.58 = bf16[64,1664]{1,0:T(8,128)(2,1)S(1)} collective-permute-done((bf16[64,1664]{1,0:T(8,128)(2,1)S(1)}, bf16[64,1664]{1,0:T(8,128)(2,1)S(1)}, u32[]{:S(2)}, u32[]{:S(2)}) %collective-permute-start.58) | collective-permute-done | bytes 213024 | tf_op jit(solution)/shard_map/ppermute | solution.py:198
  (370 shorter events, 241.0 us)
Async XLA Ops:
  7.2 126.1 %all-gather.9.cloned.1.call-start = ((), (), s32[]{:S(2)}) async-start(), calls=%async_computation.8 | async-start | bytes 7077888 | tf_op jit(solution)/shard_map/all_gather | solution.py:627
  29.7 202.2 %all-gather.5.cloned.1.call-start = ((), (), s32[]{:S(2)}) async-start(), calls=%async_computation.3 | async-start | bytes 12976128 | tf_op jit(solution)/shard_map/all_gather | solution.py:659
  36.0 30.5 %collective-permute-start.6 = (bf16[256,1664]{1,0:T(8,128)(2,1)S(1)}, bf16[256,1664]{1,0:T(8,128)(2,1)S(1)}, u32[]{:S(2)}, u32[]{:S(2)}) collective-permute-start(bf16[256,1664]{1,0:T(8,128)(2,1)S(1)} %pad_maximum_fusion.13), channel_id=1, source_target_pairs={{0,16},{16,0},{1,17},{17,1},{2,18},{18,2},{3,19},{19,3},{4,20},{20... | collective-permute-start | bytes 2555912 | tf_op jit(solution)/shard_map/ppermute | solution.py:97
  37.6 30.5 %collective-permute-start.4 = (bf16[256,1664]{1,0:T(8,128)(2,1)S(1)}, bf16[256,1664]{1,0:T(8,128)(2,1)S(1)}, u32[]{:S(2)}, u32[]{:S(2)}) collective-permute-start(bf16[256,1664]{1,0:T(8,128)(2,1)S(1)} %pad_maximum_fusion.13), channel_id=1, source_target_pairs={{0,8},{8,0},{1,9},{9,1},{2,10},{10,2},{3,11},{11,3},{4,12},{12,4},... | collective-permute-start | bytes 2555912 | tf_op jit(solution)/shard_map/ppermute | solution.py:97
  83.6 184.0 %all-gather.7.cloned.1.call-start = ((), (), s32[]{:S(2)}) async-start(), calls=%async_computation.4 | async-start | bytes 6488064 | tf_op jit(solution)/shard_map/all_gather | solution.py:634
  98.5 21.3 %collective-permute-start.12 = (bf16[256,1536]{1,0:T(8,128)(2,1)S(1)}, bf16[256,1536]{1,0:T(8,128)(2,1)S(1)}, u32[]{:S(2)}, u32[]{:S(2)}) collective-permute-start(bf16[256,1536]{1,0:T(8,128)(2,1)S(1)} %get-tuple-element.200), channel_id=1, source_target_pairs={{0,16},{16,0},{1,17},{17,1},{2,18},{18,2},{3,19},{19,3},{4,20},{20... | collective-permute-start | bytes 2359304 | tf_op jit(solution)/shard_map/ppermute | solution.py:97
  130.6 24.2 %collective-permute-start.19 = (bf16[256,2048]{1,0:T(8,128)(2,1)}, bf16[256,2048]{1,0:T(8,128)(2,1)}, u32[]{:S(2)}, u32[]{:S(2)}) collective-permute-start(bf16[256,2048]{1,0:T(8,128)(2,1)} %fusion.1), channel_id=1, source_target_pairs={{0,16},{16,0},{1,17},{17,1},{2,18},{18,2},{3,19},{19,3},{4,20},{20... | collective-permute-start | bytes 3145736 | tf_op jit(solution)/shard_map/ppermute | solution.py:97
  131.0 24.0 %collective-permute-start.18 = (bf16[256,2048]{1,0:T(8,128)(2,1)}, bf16[256,2048]{1,0:T(8,128)(2,1)}, u32[]{:S(2)}, u32[]{:S(2)}) collective-permute-start(bf16[256,2048]{1,0:T(8,128)(2,1)} %fusion.1), channel_id=1, source_target_pairs={{0,8},{8,0},{1,9},{9,1},{2,10},{10,2},{3,11},{11,3},{4,12},{12,4},... | collective-permute-start | bytes 3145736 | tf_op jit(solution)/shard_map/ppermute | solution.py:97
  155.4 22.9 %collective-permute-start.20 = (bf16[256,2048]{1,0:T(8,128)(2,1)S(1)}, bf16[256,2048]{1,0:T(8,128)(2,1)S(1)}, u32[]{:S(2)}, u32[]{:S(2)}) collective-permute-start(bf16[256,2048]{1,0:T(8,128)(2,1)S(1)} %pad_maximum_fusion.6), channel_id=1, source_target_pairs={{0,8},{8,0},{1,9},{9,1},{2,10},{10,2},{3,11},{11,3},{4,12},{12,4},... | collective-permute-start | bytes 3145736 | tf_op jit(solution)/shard_map/ppermute | solution.py:97
  157.6 23.0 %collective-permute-start.21 = (bf16[256,2048]{1,0:T(8,128)(2,1)}, bf16[256,2048]{1,0:T(8,128)(2,1)S(1)}, u32[]{:S(2)}, u32[]{:S(2)}) collective-permute-start(bf16[256,2048]{1,0:T(8,128)(2,1)} %pad_maximum_fusion.7), channel_id=1, source_target_pairs={{0,16},{16,0},{1,17},{17,1},{2,18},{18,2},{3,19},{19,3},{4,20},{20... | collective-permute-start | bytes 3145736 | tf_op jit(solution)/shard_map/ppermute | solution.py:97
  158.5 191.2 %reduce-scatter.4.cloned.1.call-start = ((), (), s32[]{:S(2)}) async-start(), calls=%async_computation.5 | async-start | bytes 6488064 | tf_op jit(solution)/shard_map/reduce_scatter | solution.py:686
  193.0 22.6 %collective-permute-start.25 = (bf16[256,2048]{1,0:T(8,128)(2,1)S(1)}, bf16[256,2048]{1,0:T(8,128)(2,1)S(1)}, u32[]{:S(2)}, u32[]{:S(2)}) collective-permute-start(bf16[256,2048]{1,0:T(8,128)(2,1)S(1)} %get-tuple-element.122), channel_id=1, source_target_pairs={{0,16},{16,0},{1,17},{17,1},{2,18},{18,2},{3,19},{19,3},{4,20},{20... | collective-permute-start | bytes 3145736 | tf_op jit(solution)/shard_map/ppermute | solution.py:97
  194.0 23.0 %collective-permute-start.24 = (bf16[256,2048]{1,0:T(8,128)(2,1)S(1)}, bf16[256,2048]{1,0:T(8,128)(2,1)S(1)}, u32[]{:S(2)}, u32[]{:S(2)}) collective-permute-start(bf16[256,2048]{1,0:T(8,128)(2,1)S(1)} %get-tuple-element.122), channel_id=1, source_target_pairs={{0,8},{8,0},{1,9},{9,1},{2,10},{10,2},{3,11},{11,3},{4,12},{12,4},... | collective-permute-start | bytes 3145736 | tf_op jit(solution)/shard_map/ppermute | solution.py:97
  265.3 207.9 %reduce-scatter.6.cloned.1.call-start = ((), (), s32[]{:S(2)}) async-start(), calls=%async_computation.6 | async-start | bytes 12976128 | tf_op jit(solution)/shard_map/reduce_scatter | solution.py:706
  301.6 25.5 %collective-permute-start.33 = (bf16[256,2048]{1,0:T(8,128)(2,1)}, bf16[256,2048]{1,0:T(8,128)(2,1)S(1)}, u32[]{:S(2)}, u32[]{:S(2)}) collective-permute-start(bf16[256,2048]{1,0:T(8,128)(2,1)} %pad_maximum_fusion.8), channel_id=1, source_target_pairs={{0,8},{8,0},{1,9},{9,1},{2,10},{10,2},{3,11},{11,3},{4,12},{12,4},... | collective-permute-start | bytes 3145736 | tf_op jit(solution)/shard_map/ppermute | solution.py:97
  304.1 25.3 %collective-permute-start.34 = (bf16[256,2048]{1,0:T(8,128)(2,1)}, bf16[256,2048]{1,0:T(8,128)(2,1)S(1)}, u32[]{:S(2)}, u32[]{:S(2)}) collective-permute-start(bf16[256,2048]{1,0:T(8,128)(2,1)} %pad_maximum_fusion.9), channel_id=1, source_target_pairs={{0,16},{16,0},{1,17},{17,1},{2,18},{18,2},{3,19},{19,3},{4,20},{20... | collective-permute-start | bytes 3145736 | tf_op jit(solution)/shard_map/ppermute | solution.py:97
  330.8 202.5 %reduce-scatter.8.cloned.1.call-start = ((), (), s32[]{:S(2)}) async-start(), calls=%async_computation.7 | async-start | bytes 7077888 | tf_op jit(solution)/shard_map/reduce_scatter | solution.py:733
  349.7 23.3 %collective-permute-start.38 = (bf16[256,2048]{1,0:T(8,128)(2,1)}, bf16[256,2048]{1,0:T(8,128)(2,1)S(1)}, u32[]{:S(2)}, u32[]{:S(2)}) collective-permute-start(bf16[256,2048]{1,0:T(8,128)(2,1)} %get-tuple-element.81), channel_id=1, source_target_pairs={{0,16},{16,0},{1,17},{17,1},{2,18},{18,2},{3,19},{19,3},{4,20},{20... | collective-permute-start | bytes 3145736 | tf_op jit(solution)/shard_map/ppermute | solution.py:97
  350.3 23.3 %collective-permute-start.37 = (bf16[256,2048]{1,0:T(8,128)(2,1)}, bf16[256,2048]{1,0:T(8,128)(2,1)S(1)}, u32[]{:S(2)}, u32[]{:S(2)}) collective-permute-start(bf16[256,2048]{1,0:T(8,128)(2,1)} %get-tuple-element.81), channel_id=1, source_target_pairs={{0,8},{8,0},{1,9},{9,1},{2,10},{10,2},{3,11},{11,3},{4,12},{12,4},... | collective-permute-start | bytes 3145736 | tf_op jit(solution)/shard_map/ppermute | solution.py:97
  385.7 26.1 %collective-permute-start.41 = (bf16[256,2048]{1,0:T(8,128)(2,1)S(1)}, bf16[256,2048]{1,0:T(8,128)(2,1)S(1)}, u32[]{:S(2)}, u32[]{:S(2)}) collective-permute-start(bf16[256,2048]{1,0:T(8,128)(2,1)S(1)} %pad_maximum_fusion.10), channel_id=1, source_target_pairs={{0,8},{8,0},{1,9},{9,1},{2,10},{10,2},{3,11},{11,3},{4,12},{12,4},... | collective-permute-start | bytes 3145736 | tf_op jit(solution)/shard_map/ppermute | solution.py:97
  387.1 24.7 %collective-permute-start.43 = (bf16[256,2048]{1,0:T(8,128)(2,1)S(1)}, bf16[256,2048]{1,0:T(8,128)(2,1)S(1)}, u32[]{:S(2)}, u32[]{:S(2)}) collective-permute-start(bf16[256,2048]{1,0:T(8,128)(2,1)S(1)} %pad_maximum_fusion.11), channel_id=1, source_target_pairs={{0,16},{16,0},{1,17},{17,1},{2,18},{18,2},{3,19},{19,3},{4,20},{20... | collective-permute-start | bytes 3145736 | tf_op jit(solution)/shard_map/ppermute | solution.py:97
  438.9 22.3 %collective-permute-start.44 = (bf16[128,2048]{1,0:T(8,128)(2,1)}, bf16[128,2048]{1,0:T(8,128)(2,1)}, u32[]{:S(2)}, u32[]{:S(2)}) collective-permute-start(bf16[128,2048]{1,0:T(8,128)(2,1)} %get-tuple-element.127), channel_id=1, source_target_pairs={{0,8},{8,0},{1,9},{9,1},{2,10},{10,2},{3,11},{11,3},{4,12},{12,4},... | collective-permute-start | bytes 1572872 | tf_op jit(solution)/shard_map/ppermute | solution.py:97
  439.8 21.4 %collective-permute-start.42 = (bf16[128,2048]{1,0:T(8,128)(2,1)}, bf16[128,2048]{1,0:T(8,128)(2,1)}, u32[]{:S(2)}, u32[]{:S(2)}) collective-permute-start(bf16[128,2048]{1,0:T(8,128)(2,1)} %get-tuple-element.128), channel_id=1, source_target_pairs={{0,16},{16,0},{1,17},{17,1},{2,18},{18,2},{3,19},{19,3},{4,20},{20... | collective-permute-start | bytes 1572872 | tf_op jit(solution)/shard_map/ppermute | solution.py:97
  504.8 22.4 %collective-permute-start.51 = (bf16[128,1664]{1,0:T(8,128)(2,1)S(1)}, bf16[128,1664]{1,0:T(8,128)(2,1)S(1)}, u32[]{:S(2)}, u32[]{:S(2)}) collective-permute-start(bf16[128,1664]{1,0:T(8,128)(2,1)S(1)} %add_convert_fusion.8), channel_id=1, source_target_pairs={{0,16},{16,0},{1,17},{17,1},{2,18},{18,2},{3,19},{19,3},{4,20},{20... | collective-permute-start | bytes 1277960 | tf_op jit(solution)/shard_map/ppermute | solution.py:97
  (87 other events, 944.4 us)
Sparse Core Ops, SparseCore 0:
  29.9 68.4 all-gather.8
  100.5 106.6 all-gather.4
  208.9 58.6 all-gather.6
  269.7 65.3 reduce-scatter.3
  337.2 117.6 reduce-scatter.5
  461.5 70.2 reduce-scatter.7

commit v6 on v5

--- a/solution.py
+++ b/solution.py
@@ -569,6 +569,73 @@
     )(jnp.stack([me, lax.axis_index("r")]), *args)
 
 
+def ffn_kernel(rows_ref, gate_ref, up_ref, hidden_ref, slope_ref, silu_ref):
+    weights = jnp.concatenate([gate_ref[...], up_ref[...]], axis=1)
+    act = dot(rows_ref[...], weights)
+    gate, up = act[:, : gate_ref.shape[1]], act[:, gate_ref.shape[1] :]
+    sigmoid = jax.nn.sigmoid(gate)
+    silu = gate * sigmoid
+    hidden_ref[...] = (silu * up).astype(bf16)
+    slope_ref[...] = (up * sigmoid * (1.0 + gate * (1.0 - sigmoid))).astype(bf16)
+    silu_ref[...] = silu.astype(bf16)
+
+
+def ffn(rows, gate_up):
+    total, width = rows.shape
+    cut = gate_up.shape[1] // 2
+    tile = 128
+    block = pl.BlockSpec((total, tile), lambda j: (0, j))
+    out = jax.ShapeDtypeStruct((total, cut), bf16)
+    return pl.pallas_call(
+        ffn_kernel,
+        grid=(cut // tile,),
+        in_specs=[
+            pl.BlockSpec((total, width), lambda j: (0, 0), pipeline_mode=pl.Buffered(1)),
+            pl.BlockSpec((width, tile), lambda j: (0, j)),
+            pl.BlockSpec((width, tile), lambda j: (0, cut // tile + j)),
+        ],
+        out_specs=[block, block, block],
+        out_shape=[out, out, out],
+        compiler_params=pltpu.CompilerParams(vmem_limit_bytes=58 * 2**20),
+        cost_estimate=pl.CostEstimate(
+            flops=4 * total * width * cut,
+            bytes_accessed=2 * (gate_up.size + rows.size + 3 * total * cut),
+            transcendentals=total * cut,
+        ),
+    )(rows, gate_up, gate_up)
+
+
+def ffn_back_kernel(grad_ref, down_ref, slope_ref, silu_ref, out_ref):
+    cut = slope_ref.shape[1]
+    hidden_grad = dot_nt(grad_ref[...], down_ref[...])
+    out_ref[:, :cut] = (hidden_grad * slope_ref[...].astype(f32)).astype(bf16)
+    out_ref[:, cut:] = (hidden_grad * silu_ref[...].astype(f32)).astype(bf16)
+
+
+def ffn_back(grads, down_full, slope, silu):
+    total, width = grads.shape
+    cut, tile = slope.shape[1], total // 2
+    block = pl.BlockSpec((tile, cut), lambda i: (i, 0))
+    return pl.pallas_call(
+        ffn_back_kernel,
+        grid=(total // tile,),
+        in_specs=[
+            pl.BlockSpec((tile, width), lambda i: (i, 0)),
+            pl.BlockSpec((cut, width), lambda i: (0, 0), pipeline_mode=pl.Buffered(1)),
+            block,
+            block,
+        ],
+        out_specs=pl.BlockSpec((tile, 2 * cut), lambda i: (i, 0)),
+        out_shape=jax.ShapeDtypeStruct((total, 2 * cut), bf16),
+        compiler_params=pltpu.CompilerParams(vmem_limit_bytes=58 * 2**20),
+        cost_estimate=pl.CostEstimate(
+            flops=2 * total * width * cut,
+            bytes_accessed=2 * (grads.size + down_full.size + 4 * total * cut),
+            transcendentals=0,
+        ),
+    )(grads, down_full, slope, silu)
+
+
 def by_block(values, code, count):
     step = values.shape[1] // count
     return jnp.concatenate(
@@ -672,25 +739,15 @@
 
     ffn_out, ffn_normed, ffn_factor = normalize(residual, mlp_scale)
     ffn_in = jnp.concatenate(gather_quad(ffn_out.astype(bf16), *GROUP), axis=0)
-    gate_up_act = dot(ffn_in, gate_up)
+    hidden, slope, silu_gate = ffn(ffn_in, gate_up)
     ffn_grad_rest = after(ffn_grad_rest, ffn_in)
-    ffn_grad_rest = after((trade(ffn_grad_rest[0], "x"), trade(ffn_grad_rest[1], "y")), gate_up_act)
+    ffn_grad_rest = after((trade(ffn_grad_rest[0], "x"), trade(ffn_grad_rest[1], "y")), hidden)
     ffn_grad = lax.dynamic_update_slice(ffn_grad, ffn_grad_rest[0], (3 * rows, 0))
     ffn_grad = lax.dynamic_update_slice(ffn_grad, ffn_grad_rest[1], (3 * rows + rows // 2, 0))
-    gate_act, up_act = gate_up_act[:, :cut], gate_up_act[:, cut:]
-    sigmoid_gate = jax.nn.sigmoid(gate_act)
-    silu_gate = gate_act * sigmoid_gate
-    hidden = (silu_gate * up_act).astype(bf16)
-
     down_wgrad = dot_tn(hidden, ffn_grad).astype(bf16)
     down_share = lax.psum_scatter(down_wgrad, RING, scatter_dimension=0, tiled=True)
 
-    hidden_grad = dot_nt(after(ffn_grad, down_wgrad), down_full)
-    gate_grad = (
-        hidden_grad * up_act * sigmoid_gate * (1.0 + gate_act * (1.0 - sigmoid_gate))
-    ).astype(bf16)
-    up_grad = (hidden_grad * silu_gate).astype(bf16)
-    gate_up_grad = jnp.concatenate([gate_grad, up_grad], axis=1)
+    gate_up_grad = ffn_back(after(ffn_grad, down_wgrad), down_full, slope, silu_gate)
     back = dot_nt(gate_up_grad, gate_up).astype(bf16)
     slots = [back[i * rows : (i + 1) * rows] for i in range(members)]
     loads = first_loads(slots)
@@ -707,9 +764,9 @@
         gate_up_wgrad.reshape(members, width // members, -1), RING, scatter_dimension=1, tiled=True
     )
     attn_found = fetch_first(attn_grad, *GROUP)
-    ffn_back = dot(after(hidden, attn_grad), down_full).astype(bf16)
-    ffn_slots = [ffn_back[i * rows : (i + 1) * rows] for i in range(members)]
-    attn_found = after(attn_found, ffn_back)
+    ffn_part = dot(after(hidden, attn_grad), down_full).astype(bf16)
+    ffn_slots = [ffn_part[i * rows : (i + 1) * rows] for i in range(members)]
+    attn_found = after(attn_found, ffn_part)
     attn_grad = jnp.concatenate(fetch_last(attn_grad, attn_found, *GROUP), axis=0)
     ffn_sent = send_loads(after(first_loads(ffn_slots), attn_grad), *GROUP)
     packed_grad, query_grads = attend_back(
@@ -762,18 +819,21 @@
     gate_up_found = swap_blocks(lambda k: lax.dynamic_index_in_dim(gate_up_share, k, 0, keepdims=False))
     small_last = after(small_last, gate_up_found)
     small_pairs = pairs_along_z(sum_up(small_slots[0], small_sent, small_last).astype(bf16))
+    small_pairs = after(small_pairs, gathered_share)
     along = [along_z(small_pairs[code], code) for code in (1, 2, 3)]
     gathered_share, down_share = after((gathered_share, down_share), small_pairs)
     held = out_weight.shape[0]
     out_share = gathered_share[:held]
 
+    query_share = after(gathered_share, along[0])
+
     def query_part(k):
-        low = lax.dynamic_slice_in_dim(gathered_share, held + (k % 2) * (held // 4), held // 4, 0)
+        low = lax.dynamic_slice_in_dim(query_share, held + (k % 2) * (held // 4), held // 4, 0)
         return lax.dynamic_slice_in_dim(low, (k // 2) * (width // 2), width // 2, 1)
 
     query_found = swap_blocks(query_part)
     small_share = add_up([small_pairs[0], *after(along, query_found)])
-    ffn_sum = sum_up(ffn_slots[0], ffn_sent, after(ffn_last, small_slots))
+    ffn_sum = sum_up(*after((ffn_slots[0], ffn_sent, ffn_last), small_slots))
     layer_out = (residual + living * ffn_sum).astype(bf16)
     found = in_order(gate_up_found)
     gate_share = jnp.concatenate([part[:, :cut] for part in found], axis=1).astype(f32)

time: 566 us -> 563 us (level)
  Pallas kernels: 68.8 us -> 101 us
  matrix products: 90.5 us -> 58.5 us
  other arithmetic: 59.7 us -> 45.3 us
  waiting for transfers between devices: 203 us -> 216 us
    pallas_call x0 -> x2, Pallas kernels: none -> 32.3 us  [the longest x1 19 us: ffn(): pl.pallas_call(ffn_kernel, grid=(cut // tile,), in_specs=[pl.BlockSpec((t...]
    dot_general x3 -> x2, matrix products: 32 us -> 14.8 us  [dot(): return jnp.dot(a, b, preferred_element_type=f32)]
    dot_general x2 -> x1, matrix products: 32.4 us -> 18 us  [dot_nt(): lax.dot_general(a, b, (((1,), (1,)), ((), ())), preferred_element_type=f32)]
    ppermute x45, waiting for transfers between devices: 163 us -> 170 us  [trade(): return lax.ppermute(values, axis, [(0, 1), (1, 0)])]
    unnamed x97 -> x93, local copies, waits for them, and re-layouts: 12 us -> 12.8 us
  transfers between devices with their start and end apart: 69 -> 69, of which waited for: 41 -> 42; matrix products, arithmetic and copies ran while one was open for 32% -> 24% of each run, Pallas kernels for 12% -> 18%
where the time goes in v6:
time: 563 us; the launch traced here: 554 us
  waiting for transfers between devices  216 us (38%)
  Pallas kernels  101 us (18%)
  starting transfers between devices  70.3 us (12%)
  matrix products  58.5 us (10%)
  local copies, waits for them, and re-layouts  45.4 us (8%)
  other arithmetic  45.3 us (8%)
  between operations  17.2 us (3%)
    ppermute x45, waiting for transfers between devices, trade(): return lax.ppermute(values, axis, [(0, 1), (1, 0)])  170 us
    ppermute x45, starting transfers between devices, trade(): return lax.ppermute(values, axis, [(0, 1), (1, 0)])  45 us
    dot_general x2, matrix products, dot_tn(): lax.dot_general(a, b, (((0,), (0,)), ((), ())), preferred_element_type=f32)  25.6 us
    ppermute x12, waiting for transfers between devices, swap_blocks(): lax.ppermute(block(me ^ code), DP, [(i, i ^ code) for i in range(4)])  24.1 us
    pallas_call x1, Pallas kernels, attend_back(): pl.pallas_call(functools.partial(attend_back_kernel, members, heads), gri...  23.4 us
    pallas_call x1, Pallas kernels, ffn(): pl.pallas_call(ffn_kernel, grid=(cut // tile,), in_specs=[pl.BlockSpec((t...  19 us
    dot_general x1, matrix products, dot_nt(): lax.dot_general(a, b, (((1,), (1,)), ((), ())), preferred_element_type=f32)  18 us
    pallas_call x1, Pallas kernels, attend(): pl.pallas_call(functools.partial(attend_kernel, members, heads), grid_spe...  16.7 us
  transfers between devices with their start and end apart: 69, of which 42 were waited for; matrix products, arithmetic and copies ran while one was open for 24% of the time, Pallas kernels for 18%

profile of v6, /device:TPU:0, one launch (start us, length us, event | category | flops | bytes accessed | tf_op | source)
XLA Modules:
  0.0 554.1 jit_solution(14465080178714520211)
XLA Ops:
  44.2 6.5 %collective-permute-done.29 = bf16[64,2816]{1,0:T(8,128)(2,1)} collective-permute-done((bf16[64,2816]{1,0:T(8,128)(2,1)}, bf16[64,2816]{1,0:T(8,128)(2,1)}, u32[]{:S(2)}, u32[]{:S(2)}) %collective-permute-start.29) | collective-permute-done | bytes 360480 | tf_op jit(solution)/shard_map/ppermute | solution.py:221
  55.3 11.3 %collective-permute-done.6 = bf16[256,1664]{1,0:T(8,128)(2,1)S(1)} collective-permute-done((bf16[256,1664]{1,0:T(8,128)(2,1)S(1)}, bf16[256,1664]{1,0:T(8,128)(2,1)S(1)}, u32[]{:S(2)}, u32[]{:S(2)}) %collective-permute-start.6) | collective-permute-done | bytes 852000 | tf_op jit(solution)/shard_map/ppermute | solution.py:97
  102.3 14.8 %collective-permute-done.11 = bf16[256,1536]{1,0:T(8,128)(2,1)S(1)} collective-permute-done((bf16[256,1536]{1,0:T(8,128)(2,1)S(1)}, bf16[256,1536]{1,0:T(8,128)(2,1)S(1)}, u32[]{:S(2)}, u32[]{:S(2)}) %collective-permute-start.11) | collective-permute-done | bytes 786464 | tf_op jit(solution)/shard_map/ppermute | solution.py:97
  119.7 9.9 %collective-permute-done.13 = bf16[128,1536]{1,0:T(8,128)(2,1)S(1)} collective-permute-done((bf16[128,1536]{1,0:T(8,128)(2,1)S(1)}, bf16[128,1536]{1,0:T(8,128)(2,1)S(1)}, u32[]{:S(2)}, u32[]{:S(2)}) %collective-permute-start.13) | collective-permute-done | bytes 393248 | tf_op jit(solution)/shard_map/ppermute | solution.py:97
  136.2 16.7 %shard_map.237 = (bf16[1024,1024]{1,0:T(8,128)(2,1)S(1)}, bf16[1024,1024]{1,0:T(8,128)(2,1)S(1)}, bf16[1024,2048]{1,0:T(8,128)(2,1)S(1)}) custom-call(s32[4,2]{1,0:T(4,128)S(1)} %copy.41.lengths_ref, bf16[1024,1536]{1,0:T(8,128)(2,1)S(1)} %copy-done.1, bf16[8,192,2048]{2,1,0:T(8,128)(2,1)} %bitcast.179, bf16[8,192,2048]{2,1,0:T(8,128)(2,1)} %bitcast.180, ...), custom_call_target="tpu_custom_call" | custom-call | flops 7516192768 | bytes 15728640 | tf_op jit(solution)/shard_map/pallas_call | solution.py:328
  165.3 13.3 %collective-permute-done.20 = bf16[256,2048]{1,0:T(8,128)(2,1)S(1)} collective-permute-done((bf16[256,2048]{1,0:T(8,128)(2,1)S(1)}, bf16[256,2048]{1,0:T(8,128)(2,1)S(1)}, u32[]{:S(2)}, u32[]{:S(2)}) %collective-permute-start.20) | collective-permute-done | bytes 1048608 | tf_op jit(solution)/shard_map/ppermute | solution.py:97
  183.1 7.6 %collective-permute-done.22 = bf16[128,2048]{1,0:T(8,128)(2,1)S(1)} collective-permute-done((bf16[128,2048]{1,0:T(8,128)(2,1)S(1)}, bf16[128,2048]{1,0:T(8,128)(2,1)S(1)}, u32[]{:S(2)}, u32[]{:S(2)}) %collective-permute-start.22) | collective-permute-done | bytes 524320 | tf_op jit(solution)/shard_map/ppermute | solution.py:97
  195.5 20.0 %collective-permute-done.25 = bf16[256,2048]{1,0:T(8,128)(2,1)S(1)} collective-permute-done((bf16[256,2048]{1,0:T(8,128)(2,1)S(1)}, bf16[256,2048]{1,0:T(8,128)(2,1)S(1)}, u32[]{:S(2)}, u32[]{:S(2)}) %collective-permute-start.25) | collective-permute-done | bytes 1048608 | tf_op jit(solution)/shard_map/ppermute | solution.py:97
  218.9 7.1 %collective-permute-done.26 = bf16[128,2048]{1,0:T(8,128)(2,1)S(1)} collective-permute-done((bf16[128,2048]{1,0:T(8,128)(2,1)S(1)}, bf16[128,2048]{1,0:T(8,128)(2,1)S(1)}, u32[]{:S(2)}, u32[]{:S(2)}) %collective-permute-start.26) | collective-permute-done | bytes 524320 | tf_op jit(solution)/shard_map/ppermute | solution.py:97
  232.0 19.0 %shard_map.238 = (bf16[1024,1408]{1,0:T(8,128)(2,1)}, bf16[1024,1408]{1,0:T(8,128)(2,1)}, bf16[1024,1408]{1,0:T(8,128)(2,1)}) custom-call(bf16[1024,2048]{1,0:T(8,128)(2,1)} %copy-done.33, bf16[2048,2816]{1,0:T(8,128)(2,1)} %bitcast.176, bf16[2048,2816]{1,0:T(8,128)(2,1)} %bitcast.177), custom_call_target="tpu_custom_call" | custom-call | flops 11811160064 | bytes 24379392 | tf_op jit(solution)/shard_map/pallas_call | solution.py:589
  252.7 10.5 %convolution_convert_fusion.1 = bf16[1408,2048]{1,0:T(8,128)(2,1)} fusion(bf16[1024,1408]{1,0:T(8,128)(2,1)} %get-tuple-element.96, bf16[1024,2048]{1,0:T(8,128)(2,1)} %constant_dynamic-update-slice_fusion.17.grad_ref), kind=kOutput, calls=%fused_computation.1 | convolution fusion | flops 5908463616 | bytes 12845056 | tf_op jit(solution)/shard_map/dot_general | solution.py:89
  267.6 13.3 %shard_map.239 = bf16[1024,2816]{1,0:T(8,128)(2,1)} custom-call(bf16[1024,2048]{1,0:T(8,128)(2,1)} %constant_dynamic-update-slice_fusion.17.grad_ref, bf16[1408,2048]{1,0:T(8,128)(2,1)} %all-gather.7.cloned.1.call-done.down_ref, bf16[1024,1408]{1,0:T(8,128)(2,1)} %get-tuple-element.89.slope_ref, bf16[1024,1408]{1,0:T(8,128)(2,1)} %get-tuple-element.90.silu_ref), custom_call_target="tpu_custom_call" | custom-call | flops 5905580032 | bytes 21495808 | tf_op jit(solution)/shard_map/pallas_call | solution.py:619
  280.9 18.0 %convolution_convert_fusion.2 = bf16[1024,2048]{1,0:T(8,128)(2,1)S(1)} fusion(bf16[1024,2816]{1,0:T(8,128)(2,1)} %shard_map.239, bf16[2048,2816]{1,0:T(8,128)(2,1)} %bitcast.178), kind=kOutput, calls=%fused_computation.4 | convolution fusion | flops 11813257216 | bytes 21495808 | tf_op jit(solution)/shard_map/dot_general | solution.py:85
  302.6 15.1 %convolution_convert_fusion = bf16[2048,2816]{1,0:T(8,128)(2,1)} fusion(bf16[1024,2048]{1,0:T(8,128)(2,1)S(1)} %copy-done.34, bf16[1024,2816]{1,0:T(8,128)(2,1)S(1)} %copy-done.39), kind=kOutput, calls=%fused_computation | convolution fusion | flops 11816927232 | bytes 21495808 | tf_op jit(solution)/shard_map/dot_general | solution.py:89
  317.7 6.9 %collective-permute-done.33 = bf16[256,2048]{1,0:T(8,128)(2,1)S(1)} collective-permute-done((bf16[256,2048]{1,0:T(8,128)(2,1)S(1)}, bf16[256,2048]{1,0:T(8,128)(2,1)S(1)}, u32[]{:S(2)}, u32[]{:S(2)}) %collective-permute-start.33) | collective-permute-done | bytes 1048608 | tf_op jit(solution)/shard_map/ppermute | solution.py:97
  331.1 9.7 %collective-permute-done.35 = bf16[128,2048]{1,0:T(8,128)(2,1)S(1)} collective-permute-done((bf16[128,2048]{1,0:T(8,128)(2,1)}, bf16[128,2048]{1,0:T(8,128)(2,1)S(1)}, u32[]{:S(2)}, u32[]{:S(2)}) %collective-permute-start.35) | collective-permute-done | bytes 524320 | tf_op jit(solution)/shard_map/ppermute | solution.py:97
  346.4 9.6 %convolution_convert_fusion.3 = bf16[1024,2048]{1,0:T(8,128)(2,1)S(1)} fusion(bf16[1024,1408]{1,0:T(8,128)(2,1)} %get-tuple-element.96, bf16[1408,2048]{1,0:T(8,128)(2,1)} %all-gather.7.cloned.1.call-done.down_ref), kind=kOutput, calls=%fused_computation.5 | convolution fusion | flops 5907677184 | bytes 12845056 | tf_op jit(solution)/shard_map/dot_general | solution.py:81
  358.2 10.2 %collective-permute-done.38 = bf16[256,2048]{1,0:T(8,128)(2,1)S(1)} collective-permute-done((bf16[256,2048]{1,0:T(8,128)(2,1)S(1)}, bf16[256,2048]{1,0:T(8,128)(2,1)S(1)}, u32[]{:S(2)}, u32[]{:S(2)}) %collective-permute-start.38) | collective-permute-done | bytes 1048608 | tf_op jit(solution)/shard_map/ppermute | solution.py:97
  371.5 9.4 %collective-permute-done.39 = bf16[128,2048]{1,0:T(8,128)(2,1)S(1)} collective-permute-done((bf16[128,2048]{1,0:T(8,128)(2,1)S(1)}, bf16[128,2048]{1,0:T(8,128)(2,1)S(1)}, u32[]{:S(2)}, u32[]{:S(2)}) %collective-permute-start.39) | collective-permute-done | bytes 524320 | tf_op jit(solution)/shard_map/ppermute | solution.py:97
  383.8 23.4 %shard_map.240 = (bf16[1024,1536]{1,0:T(8,128)(2,1)}, bf16[1024,1024]{1,0:T(8,128)(2,1)}) custom-call(s32[4,2]{1,0:T(4,128)} %copy-done.4, bf16[1024,2048]{1,0:T(8,128)(2,1)} %copy-done.35, bf16[8,192,2048]{2,1,0:T(8,128)(2,1)} %bitcast.181, bf16[8,192,2048]{2,1,0:T(8,128)(2,1)} %bitcast.182, bf16[1024,1024]{1,0:T(8,128)(2,1)} %copy-done.6, ...), custom_call_target="tpu_custom_call" | custom-call | flops 9126805504 | bytes 16777216 | tf_op jit(solution)/shard_map/pallas_call | solution.py:438
  412.4 13.5 %shard_map.241 = bf16[8,192,2048]{2,1,0:T(8,128)(2,1)} custom-call(bf16[1024,2048]{1,0:T(8,128)(2,1)} %copy-done.35, bf16[1024,1024]{1,0:T(8,128)(2,1)} %copy-done.5, bf16[1024,1536]{1,0:T(8,128)(2,1)} %copy-done, bf16[1024,1024]{1,0:T(8,128)(2,1)} %get-tuple-element.106.query_grads_ref), custom_call_target="tpu_custom_call" | custom-call | flops 6442450944 | bytes 16777216 | tf_op jit(solution)/shard_map/pallas_call | solution.py:417
  440.7 15.4 %shard_map.242 = (bf16[1024,1664]{1,0:T(8,128)(2,1)}, bf16[1024,1664]{1,0:T(8,128)(2,1)}, f32[256,2048]{1,0:T(8,128)}) custom-call(s32[2]{0:T(128)S(1)} %pad_add_fusion.me_ref, bf16[256,1536]{1,0:T(8,128)(2,1)S(1)} %slice.396.own_ref, bf16[256,1536]{1,0:T(8,128)(2,1)} %copy-done.16, bf16[256,1536]{1,0:T(8,128)(2,1)} %copy-done.17, ...), custom_call_target="tpu_custom_call" | custom-call | flops 3221225472 | bytes 20971520 | tf_op jit(solution)/shard_map/pallas_call | solution.py:557
  456.2 6.2 %collective-permute-done.49 = bf16[1024,1664]{1,0:T(8,128)(2,1)S(1)} collective-permute-done((bf16[1024,1664]{1,0:T(8,128)(2,1)}, bf16[1024,1664]{1,0:T(8,128)(2,1)S(1)}, u32[]{:S(2)}, u32[]{:S(2)}) %collective-permute-start.49) | collective-permute-done | bytes 3407904 | tf_op jit(solution)/shard_map/ppermute | solution.py:97
  471.8 16.9 %collective-permute-done.50 = bf16[256,1664]{1,0:T(8,128)(2,1)S(1)} collective-permute-done((bf16[256,1664]{1,0:T(8,128)(2,1)}, bf16[256,1664]{1,0:T(8,128)(2,1)S(1)}, u32[]{:S(2)}, u32[]{:S(2)}) %collective-permute-start.50) | collective-permute-done | bytes 852000 | tf_op jit(solution)/shard_map/ppermute | solution.py:97
  (366 shorter events, 232.6 us)
Async XLA Ops:
  7.2 127.1 %all-gather.9.cloned.1.call-start = ((), (), s32[]{:S(2)}) async-start(), calls=%async_computation.8 | async-start | bytes 7077888 | tf_op jit(solution)/shard_map/all_gather | solution.py:694
  29.8 202.2 %all-gather.5.cloned.1.call-start = ((), (), s32[]{:S(2)}) async-start(), calls=%async_computation.3 | async-start | bytes 12976128 | tf_op jit(solution)/shard_map/all_gather | solution.py:726
  36.1 30.5 %collective-permute-start.6 = (bf16[256,1664]{1,0:T(8,128)(2,1)S(1)}, bf16[256,1664]{1,0:T(8,128)(2,1)S(1)}, u32[]{:S(2)}, u32[]{:S(2)}) collective-permute-start(bf16[256,1664]{1,0:T(8,128)(2,1)S(1)} %pad_maximum_fusion.12), channel_id=1, source_target_pairs={{0,16},{16,0},{1,17},{17,1},{2,18},{18,2},{3,19},{19,3},{4,20},{20... | collective-permute-start | bytes 2555912 | tf_op jit(solution)/shard_map/ppermute | solution.py:97
  37.7 30.5 %collective-permute-start.4 = (bf16[256,1664]{1,0:T(8,128)(2,1)S(1)}, bf16[256,1664]{1,0:T(8,128)(2,1)S(1)}, u32[]{:S(2)}, u32[]{:S(2)}) collective-permute-start(bf16[256,1664]{1,0:T(8,128)(2,1)S(1)} %pad_maximum_fusion.12), channel_id=1, source_target_pairs={{0,8},{8,0},{1,9},{9,1},{2,10},{10,2},{3,11},{11,3},{4,12},{12,4},... | collective-permute-start | bytes 2555912 | tf_op jit(solution)/shard_map/ppermute | solution.py:97
  83.7 183.9 %all-gather.7.cloned.1.call-start = ((), (), s32[]{:S(2)}) async-start(), calls=%async_computation.4 | async-start | bytes 6488064 | tf_op jit(solution)/shard_map/all_gather | solution.py:701
  131.4 23.9 %collective-permute-start.19 = (bf16[256,2048]{1,0:T(8,128)(2,1)S(1)}, bf16[256,2048]{1,0:T(8,128)(2,1)}, u32[]{:S(2)}, u32[]{:S(2)}) collective-permute-start(bf16[256,2048]{1,0:T(8,128)(2,1)S(1)} %fusion), channel_id=1, source_target_pairs={{0,16},{16,0},{1,17},{17,1},{2,18},{18,2},{3,19},{19,3},{4,20},{20... | collective-permute-start | bytes 3145736 | tf_op jit(solution)/shard_map/ppermute | solution.py:97
  131.7 23.8 %collective-permute-start.18 = (bf16[256,2048]{1,0:T(8,128)(2,1)S(1)}, bf16[256,2048]{1,0:T(8,128)(2,1)}, u32[]{:S(2)}, u32[]{:S(2)}) collective-permute-start(bf16[256,2048]{1,0:T(8,128)(2,1)S(1)} %fusion), channel_id=1, source_target_pairs={{0,8},{8,0},{1,9},{9,1},{2,10},{10,2},{3,11},{11,3},{4,12},{12,4},... | collective-permute-start | bytes 3145736 | tf_op jit(solution)/shard_map/ppermute | solution.py:97
  134.0 211.3 %reduce-scatter.4.cloned.1.call-start = ((), (), s32[]{:S(2)}) async-start(), calls=%async_computation.5 | async-start | bytes 6488064 | tf_op jit(solution)/shard_map/reduce_scatter | solution.py:748
  155.8 22.8 %collective-permute-start.20 = (bf16[256,2048]{1,0:T(8,128)(2,1)S(1)}, bf16[256,2048]{1,0:T(8,128)(2,1)S(1)}, u32[]{:S(2)}, u32[]{:S(2)}) collective-permute-start(bf16[256,2048]{1,0:T(8,128)(2,1)S(1)} %pad_maximum_fusion.5), channel_id=1, source_target_pairs={{0,8},{8,0},{1,9},{9,1},{2,10},{10,2},{3,11},{11,3},{4,12},{12,4},... | collective-permute-start | bytes 3145736 | tf_op jit(solution)/shard_map/ppermute | solution.py:97
  157.1 22.8 %collective-permute-start.21 = (bf16[256,2048]{1,0:T(8,128)(2,1)S(1)}, bf16[256,2048]{1,0:T(8,128)(2,1)S(1)}, u32[]{:S(2)}, u32[]{:S(2)}) collective-permute-start(bf16[256,2048]{1,0:T(8,128)(2,1)S(1)} %pad_maximum_fusion.6), channel_id=1, source_target_pairs={{0,16},{16,0},{1,17},{17,1},{2,18},{18,2},{3,19},{19,3},{4,20},{20... | collective-permute-start | bytes 3145736 | tf_op jit(solution)/shard_map/ppermute | solution.py:97
  193.4 22.0 %collective-permute-start.25 = (bf16[256,2048]{1,0:T(8,128)(2,1)S(1)}, bf16[256,2048]{1,0:T(8,128)(2,1)S(1)}, u32[]{:S(2)}, u32[]{:S(2)}) collective-permute-start(bf16[256,2048]{1,0:T(8,128)(2,1)S(1)} %get-tuple-element.144), channel_id=1, source_target_pairs={{0,16},{16,0},{1,17},{17,1},{2,18},{18,2},{3,19},{19,3},{4,20},{20... | collective-permute-start | bytes 3145736 | tf_op jit(solution)/shard_map/ppermute | solution.py:97
  194.1 24.4 %collective-permute-start.24 = (bf16[256,2048]{1,0:T(8,128)(2,1)S(1)}, bf16[256,2048]{1,0:T(8,128)(2,1)S(1)}, u32[]{:S(2)}, u32[]{:S(2)}) collective-permute-start(bf16[256,2048]{1,0:T(8,128)(2,1)S(1)} %get-tuple-element.144), channel_id=1, source_target_pairs={{0,8},{8,0},{1,9},{9,1},{2,10},{10,2},{3,11},{11,3},{4,12},{12,4},... | collective-permute-start | bytes 3145736 | tf_op jit(solution)/shard_map/ppermute | solution.py:97
  263.2 202.4 %reduce-scatter.6.cloned.1.call-start = ((), (), s32[]{:S(2)}) async-start(), calls=%async_computation.6 | async-start | bytes 12976128 | tf_op jit(solution)/shard_map/reduce_scatter | solution.py:763
  299.2 25.4 %collective-permute-start.33 = (bf16[256,2048]{1,0:T(8,128)(2,1)S(1)}, bf16[256,2048]{1,0:T(8,128)(2,1)S(1)}, u32[]{:S(2)}, u32[]{:S(2)}) collective-permute-start(bf16[256,2048]{1,0:T(8,128)(2,1)S(1)} %pad_maximum_fusion.7), channel_id=1, source_target_pairs={{0,8},{8,0},{1,9},{9,1},{2,10},{10,2},{3,11},{11,3},{4,12},{12,4},... | collective-permute-start | bytes 3145736 | tf_op jit(solution)/shard_map/ppermute | solution.py:97
  300.8 25.1 %collective-permute-start.34 = (bf16[256,2048]{1,0:T(8,128)(2,1)S(1)}, bf16[256,2048]{1,0:T(8,128)(2,1)S(1)}, u32[]{:S(2)}, u32[]{:S(2)}) collective-permute-start(bf16[256,2048]{1,0:T(8,128)(2,1)S(1)} %pad_maximum_fusion.8), channel_id=1, source_target_pairs={{0,16},{16,0},{1,17},{17,1},{2,18},{18,2},{3,19},{19,3},{4,20},{20... | collective-permute-start | bytes 3145736 | tf_op jit(solution)/shard_map/ppermute | solution.py:97
  327.3 196.3 %reduce-scatter.8.cloned.1.call-start = ((), (), s32[]{:S(2)}) async-start(), calls=%async_computation.7 | async-start | bytes 7077888 | tf_op jit(solution)/shard_map/reduce_scatter | solution.py:790
  345.3 23.1 %collective-permute-start.38 = (bf16[256,2048]{1,0:T(8,128)(2,1)S(1)}, bf16[256,2048]{1,0:T(8,128)(2,1)S(1)}, u32[]{:S(2)}, u32[]{:S(2)}) collective-permute-start(bf16[256,2048]{1,0:T(8,128)(2,1)S(1)} %get-tuple-element.95), channel_id=1, source_target_pairs={{0,16},{16,0},{1,17},{17,1},{2,18},{18,2},{3,19},{19,3},{4,20},{20... | collective-permute-start | bytes 3145736 | tf_op jit(solution)/shard_map/ppermute | solution.py:97
  345.9 23.1 %collective-permute-start.37 = (bf16[256,2048]{1,0:T(8,128)(2,1)S(1)}, bf16[256,2048]{1,0:T(8,128)(2,1)S(1)}, u32[]{:S(2)}, u32[]{:S(2)}) collective-permute-start(bf16[256,2048]{1,0:T(8,128)(2,1)S(1)} %get-tuple-element.95), channel_id=1, source_target_pairs={{0,8},{8,0},{1,9},{9,1},{2,10},{10,2},{3,11},{11,3},{4,12},{12,4},... | collective-permute-start | bytes 3145736 | tf_op jit(solution)/shard_map/ppermute | solution.py:97
  381.0 26.2 %collective-permute-start.41 = (bf16[256,2048]{1,0:T(8,128)(2,1)S(1)}, bf16[256,2048]{1,0:T(8,128)(2,1)S(1)}, u32[]{:S(2)}, u32[]{:S(2)}) collective-permute-start(bf16[256,2048]{1,0:T(8,128)(2,1)S(1)} %pad_maximum_fusion.9), channel_id=1, source_target_pairs={{0,8},{8,0},{1,9},{9,1},{2,10},{10,2},{3,11},{11,3},{4,12},{12,4},... | collective-permute-start | bytes 3145736 | tf_op jit(solution)/shard_map/ppermute | solution.py:97
  382.4 24.9 %collective-permute-start.42 = (bf16[256,2048]{1,0:T(8,128)(2,1)S(1)}, bf16[256,2048]{1,0:T(8,128)(2,1)S(1)}, u32[]{:S(2)}, u32[]{:S(2)}) collective-permute-start(bf16[256,2048]{1,0:T(8,128)(2,1)S(1)} %pad_maximum_fusion.10), channel_id=1, source_target_pairs={{0,16},{16,0},{1,17},{17,1},{2,18},{18,2},{3,19},{19,3},{4,20},{20... | collective-permute-start | bytes 3145736 | tf_op jit(solution)/shard_map/ppermute | solution.py:97
  433.9 22.2 %collective-permute-start.44 = (bf16[128,2048]{1,0:T(8,128)(2,1)}, bf16[128,2048]{1,0:T(8,128)(2,1)S(1)}, u32[]{:S(2)}, u32[]{:S(2)}) collective-permute-start(bf16[128,2048]{1,0:T(8,128)(2,1)} %get-tuple-element.147), channel_id=1, source_target_pairs={{0,8},{8,0},{1,9},{9,1},{2,10},{10,2},{3,11},{11,3},{4,12},{12,4},... | collective-permute-start | bytes 1572872 | tf_op jit(solution)/shard_map/ppermute | solution.py:97
  434.6 21.5 %collective-permute-start.43 = (bf16[128,2048]{1,0:T(8,128)(2,1)}, bf16[128,2048]{1,0:T(8,128)(2,1)S(1)}, u32[]{:S(2)}, u32[]{:S(2)}) collective-permute-start(bf16[128,2048]{1,0:T(8,128)(2,1)} %get-tuple-element.148), channel_id=1, source_target_pairs={{0,16},{16,0},{1,17},{17,1},{2,18},{18,2},{3,19},{19,3},{4,20},{20... | collective-permute-start | bytes 1572872 | tf_op jit(solution)/shard_map/ppermute | solution.py:97
  467.5 21.2 %collective-permute-start.50 = (bf16[256,1664]{1,0:T(8,128)(2,1)}, bf16[256,1664]{1,0:T(8,128)(2,1)S(1)}, u32[]{:S(2)}, u32[]{:S(2)}) collective-permute-start(bf16[256,1664]{1,0:T(8,128)(2,1)} %pad_maximum_fusion.13), channel_id=1, source_target_pairs={{0,8},{8,0},{1,9},{9,1},{2,10},{10,2},{3,11},{11,3},{4,12},{12,4},... | collective-permute-start | bytes 2555912 | tf_op jit(solution)/shard_map/ppermute | solution.py:97
  495.3 22.4 %collective-permute-start.51 = (bf16[128,1664]{1,0:T(8,128)(2,1)S(1)}, bf16[128,1664]{1,0:T(8,128)(2,1)S(1)}, u32[]{:S(2)}, u32[]{:S(2)}) collective-permute-start(bf16[128,1664]{1,0:T(8,128)(2,1)S(1)} %add_convert_fusion.8), channel_id=1, source_target_pairs={{0,16},{16,0},{1,17},{17,1},{2,18},{18,2},{3,19},{19,3},{4,20},{20... | collective-permute-start | bytes 1277960 | tf_op jit(solution)/shard_map/ppermute | solution.py:97
  (86 other events, 822.1 us)
Sparse Core Ops, SparseCore 0:
  29.9 68.3 all-gather.8
  100.5 106.7 all-gather.4
  208.9 58.6 all-gather.6
  269.8 63.5 reduce-scatter.3
  335.5 117.6 reduce-scatter.5
  455.4 68.1 reduce-scatter.7

commit v7 on v6

--- a/solution.py
+++ b/solution.py
@@ -204,14 +204,15 @@
         whole = lax.all_gather(values, RING, axis=0, tiled=True)
         return jnp.concatenate(gather_quad(whole, *GROUP), axis=0), whole
     core, place = lax.axis_index("r"), lax.axis_index("zh") * 2 + lax.axis_index("zl")
-    line = jnp.stack([values] + [along_z(values, code) for code in (1, 2, 3)])
+    sent = [along_z(values, code) for code in (1, 2, 3)]
+    line = jnp.stack([values] + sent)
     line = [lax.dynamic_index_in_dim(line, place ^ k, 0, keepdims=False) for k in range(4)]
     line = jnp.concatenate(line, axis=0)
     total = jnp.zeros((4, 4, 2, n, c), values.dtype)
     for slot, part in enumerate(gather_quad(line, *GROUP)):
         for where, piece in ((core, part), (1 - core, trade(part, "r"))):
             total = lax.dynamic_update_slice(total, piece.reshape(1, 4, 1, n, c), (slot, 0, where, 0, 0))
-    return total.reshape(32 * n, c), line
+    return total.reshape(32 * n, c), sent[:2]
 
 
 def swap_blocks(block):

time: 563 us -> 558 us (level)
  waiting for transfers between devices: 216 us -> 209 us
    unnamed x93 -> x99, local copies, waits for them, and re-layouts: 12.8 us -> 11.9 us
where the time goes in v7:
time: 558 us; the launch traced here: 549 us
  waiting for transfers between devices  209 us (37%)
  Pallas kernels  101 us (18%)
  starting transfers between devices  75.6 us (14%)
  matrix products  58.5 us (10%)
  other arithmetic  44.5 us (8%)
  local copies, waits for them, and re-layouts  43.2 us (8%)
  between operations  17.2 us (3%)
    ppermute x45, waiting for transfers between devices, trade(): return lax.ppermute(values, axis, [(0, 1), (1, 0)])  165 us
    ppermute x45, starting transfers between devices, trade(): return lax.ppermute(values, axis, [(0, 1), (1, 0)])  46.9 us
    dot_general x2, matrix products, dot_tn(): lax.dot_general(a, b, (((0,), (0,)), ((), ())), preferred_element_type=f32)  25.7 us
    pallas_call x1, Pallas kernels, attend_back(): pl.pallas_call(functools.partial(attend_back_kernel, members, heads), gri...  23.4 us
    ppermute x12, waiting for transfers between devices, swap_blocks(): lax.ppermute(block(me ^ code), DP, [(i, i ^ code) for i in range(4)])  21.2 us
    pallas_call x1, Pallas kernels, ffn(): pl.pallas_call(ffn_kernel, grid=(cut // tile,), in_specs=[pl.BlockSpec((t...  19.1 us
    dot_general x1, matrix products, dot_nt(): lax.dot_general(a, b, (((1,), (1,)), ((), ())), preferred_element_type=f32)  18 us
    pallas_call x1, Pallas kernels, attend(): pl.pallas_call(functools.partial(attend_kernel, members, heads), grid_spe...  16.6 us
  transfers between devices with their start and end apart: 69, of which 42 were waited for; matrix products, arithmetic and copies ran while one was open for 24% of the time, Pallas kernels for 18%

profile of v7, /device:TPU:0, one launch (start us, length us, event | category | flops | bytes accessed | tf_op | source)
XLA Modules:
  0.0 549.4 jit_solution(17549645873169181253)
XLA Ops:
  21.0 6.5 %collective-permute-done.1 = bf16[64,1664]{1,0:T(8,128)(2,1)S(1)} collective-permute-done((bf16[64,1664]{1,0:T(8,128)(2,1)S(1)}, bf16[64,1664]{1,0:T(8,128)(2,1)S(1)}, u32[]{:S(2)}, u32[]{:S(2)}) %collective-permute-start.1) | collective-permute-done | bytes 213024 | tf_op jit(solution)/shard_map/ppermute | solution.py:198
  44.5 6.0 %collective-permute-done.29 = bf16[64,2816]{1,0:T(8,128)(2,1)} collective-permute-done((bf16[64,2816]{1,0:T(8,128)(2,1)S(1)}, bf16[64,2816]{1,0:T(8,128)(2,1)}, u32[]{:S(2)}, u32[]{:S(2)}) %collective-permute-start.29) | collective-permute-done | bytes 360480 | tf_op jit(solution)/shard_map/ppermute | solution.py:222
  55.7 11.6 %collective-permute-done.6 = bf16[256,1664]{1,0:T(8,128)(2,1)S(1)} collective-permute-done((bf16[256,1664]{1,0:T(8,128)(2,1)S(1)}, bf16[256,1664]{1,0:T(8,128)(2,1)S(1)}, u32[]{:S(2)}, u32[]{:S(2)}) %collective-permute-start.6) | collective-permute-done | bytes 852000 | tf_op jit(solution)/shard_map/ppermute | solution.py:97
  104.6 14.1 %collective-permute-done.11 = bf16[256,1536]{1,0:T(8,128)(2,1)S(1)} collective-permute-done((bf16[256,1536]{1,0:T(8,128)(2,1)S(1)}, bf16[256,1536]{1,0:T(8,128)(2,1)S(1)}, u32[]{:S(2)}, u32[]{:S(2)}) %collective-permute-start.11) | collective-permute-done | bytes 786464 | tf_op jit(solution)/shard_map/ppermute | solution.py:97
  122.0 8.9 %collective-permute-done.13 = bf16[128,1536]{1,0:T(8,128)(2,1)S(1)} collective-permute-done((bf16[128,1536]{1,0:T(8,128)(2,1)S(1)}, bf16[128,1536]{1,0:T(8,128)(2,1)S(1)}, u32[]{:S(2)}, u32[]{:S(2)}) %collective-permute-start.13) | collective-permute-done | bytes 393248 | tf_op jit(solution)/shard_map/ppermute | solution.py:97
  137.9 16.6 %shard_map.237 = (bf16[1024,1024]{1,0:T(8,128)(2,1)S(1)}, bf16[1024,1024]{1,0:T(8,128)(2,1)S(1)}, bf16[1024,2048]{1,0:T(8,128)(2,1)S(1)}) custom-call(s32[4,2]{1,0:T(4,128)S(1)} %copy.41.lengths_ref, bf16[1024,1536]{1,0:T(8,128)(2,1)S(1)} %copy-done.1, bf16[8,192,2048]{2,1,0:T(8,128)(2,1)} %bitcast.180, bf16[8,192,2048]{2,1,0:T(8,128)(2,1)} %bitcast.181, ...), custom_call_target="tpu_custom_call" | custom-call | flops 7516192768 | bytes 15728640 | tf_op jit(solution)/shard_map/pallas_call | solution.py:329
  167.6 12.5 %collective-permute-done.20 = bf16[256,2048]{1,0:T(8,128)(2,1)S(1)} collective-permute-done((bf16[256,2048]{1,0:T(8,128)(2,1)S(1)}, bf16[256,2048]{1,0:T(8,128)(2,1)S(1)}, u32[]{:S(2)}, u32[]{:S(2)}) %collective-permute-start.20) | collective-permute-done | bytes 1048608 | tf_op jit(solution)/shard_map/ppermute | solution.py:97
  184.3 8.0 %collective-permute-done.22 = bf16[128,2048]{1,0:T(8,128)(2,1)S(1)} collective-permute-done((bf16[128,2048]{1,0:T(8,128)(2,1)S(1)}, bf16[128,2048]{1,0:T(8,128)(2,1)S(1)}, u32[]{:S(2)}, u32[]{:S(2)}) %collective-permute-start.22) | collective-permute-done | bytes 524320 | tf_op jit(solution)/shard_map/ppermute | solution.py:97
  196.7 20.2 %collective-permute-done.25 = bf16[256,2048]{1,0:T(8,128)(2,1)S(1)} collective-permute-done((bf16[256,2048]{1,0:T(8,128)(2,1)S(1)}, bf16[256,2048]{1,0:T(8,128)(2,1)S(1)}, u32[]{:S(2)}, u32[]{:S(2)}) %collective-permute-start.25) | collective-permute-done | bytes 1048608 | tf_op jit(solution)/shard_map/ppermute | solution.py:97
  221.0 6.6 %collective-permute-done.26 = bf16[128,2048]{1,0:T(8,128)(2,1)S(1)} collective-permute-done((bf16[128,2048]{1,0:T(8,128)(2,1)S(1)}, bf16[128,2048]{1,0:T(8,128)(2,1)S(1)}, u32[]{:S(2)}, u32[]{:S(2)}) %collective-permute-start.26) | collective-permute-done | bytes 524320 | tf_op jit(solution)/shard_map/ppermute | solution.py:97
  233.0 19.1 %shard_map.238 = (bf16[1024,1408]{1,0:T(8,128)(2,1)}, bf16[1024,1408]{1,0:T(8,128)(2,1)}, bf16[1024,1408]{1,0:T(8,128)(2,1)}) custom-call(bf16[1024,2048]{1,0:T(8,128)(2,1)} %copy-done.34, bf16[2048,2816]{1,0:T(8,128)(2,1)} %bitcast.177, bf16[2048,2816]{1,0:T(8,128)(2,1)} %bitcast.178), custom_call_target="tpu_custom_call" | custom-call | flops 11811160064 | bytes 24379392 | tf_op jit(solution)/shard_map/pallas_call | solution.py:590
  253.8 10.5 %convolution_convert_fusion.1 = bf16[1408,2048]{1,0:T(8,128)(2,1)} fusion(bf16[1024,1408]{1,0:T(8,128)(2,1)} %get-tuple-element.96, bf16[1024,2048]{1,0:T(8,128)(2,1)} %constant_dynamic-update-slice_fusion.17.grad_ref), kind=kOutput, calls=%fused_computation.1 | convolution fusion | flops 5908463616 | bytes 12845056 | tf_op jit(solution)/shard_map/dot_general | solution.py:89
  264.8 13.3 %shard_map.239 = bf16[1024,2816]{1,0:T(8,128)(2,1)} custom-call(bf16[1024,2048]{1,0:T(8,128)(2,1)} %constant_dynamic-update-slice_fusion.17.grad_ref, bf16[1408,2048]{1,0:T(8,128)(2,1)} %all-gather.7.cloned.1.call-done.down_ref, bf16[1024,1408]{1,0:T(8,128)(2,1)} %get-tuple-element.89.slope_ref, bf16[1024,1408]{1,0:T(8,128)(2,1)} %get-tuple-element.90.silu_ref), custom_call_target="tpu_custom_call" | custom-call | flops 5905580032 | bytes 21495808 | tf_op jit(solution)/shard_map/pallas_call | solution.py:620
  278.1 18.0 %convolution_convert_fusion.2 = bf16[1024,2048]{1,0:T(8,128)(2,1)S(1)} fusion(bf16[1024,2816]{1,0:T(8,128)(2,1)} %shard_map.239, bf16[2048,2816]{1,0:T(8,128)(2,1)} %bitcast.179), kind=kOutput, calls=%fused_computation.4 | convolution fusion | flops 11813257216 | bytes 21495808 | tf_op jit(solution)/shard_map/dot_general | solution.py:85
  301.1 15.2 %convolution_convert_fusion = bf16[2048,2816]{1,0:T(8,128)(2,1)} fusion(bf16[1024,2048]{1,0:T(8,128)(2,1)S(1)} %copy-done.35, bf16[1024,2816]{1,0:T(8,128)(2,1)S(1)} %copy-done.42), kind=kOutput, calls=%fused_computation | convolution fusion | flops 11816927232 | bytes 21495808 | tf_op jit(solution)/shard_map/dot_general | solution.py:89
  326.3 6.8 %collective-permute-done.35 = bf16[128,2048]{1,0:T(8,128)(2,1)S(1)} collective-permute-done((bf16[128,2048]{1,0:T(8,128)(2,1)}, bf16[128,2048]{1,0:T(8,128)(2,1)S(1)}, u32[]{:S(2)}, u32[]{:S(2)}) %collective-permute-start.35) | collective-permute-done | bytes 524320 | tf_op jit(solution)/shard_map/ppermute | solution.py:97
  339.2 9.6 %convolution_convert_fusion.3 = bf16[1024,2048]{1,0:T(8,128)(2,1)S(1)} fusion(bf16[1024,1408]{1,0:T(8,128)(2,1)} %get-tuple-element.96, bf16[1408,2048]{1,0:T(8,128)(2,1)} %all-gather.7.cloned.1.call-done.down_ref), kind=kOutput, calls=%fused_computation.5 | convolution fusion | flops 5907677184 | bytes 12845056 | tf_op jit(solution)/shard_map/dot_general | solution.py:81
  363.3 10.3 %collective-permute-done.39 = bf16[128,2048]{1,0:T(8,128)(2,1)S(1)} collective-permute-done((bf16[128,2048]{1,0:T(8,128)(2,1)S(1)}, bf16[128,2048]{1,0:T(8,128)(2,1)S(1)}, u32[]{:S(2)}, u32[]{:S(2)}) %collective-permute-start.39) | collective-permute-done | bytes 524320 | tf_op jit(solution)/shard_map/ppermute | solution.py:97
  377.6 23.4 %shard_map.240 = (bf16[1024,1536]{1,0:T(8,128)(2,1)}, bf16[1024,1024]{1,0:T(8,128)(2,1)}) custom-call(s32[4,2]{1,0:T(4,128)} %copy-done.4, bf16[1024,2048]{1,0:T(8,128)(2,1)} %copy-done.36, bf16[8,192,2048]{2,1,0:T(8,128)(2,1)} %bitcast.182, bf16[8,192,2048]{2,1,0:T(8,128)(2,1)} %bitcast.183, bf16[1024,1024]{1,0:T(8,128)(2,1)} %copy-done.6, ...), custom_call_target="tpu_custom_call" | custom-call | flops 9126805504 | bytes 16777216 | tf_op jit(solution)/shard_map/pallas_call | solution.py:439
  406.7 13.5 %shard_map.241 = bf16[8,192,2048]{2,1,0:T(8,128)(2,1)} custom-call(bf16[1024,2048]{1,0:T(8,128)(2,1)} %copy-done.36, bf16[1024,1024]{1,0:T(8,128)(2,1)} %copy-done.5, bf16[1024,1536]{1,0:T(8,128)(2,1)} %copy-done, bf16[1024,1024]{1,0:T(8,128)(2,1)} %get-tuple-element.106.query_grads_ref), custom_call_target="tpu_custom_call" | custom-call | flops 6442450944 | bytes 16777216 | tf_op jit(solution)/shard_map/pallas_call | solution.py:418
  432.6 15.4 %shard_map.242 = (bf16[1024,1664]{1,0:T(8,128)(2,1)}, bf16[1024,1664]{1,0:T(8,128)(2,1)}, f32[256,2048]{1,0:T(8,128)}) custom-call(s32[2]{0:T(128)S(1)} %pad_add_fusion.me_ref, bf16[256,1536]{1,0:T(8,128)(2,1)S(1)} %slice.396.own_ref, bf16[256,1536]{1,0:T(8,128)(2,1)} %copy-done.16, bf16[256,1536]{1,0:T(8,128)(2,1)} %copy-done.17, ...), custom_call_target="tpu_custom_call" | custom-call | flops 3221225472 | bytes 20971520 | tf_op jit(solution)/shard_map/pallas_call | solution.py:558
  448.1 6.2 %collective-permute-done.49 = bf16[1024,1664]{1,0:T(8,128)(2,1)S(1)} collective-permute-done((bf16[1024,1664]{1,0:T(8,128)(2,1)}, bf16[1024,1664]{1,0:T(8,128)(2,1)S(1)}, u32[]{:S(2)}, u32[]{:S(2)}) %collective-permute-start.49) | collective-permute-done | bytes 3407904 | tf_op jit(solution)/shard_map/ppermute | solution.py:97
  464.6 16.5 %collective-permute-done.50 = bf16[256,1664]{1,0:T(8,128)(2,1)S(1)} collective-permute-done((bf16[256,1664]{1,0:T(8,128)(2,1)}, bf16[256,1664]{1,0:T(8,128)(2,1)S(1)}, u32[]{:S(2)}, u32[]{:S(2)}) %collective-permute-start.50) | collective-permute-done | bytes 852000 | tf_op jit(solution)/shard_map/ppermute | solution.py:97
  511.0 7.9 %reduce-scatter.8.cloned.1.call-done = bf16[1,192,2048]{2,1,0:T(8,128)(2,1)} async-done(((bf16[8,192,2048]{2,1,0:T(8,128)(2,1)}), bf16[1,192,2048]{2,1,0:T(8,128)(2,1)}) %reduce-scatter.8.cloned.1.call-update) | async-done | bytes 786448 | tf_op jit(solution)/shard_map/reduce_scatter | solution.py:791
  (372 shorter events, 235.5 us)
Async XLA Ops:
  7.2 128.8 %all-gather.9.cloned.1.call-start = ((), (), s32[]{:S(2)}) async-start(), calls=%async_computation.8 | async-start | bytes 7077888 | tf_op jit(solution)/shard_map/all_gather | solution.py:695
  27.7 205.3 %all-gather.5.cloned.1.call-start = ((), (), s32[]{:S(2)}) async-start(), calls=%async_computation.3 | async-start | bytes 12976128 | tf_op jit(solution)/shard_map/all_gather | solution.py:727
  36.9 30.5 %collective-permute-start.6 = (bf16[256,1664]{1,0:T(8,128)(2,1)S(1)}, bf16[256,1664]{1,0:T(8,128)(2,1)S(1)}, u32[]{:S(2)}, u32[]{:S(2)}) collective-permute-start(bf16[256,1664]{1,0:T(8,128)(2,1)S(1)} %pad_maximum_fusion.12), channel_id=1, source_target_pairs={{0,16},{16,0},{1,17},{17,1},{2,18},{18,2},{3,19},{19,3},{4,20},{20... | collective-permute-start | bytes 2555912 | tf_op jit(solution)/shard_map/ppermute | solution.py:97
  38.5 31.6 %collective-permute-start.4 = (bf16[256,1664]{1,0:T(8,128)(2,1)S(1)}, bf16[256,1664]{1,0:T(8,128)(2,1)S(1)}, u32[]{:S(2)}, u32[]{:S(2)}) collective-permute-start(bf16[256,1664]{1,0:T(8,128)(2,1)S(1)} %pad_maximum_fusion.12), channel_id=1, source_target_pairs={{0,8},{8,0},{1,9},{9,1},{2,10},{10,2},{3,11},{11,3},{4,12},{12,4},... | collective-permute-start | bytes 2555912 | tf_op jit(solution)/shard_map/ppermute | solution.py:97
  50.5 21.7 %collective-permute-start.3 = (bf16[256,1664]{1,0:T(8,128)(2,1)S(1)}, bf16[256,1664]{1,0:T(8,128)(2,1)S(1)}, u32[]{:S(2)}, u32[]{:S(2)}) collective-permute-start(bf16[256,1664]{1,0:T(8,128)(2,1)S(1)} %pad_maximum_fusion.12), channel_id=1, source_target_pairs={{0,1},{1,0},{2,3},{3,2},{4,5},{5,4},{6,7},{7,6},{8,9},{9,8},{10,11... | collective-permute-start | bytes 2555912 | tf_op jit(solution)/shard_map/ppermute | solution.py:97
  85.3 179.5 %all-gather.7.cloned.1.call-start = ((), (), s32[]{:S(2)}) async-start(), calls=%async_computation.4 | async-start | bytes 6488064 | tf_op jit(solution)/shard_map/all_gather | solution.py:702
  132.7 23.8 %collective-permute-start.19 = (bf16[256,2048]{1,0:T(8,128)(2,1)S(1)}, bf16[256,2048]{1,0:T(8,128)(2,1)}, u32[]{:S(2)}, u32[]{:S(2)}) collective-permute-start(bf16[256,2048]{1,0:T(8,128)(2,1)S(1)} %fusion), channel_id=1, source_target_pairs={{0,16},{16,0},{1,17},{17,1},{2,18},{18,2},{3,19},{19,3},{4,20},{20... | collective-permute-start | bytes 3145736 | tf_op jit(solution)/shard_map/ppermute | solution.py:97
  133.7 23.5 %collective-permute-start.18 = (bf16[256,2048]{1,0:T(8,128)(2,1)S(1)}, bf16[256,2048]{1,0:T(8,128)(2,1)}, u32[]{:S(2)}, u32[]{:S(2)}) collective-permute-start(bf16[256,2048]{1,0:T(8,128)(2,1)S(1)} %fusion), channel_id=1, source_target_pairs={{0,8},{8,0},{1,9},{9,1},{2,10},{10,2},{3,11},{11,3},{4,12},{12,4},... | collective-permute-start | bytes 3145736 | tf_op jit(solution)/shard_map/ppermute | solution.py:97
  135.7 201.3 %reduce-scatter.4.cloned.1.call-start = ((), (), s32[]{:S(2)}) async-start(), calls=%async_computation.5 | async-start | bytes 6488064 | tf_op jit(solution)/shard_map/reduce_scatter | solution.py:749
  157.6 22.5 %collective-permute-start.20 = (bf16[256,2048]{1,0:T(8,128)(2,1)S(1)}, bf16[256,2048]{1,0:T(8,128)(2,1)S(1)}, u32[]{:S(2)}, u32[]{:S(2)}) collective-permute-start(bf16[256,2048]{1,0:T(8,128)(2,1)S(1)} %pad_maximum_fusion.5), channel_id=1, source_target_pairs={{0,8},{8,0},{1,9},{9,1},{2,10},{10,2},{3,11},{11,3},{4,12},{12,4},... | collective-permute-start | bytes 3145736 | tf_op jit(solution)/shard_map/ppermute | solution.py:97
  158.8 22.8 %collective-permute-start.21 = (bf16[256,2048]{1,0:T(8,128)(2,1)S(1)}, bf16[256,2048]{1,0:T(8,128)(2,1)S(1)}, u32[]{:S(2)}, u32[]{:S(2)}) collective-permute-start(bf16[256,2048]{1,0:T(8,128)(2,1)S(1)} %pad_maximum_fusion.6), channel_id=1, source_target_pairs={{0,16},{16,0},{1,17},{17,1},{2,18},{18,2},{3,19},{19,3},{4,20},{20... | collective-permute-start | bytes 3145736 | tf_op jit(solution)/shard_map/ppermute | solution.py:97
  195.2 21.8 %collective-permute-start.25 = (bf16[256,2048]{1,0:T(8,128)(2,1)S(1)}, bf16[256,2048]{1,0:T(8,128)(2,1)S(1)}, u32[]{:S(2)}, u32[]{:S(2)}) collective-permute-start(bf16[256,2048]{1,0:T(8,128)(2,1)S(1)} %get-tuple-element.144), channel_id=1, source_target_pairs={{0,16},{16,0},{1,17},{17,1},{2,18},{18,2},{3,19},{19,3},{4,20},{20... | collective-permute-start | bytes 3145736 | tf_op jit(solution)/shard_map/ppermute | solution.py:97
  196.1 24.6 %collective-permute-start.24 = (bf16[256,2048]{1,0:T(8,128)(2,1)S(1)}, bf16[256,2048]{1,0:T(8,128)(2,1)S(1)}, u32[]{:S(2)}, u32[]{:S(2)}) collective-permute-start(bf16[256,2048]{1,0:T(8,128)(2,1)S(1)} %get-tuple-element.144), channel_id=1, source_target_pairs={{0,8},{8,0},{1,9},{9,1},{2,10},{10,2},{3,11},{11,3},{4,12},{12,4},... | collective-permute-start | bytes 3145736 | tf_op jit(solution)/shard_map/ppermute | solution.py:97
  264.3 193.6 %reduce-scatter.6.cloned.1.call-start = ((), (), s32[]{:S(2)}) async-start(), calls=%async_computation.6 | async-start | bytes 12976128 | tf_op jit(solution)/shard_map/reduce_scatter | solution.py:764
  296.5 23.3 %collective-permute-start.33 = (bf16[256,2048]{1,0:T(8,128)(2,1)S(1)}, bf16[256,2048]{1,0:T(8,128)(2,1)S(1)}, u32[]{:S(2)}, u32[]{:S(2)}) collective-permute-start(bf16[256,2048]{1,0:T(8,128)(2,1)S(1)} %pad_maximum_fusion.7), channel_id=1, source_target_pairs={{0,8},{8,0},{1,9},{9,1},{2,10},{10,2},{3,11},{11,3},{4,12},{12,4},... | collective-permute-start | bytes 3145736 | tf_op jit(solution)/shard_map/ppermute | solution.py:97
  298.6 22.5 %collective-permute-start.34 = (bf16[256,2048]{1,0:T(8,128)(2,1)S(1)}, bf16[256,2048]{1,0:T(8,128)(2,1)S(1)}, u32[]{:S(2)}, u32[]{:S(2)}) collective-permute-start(bf16[256,2048]{1,0:T(8,128)(2,1)S(1)} %pad_maximum_fusion.8), channel_id=1, source_target_pairs={{0,16},{16,0},{1,17},{17,1},{2,18},{18,2},{3,19},{19,3},{4,20},{20... | collective-permute-start | bytes 3145736 | tf_op jit(solution)/shard_map/ppermute | solution.py:97
  322.5 196.3 %reduce-scatter.8.cloned.1.call-start = ((), (), s32[]{:S(2)}) async-start(), calls=%async_computation.7 | async-start | bytes 7077888 | tf_op jit(solution)/shard_map/reduce_scatter | solution.py:791
  338.1 22.7 %collective-permute-start.37 = (bf16[256,2048]{1,0:T(8,128)(2,1)S(1)}, bf16[256,2048]{1,0:T(8,128)(2,1)S(1)}, u32[]{:S(2)}, u32[]{:S(2)}) collective-permute-start(bf16[256,2048]{1,0:T(8,128)(2,1)S(1)} %get-tuple-element.95), channel_id=1, source_target_pairs={{0,8},{8,0},{1,9},{9,1},{2,10},{10,2},{3,11},{11,3},{4,12},{12,4},... | collective-permute-start | bytes 3145736 | tf_op jit(solution)/shard_map/ppermute | solution.py:97
  375.7 25.4 %collective-permute-start.41 = (bf16[256,2048]{1,0:T(8,128)(2,1)S(1)}, bf16[256,2048]{1,0:T(8,128)(2,1)S(1)}, u32[]{:S(2)}, u32[]{:S(2)}) collective-permute-start(bf16[256,2048]{1,0:T(8,128)(2,1)S(1)} %pad_maximum_fusion.9), channel_id=1, source_target_pairs={{0,8},{8,0},{1,9},{9,1},{2,10},{10,2},{3,11},{11,3},{4,12},{12,4},... | collective-permute-start | bytes 3145736 | tf_op jit(solution)/shard_map/ppermute | solution.py:97
  376.4 24.7 %collective-permute-start.42 = (bf16[256,2048]{1,0:T(8,128)(2,1)S(1)}, bf16[256,2048]{1,0:T(8,128)(2,1)S(1)}, u32[]{:S(2)}, u32[]{:S(2)}) collective-permute-start(bf16[256,2048]{1,0:T(8,128)(2,1)S(1)} %pad_maximum_fusion.10), channel_id=1, source_target_pairs={{0,16},{16,0},{1,17},{17,1},{2,18},{18,2},{3,19},{19,3},{4,20},{20... | collective-permute-start | bytes 3145736 | tf_op jit(solution)/shard_map/ppermute | solution.py:97
  459.7 21.4 %collective-permute-start.50 = (bf16[256,1664]{1,0:T(8,128)(2,1)}, bf16[256,1664]{1,0:T(8,128)(2,1)S(1)}, u32[]{:S(2)}, u32[]{:S(2)}) collective-permute-start(bf16[256,1664]{1,0:T(8,128)(2,1)} %pad_maximum_fusion.13), channel_id=1, source_target_pairs={{0,8},{8,0},{1,9},{9,1},{2,10},{10,2},{3,11},{11,3},{4,12},{12,4},... | collective-permute-start | bytes 2555912 | tf_op jit(solution)/shard_map/ppermute | solution.py:97
  462.0 20.8 %collective-permute-start.52 = (bf16[256,1664]{1,0:T(8,128)(2,1)S(1)}, bf16[256,1664]{1,0:T(8,128)(2,1)S(1)}, u32[]{:S(2)}, u32[]{:S(2)}) collective-permute-start(bf16[256,1664]{1,0:T(8,128)(2,1)S(1)} %pad_maximum_fusion.14), channel_id=1, source_target_pairs={{0,16},{16,0},{1,17},{17,1},{2,18},{18,2},{3,19},{19,3},{4,20},{20... | collective-permute-start | bytes 2555912 | tf_op jit(solution)/shard_map/ppermute | solution.py:97
  487.8 22.5 %collective-permute-start.51 = (bf16[128,1664]{1,0:T(8,128)(2,1)S(1)}, bf16[128,1664]{1,0:T(8,128)(2,1)S(1)}, u32[]{:S(2)}, u32[]{:S(2)}) collective-permute-start(bf16[128,1664]{1,0:T(8,128)(2,1)S(1)} %add_convert_fusion.8), channel_id=1, source_target_pairs={{0,16},{16,0},{1,17},{17,1},{2,18},{18,2},{3,19},{19,3},{4,20},{20... | collective-permute-start | bytes 1277960 | tf_op jit(solution)/shard_map/ppermute | solution.py:97
  489.5 21.0 %collective-permute-start.53 = (bf16[128,1664]{1,0:T(8,128)(2,1)S(1)}, bf16[128,1664]{1,0:T(8,128)(2,1)S(1)}, u32[]{:S(2)}, u32[]{:S(2)}) collective-permute-start(bf16[128,1664]{1,0:T(8,128)(2,1)S(1)} %add_convert_fusion.7), channel_id=1, source_target_pairs={{0,8},{8,0},{1,9},{9,1},{2,10},{10,2},{3,11},{11,3},{4,12},{12,4},... | collective-permute-start | bytes 1277960 | tf_op jit(solution)/shard_map/ppermute | solution.py:97
  (89 other events, 867.4 us)
Sparse Core Ops, SparseCore 0:
  27.8 65.6 all-gather.8
  95.7 106.7 all-gather.4
  204.1 58.6 all-gather.6
  265.0 63.6 reduce-scatter.3
  330.8 117.6 reduce-scatter.5
  450.7 68.1 reduce-scatter.7
